TPU v7x, 128 devices: a whole 4x4x4 slice. The times are simulated.
128 devices in a mesh: gx: 16 (over y, x), gy: 8 (over z, core).
Axes of the slice: x: 4, y: 4, z: 4, core: 2. Of those that a mesh axis runs over, the one named last changes fastest.
Arguments:
- velocity: float32 [3, 32, 512, 4096], P(None, None, 'gx', 'gy'), may hold values from -6 to 6
- fiber_points: float32 [1024, 3, 128], P(('gx', 'gy')), may hold values from -6 to 6
- stiffness: float32 [1024], P(('gx', 'gy')), may hold values from 0.5 to 2
- links: int32 [1024, 128], P(('gx', 'gy')), may hold values from 1 to 127
- delta_weights: bfloat16 [1024, 8, 128, 512], P(('gx', 'gy')), may hold values from -0.5 to 0.5
- owners: int32 [1024, 8, 1], P(('gx', 'gy')), may hold values from 0 to 127; in each aligned block of 64 rows (0 to 63, 64 to 127, ..., all dimensions but the last counted through in order) at most 2 rows name the same one
- patch_slots: int32 [1024, 8], P(('gx', 'gy')), may hold values from 0 to 1023
Outputs:
- fluid: float32 [3, 32, 512, 4096], P(None, None, 'gx', 'gy')
- moved_points: float32 [1024, 3, 128], P(('gx', 'gy'))
Inputs may be any that keep to these rules, and one draw needn't show every extreme that they name: owners counts devices in the order gx slower, gy faster; among the rows of one device, no owner is named more than 2 times, a bound that some block reaches.
All inputs are finite; a program needn't handle non-finite values.
Results may differ from a plain program's by a relative error of at most 0.0037.
Values may be sent and summed in bfloat16 or wider, within the bound.
No kernel may reach another device: no remote copies, remote signals or barrier semaphores. Data moves between devices by JAX's collectives and lax.ppermute only.
A program may use at most 128 MiB of HBM per device.

v0:
```python
import jax
import jax.numpy as jnp
from jax import lax
from jax.sharding import PartitionSpec as P

STEPS = 2


viscosity = 0.1
transport_rate = 0.1
force_step = 0.5
fiber_step = 0.25


def extended_2(x, sides, width):
    edges = {}
    for axis, dim in sides:
        peers, length = (lax.axis_size(axis), x.shape[dim])
        up = [(i, (i + 1) % peers) for i in range(peers - 1)]
        last = lax.slice_in_dim(x, length - width, length, axis=dim)
        first = lax.slice_in_dim(x, 0, width, axis=dim)
        edges[dim] = (
            lax.ppermute(last, axis, up),
            lax.ppermute(first, axis, [(b, a) for a, b in up]),
        )
    done = []
    for _, dim in sides:
        low, high = edges[dim]
        around = [(width, width) if d in done else (0, 0) for d in range(x.ndim)]
        x = jnp.concatenate([jnp.pad(low, around), x, jnp.pad(high, around)], axis=dim)
        done.append(dim)
    return x


def advance(extended):
    middle = extended[:, :, 1:-1, 1:-1]
    east_cells = extended[:, :, 2:, 1:-1]
    west_cells = extended[:, :, :-2, 1:-1]
    north_cells = extended[:, :, 1:-1, 2:]
    south_cells = extended[:, :, 1:-1, :-2]
    above_cells = jnp.roll(middle, -1, axis=1)
    below_cells = jnp.roll(middle, 1, axis=1)
    laplace = (
        east_cells
        + west_cells
        + north_cells
        + south_cells
        + above_cells
        + below_cells
        - 6.0 * middle
    )
    transport = (
        middle[0:1] * (east_cells - west_cells)
        + middle[1:2] * (north_cells - south_cells)
        + middle[2:3] * (above_cells - below_cells)
    )
    return middle + viscosity * laplace - transport_rate * transport


def shards(velocity, fiber_points, stiffness, links, delta_weights, owners, patch_slots):
    blocks, intersection = (delta_weights.shape[0], delta_weights.shape[1])
    points, patch = (delta_weights.shape[2], delta_weights.shape[3])
    layers, rows, columns = (velocity.shape[1], velocity.shape[2], velocity.shape[3])
    patch_count = layers * rows * columns // patch
    rows_grid, columns_grid = (lax.axis_size("gx"), lax.axis_size("gy"))
    device_count = rows_grid * columns_grid
    entry_total = blocks * intersection
    per_owner = max(2, (2 * entry_total + device_count - 1) // device_count)
    slot_total = device_count * per_owner
    partner = (jnp.arange(points, dtype=jnp.int32)[None, :] + links) % points
    partner_full = jnp.broadcast_to(partner[:, None, :], fiber_points.shape)
    partner_points = jnp.take_along_axis(fiber_points, partner_full, axis=2)
    fiber_force = stiffness[:, None, None] * (partner_points - fiber_points)
    force_bf = fiber_force.astype(jnp.bfloat16)
    contrib = jnp.einsum(
        "bcp,bkpq->bkcq", force_bf, delta_weights, preferred_element_type=jnp.float32
    )
    contrib_flat = contrib.reshape(entry_total, 3, patch)
    owner_list = owners.reshape(entry_total)
    slot_list = patch_slots.reshape(entry_total)
    positions = jnp.arange(entry_total, dtype=jnp.int32)
    earlier = (owner_list[:, None] == owner_list[None, :]) & (
        positions[None, :] < positions[:, None]
    )
    rank = jnp.sum(earlier.astype(jnp.int32), axis=1)
    destination = owner_list * per_owner + rank
    selector = jnp.arange(slot_total, dtype=jnp.int32)[:, None] == destination[None, :]
    outgoing = jnp.einsum(
        "sr,rcq->scq", selector.astype(jnp.float32), contrib_flat, precision=lax.Precision.HIGHEST
    )
    slot_patch = jnp.max(jnp.where(selector, slot_list[None, :], -1), axis=1)
    flat_data, flat_slots = (
        lax.all_to_all(
            outgoing.reshape(device_count, per_owner, 3, patch),
            ("gx", "gy"),
            split_axis=0,
            concat_axis=0,
            tiled=True,
        ),
        lax.all_to_all(
            slot_patch.reshape(device_count, per_owner),
            ("gx", "gy"),
            split_axis=0,
            concat_axis=0,
            tiled=True,
        ),
    )
    received = flat_data.reshape(slot_total, 3, patch)
    received_slots = flat_slots.reshape(slot_total)
    placing = jnp.arange(patch_count, dtype=jnp.int32)[:, None] == received_slots[None, :]
    force_field = jnp.einsum(
        "ps,scq->cpq", placing.astype(jnp.float32), received, precision=lax.Precision.HIGHEST
    )
    moving = velocity + force_step * force_field.reshape(3, layers, rows, columns)
    for step_index in range(STEPS):
        moving = advance(extended_2(moving, (("gx", 2), ("gy", 3)), 1))
    fluid_bf = moving.astype(jnp.bfloat16).reshape(3, patch_count, patch)
    replies = jnp.einsum(
        "ps,cpq->scq", placing.astype(jnp.bfloat16), fluid_bf, preferred_element_type=jnp.float32
    ).astype(jnp.bfloat16)
    returned = lax.all_to_all(
        replies.reshape(device_count, per_owner, 3, patch),
        ("gx", "gy"),
        split_axis=0,
        concat_axis=0,
        tiled=True,
    ).reshape(slot_total, 3, patch)
    picked = jnp.einsum(
        "sr,scq->rcq", selector.astype(jnp.bfloat16), returned, preferred_element_type=jnp.float32
    ).astype(jnp.bfloat16)
    picked = picked.reshape(blocks, intersection, 3, patch)
    interp = jnp.einsum("bkcq,bkpq->bcp", picked, delta_weights, preferred_element_type=jnp.float32)
    return (moving, fiber_points + fiber_step * interp)


def solution(mesh):
    placed = (
        P(None, None, "gx", "gy"),
        P(("gx", "gy"), None, None),
        P(("gx", "gy")),
        P(("gx", "gy"), None),
        P(("gx", "gy"), None, None, None),
        P(("gx", "gy"), None, None),
        P(("gx", "gy"), None),
    )
    return jax.shard_map(
        shards,
        mesh=mesh,
        in_specs=placed,
        out_specs=(P(None, None, "gx", "gy"), P(("gx", "gy"), None, None)),
        check_vma=False,
    )
```

profile of v0, /device:TPU:1, one launch (start us, length us, event | category | flops | bytes accessed | tf_op | source)
XLA Modules:
  0.0 236.1 jit_solution(13579644840580795867)
XLA Ops:
  4.4 11.5 %all-to-all-start.1 = ((s32[128,1,2]{2,1,0:T(1,128)}), s32[128,1,2]{2,1,0:T(1,128)S(1)}, u32[]{:S(2)}, u32[]{:S(2)}) async-start(s32[128,1,2]{2,1,0:T(1,128)} %bitcast.7), calls=%async_computation.1 | async-start | bytes 131072 | tf_op jit(solution)/shard_map/all_to_all | solution.py:100
  16.7 18.5 %gather_fusion = f32[3072]{0:T(1024)S(1)} fusion(f32[8,3,128]{2,0,1:T(8,128)S(1)} %copy-done, s32[3072]{0:T(1024)S(1)} %reshape.82), kind=kCustom, calls=%fused_computation | custom fusion | bytes 61440 | tf_op jit(solution)/shard_map/jit(take_along_axis)/gather | solution.py:72
  35.2 4.6 %fusion.27 = f32[8,3,8,512]{3,1,2,0:T(4,128)S(1)} fusion(bf16[8,8,128,512]{3,2,1,0:T(8,128)(2,1)} %param.11, f32[8,3,128]{2,0,1:T(8,128)S(1)} %copy-done, f32[8,3,128]{2,1,0:T(4,128)S(1)} %reshape.85, s32[8,128]{1,0:T(8,128)S(1)} %get-tuple-element.15, s32[8,128]{1,0:T(8,128)S(1)} %broadcast_add_fusion, f32[8]{0:T(128)S(1)} %copy-done.6, ...), kind=kOutput, calls=%fused_computation.68 | convolution fusion | flops 25190400 | bytes 8815648 | tf_op jit(solution)/shard_map/bcp,bkpq->bkcq/dot_general | solution.py:75
  40.7 2.4 copy.69
  43.1 9.8 %all-to-all-start = ((f32[128,2,3,512]{3,1,2,0:T(2,128)}), f32[128,2,3,512]{3,1,2,0:T(2,128)S(1)}, u32[]{:S(2)}, u32[]{:S(2)}) async-start(f32[128,2,3,512]{3,1,2,0:T(2,128)} %copy.69), calls=%async_computation | async-start | bytes 3145728 | tf_op jit(solution)/shard_map/all_to_all | solution.py:93
  53.8 23.7 %all-to-all-done = f32[128,2,3,512]{3,1,2,0:T(2,128)S(1)} async-done(((f32[128,2,3,512]{3,1,2,0:T(2,128)}), f32[128,2,3,512]{3,1,2,0:T(2,128)S(1)}, u32[]{:S(2)}, u32[]{:S(2)}) %all-to-all-start) | async-done | bytes 1572896 | tf_op jit(solution)/shard_map/all_to_all | solution.py:93
  79.2 4.9 %multiply_bitcast_fusion = f32[3,1024,512]{1,2,0:T(8,128)} fusion(f32[256,3,512]{2,0,1:T(8,128)S(1)} %reshape.77, s32[256]{0:T(256)S(1)} %eq.73), kind=kOutput, calls=%fused_computation.29 | convolution fusion | flops 4833673216 | bytes 7865344 | tf_op jit(solution)/shard_map/ps,scq->cpq/dot_general | solution.py:111
  84.1 6.5 %copy.74 = f32[3,1024,512]{2,1,0:T(8,128)} copy(f32[3,1024,512]{1,2,0:T(8,128)} %multiply_bitcast_fusion) | data formatting | bytes 12582912 | tf_op jit(solution)/shard_map/mul | solution.py:114
  90.6 6.2 %add.99 = f32[3,32,32,512]{3,2,1,0:T(8,128)S(1)} add(f32[3,32,32,512]{3,2,1,0:T(8,128)} %param.7, f32[3,32,32,512]{3,2,1,0:T(8,128)} %bitcast.64) | non-fusion elementwise | flops 1572864 | bytes 18874368 | tf_op jit(solution)/shard_map/add | solution.py:114
  100.1 2.9 %slice_bitcast_fusion.5 = (f32[32,32,512]{2,1,0:T(8,128)}, f32[32,32,512]{2,1,0:T(8,128)}, f32[32,32,512]{2,1,0:T(8,128)}) fusion(f32[3,32,32,512]{3,2,1,0:T(8,128)S(1)} %add.99), kind=kLoop, calls=%fused_computation.35 | loop fusion | bytes 12582912 | tf_op jit(solution)/shard_map/mul | solution.py:53
  103.0 6.0 %fusion.47 = (f32[3,31,32,512]{3,2,1,0:T(8,128)}, f32[3,31,32,512]{3,2,1,0:T(8,128)}) fusion(f32[3,32,32,512]{3,2,1,0:T(8,128)S(1)} %add.99), kind=kLoop, calls=%fused_computation.94 | loop fusion | bytes 24379392 | tf_op jit(solution)/shard_map/jit(_roll_static)/slice | solution.py:41
  109.0 2.4 %collective-permute-start.1 = (f32[3,32,1,512]{3,2,1,0:T(1,128)}, f32[3,32,1,512]{3,2,1,0:T(1,128)S(1)}, u32[]{:S(2)}, u32[]{:S(2)}) collective-permute-start(f32[3,32,1,512]{3,2,1,0:T(1,128)} %get-tuple-element.32), channel_id=1, source_target_pairs={{0,8},{8,16},{16,24},{24,32},{32,40},{40,48},{48,56},{56,64},{64,7... | collective-permute-start | bytes 589832 | tf_op jit(solution)/shard_map/ppermute | solution.py:23
  117.3 2.9 %collective-permute-start.2 = (f32[3,32,32,1]{2,1,3,0:T(8,128)S(1)}, f32[3,32,32,1]{2,1,3,0:T(8,128)S(1)}, u32[]{:S(2)}, u32[]{:S(2)}) collective-permute-start(f32[3,32,32,1]{2,1,3,0:T(8,128)S(1)} %copy.75), channel_id=1, source_target_pairs={{1,0},{2,1},{3,2},{4,3},{5,4},{6,5},{7,6},{9,8},{10,9},{11,10},{12... | collective-permute-start | bytes 36872 | tf_op jit(solution)/shard_map/ppermute | solution.py:24
  125.9 20.1 %multiply_subtract_fusion.1 = f32[3,32,32,512]{3,2,1,0:T(8,128)S(1)} fusion(f32[3,32,32,512]{3,2,1,0:T(8,128)} %copy-done.2, f32[3,31,32,512]{3,2,1,0:T(8,128)} %get-tuple-element.35, f32[3,1,32,512]{3,2,1,0:T(8,128)S(1)} %get-tuple-element.37, f32[3,1,32,512]{3,2,1,0:T(8,128)S(1)} %get-tuple-element.36, f32[3,31,32,512]{3,2,1,0:T(8,128)} %get-tuple-element.34, ...), kind=kLoop, calls=%fused_computation.28 | loop fusion | flops 55050240 | bytes 31875072 | tf_op jit(solution)/shard_map/sub | solution.py:57
  146.4 2.8 %fusion.41 = (f32[3,32,32,1]{3,2,1,0:T(8,128)}, f32[3,32,32,1]{3,2,1,0:T(8,128)}) fusion(f32[3,32,32,512]{3,2,1,0:T(8,128)S(1)} %multiply_subtract_fusion.1), kind=kLoop, calls=%fused_computation.88 | loop fusion | bytes 49152 | tf_op jit(solution)/shard_map/slice | solution.py:21
  149.2 2.9 %slice_bitcast_fusion.2 = (f32[32,32,512]{2,1,0:T(8,128)}, f32[32,32,512]{2,1,0:T(8,128)}, f32[32,32,512]{2,1,0:T(8,128)}) fusion(f32[3,32,32,512]{3,2,1,0:T(8,128)S(1)} %multiply_subtract_fusion.1), kind=kLoop, calls=%fused_computation.32 | loop fusion | bytes 12582912 | tf_op jit(solution)/shard_map/mul | solution.py:53
  152.1 6.0 %fusion.43 = (f32[3,31,32,512]{3,2,1,0:T(8,128)}, f32[3,31,32,512]{3,2,1,0:T(8,128)}) fusion(f32[3,32,32,512]{3,2,1,0:T(8,128)S(1)} %multiply_subtract_fusion.1), kind=kLoop, calls=%fused_computation.90 | loop fusion | bytes 24379392 | tf_op jit(solution)/shard_map/jit(_roll_static)/slice | solution.py:41
  158.0 4.4 %collective-permute-start.5 = (f32[3,32,1,512]{3,2,1,0:T(1,128)S(1)}, f32[3,32,1,512]{3,2,1,0:T(1,128)S(1)}, u32[]{:S(2)}, u32[]{:S(2)}) collective-permute-start(f32[3,32,1,512]{3,2,1,0:T(1,128)S(1)} %get-tuple-element.18), channel_id=1, source_target_pairs={{0,8},{8,16},{16,24},{24,32},{32,40},{40,48},{48,56},{56,64},{64,7... | collective-permute-start | bytes 589832 | tf_op jit(solution)/shard_map/ppermute | solution.py:23
  167.8 2.2 collective-permute-start.7
  170.0 2.2 collective-permute-start.6
  173.2 2.2 collective-permute-done.6
  179.1 20.8 %fusion.40 = (bf16[3,32,32,512]{3,2,1,0:T(8,128)(2,1)S(1)}, f32[3,32,32,512]{3,2,1,0:T(8,128)}) fusion(f32[32,32,512]{2,1,0:T(8,128)} %get-tuple-element.26, f32[32,32,512]{2,1,0:T(8,128)} %get-tuple-element.25, f32[32,32,512]{2,1,0:T(8,128)S(1)} %copy-done.3, f32[3,32,32,512]{3,2,1,0:T(8,128)} %copy-done.1, f32[3,31,32,512]{3,2,1,0:T(8,128)} %get-tuple-element.21, ...), kind=kLoop, calls=%fused_computation.87 | loop fusion | flops 56623104 | bytes 35020800 | tf_op jit(solution)/shard_map/convert_element_type | solution.py:117
  201.8 26.9 %all_to_all.19 = bf16[128,2,3,512]{3,1,2,0:T(2,128)(2,1)S(1)} all-to-all(bf16[128,2,3,512]{3,1,2,0:T(2,128)(2,1)S(1)} %copy.83), channel_id=1, replica_groups=mesh['gx'=16,'gy'=8] {'gx','gy'}, dimensions={0} | all-to-all | bytes 1572864 | tf_op jit(solution)/shard_map/all_to_all | solution.py:121
  229.8 5.7 %fusion.6 = f32[8,3,128]{2,1,0:T(4,128)S(1)} fusion(bf16[8,8,128,512]{3,2,1,0:T(8,128)(2,1)} %param.11, bf16[8,8,3,512]{3,1,0,2:T(8,128)(2,1)S(1)} %fusion.4, f32[8,3,128]{2,0,1:T(8,128)S(1)} %copy-done), kind=kOutput, calls=%fused_computation.41 | convolution fusion | flops 25171968 | bytes 8609792 | tf_op jit(solution)/shard_map/bkcq,bkpq->bcp/dot_general | solution.py:132
  (64 shorter events, 37.0 us)
Async XLA Ops:
  0.6 16.1 %copy-start = (f32[8,3,128]{2,0,1:T(8,128)S(1)}, f32[8,3,128]{2,0,1:T(8,128)}, u32[]{:S(2)}) copy-start(f32[8,3,128]{2,0,1:T(8,128)} %param.8) | copy-start | bytes 36868
  4.4 38.7 %all-to-all-start.1 = ((s32[128,1,2]{2,1,0:T(1,128)}), s32[128,1,2]{2,1,0:T(1,128)S(1)}, u32[]{:S(2)}, u32[]{:S(2)}) async-start(s32[128,1,2]{2,1,0:T(1,128)} %bitcast.7), calls=%async_computation.1 | async-start | bytes 131072 | tf_op jit(solution)/shard_map/all_to_all | solution.py:100
  16.7 18.5 %copy-start.6 = (f32[8]{0:T(128)S(1)}, f32[8]{0:T(128)}, u32[]{:S(2)}) copy-start(f32[8]{0:T(128)} %param.9) | copy-start | bytes 100
  43.1 34.5 %all-to-all-start = ((f32[128,2,3,512]{3,1,2,0:T(2,128)}), f32[128,2,3,512]{3,1,2,0:T(2,128)S(1)}, u32[]{:S(2)}, u32[]{:S(2)}) async-start(f32[128,2,3,512]{3,1,2,0:T(2,128)} %copy.69), calls=%async_computation | async-start | bytes 3145728 | tf_op jit(solution)/shard_map/all_to_all | solution.py:93
  96.7 6.2 %copy-start.2 = (f32[3,32,32,512]{3,2,1,0:T(8,128)}, f32[3,32,32,512]{3,2,1,0:T(8,128)S(1)}, u32[]{:S(2)}) copy-start(f32[3,32,32,512]{3,2,1,0:T(8,128)S(1)} %add.99) | copy-start | bytes 18874372
  109.0 16.2 %collective-permute-start.1 = (f32[3,32,1,512]{3,2,1,0:T(1,128)}, f32[3,32,1,512]{3,2,1,0:T(1,128)S(1)}, u32[]{:S(2)}, u32[]{:S(2)}) collective-permute-start(f32[3,32,1,512]{3,2,1,0:T(1,128)} %get-tuple-element.32), channel_id=1, source_target_pairs={{0,8},{8,16},{16,24},{24,32},{32,40},{40,48},{48,56},{56,64},{64,7... | collective-permute-start | bytes 589832 | tf_op jit(solution)/shard_map/ppermute | solution.py:23
  111.4 13.8 %collective-permute-start = (f32[3,32,1,512]{3,2,1,0:T(1,128)}, f32[3,32,1,512]{3,2,1,0:T(1,128)S(1)}, u32[]{:S(2)}, u32[]{:S(2)}) collective-permute-start(f32[3,32,1,512]{3,2,1,0:T(1,128)} %get-tuple-element.33), channel_id=1, source_target_pairs={{8,0},{16,8},{24,16},{32,24},{40,32},{48,40},{56,48},{64,56},{72,6... | collective-permute-start | bytes 589832 | tf_op jit(solution)/shard_map/ppermute | solution.py:24
  115.4 8.0 %collective-permute-start.3 = (f32[3,32,32,1]{2,1,3,0:T(8,128)S(1)}, f32[3,32,32,1]{2,1,3,0:T(8,128)S(1)}, u32[]{:S(2)}, u32[]{:S(2)}) collective-permute-start(f32[3,32,32,1]{2,1,3,0:T(8,128)S(1)} %copy.77), channel_id=1, source_target_pairs={{0,1},{1,2},{2,3},{3,4},{4,5},{5,6},{6,7},{8,9},{9,10},{10,11},{11... | collective-permute-start | bytes 36872 | tf_op jit(solution)/shard_map/ppermute | solution.py:23
  117.3 5.4 %collective-permute-start.2 = (f32[3,32,32,1]{2,1,3,0:T(8,128)S(1)}, f32[3,32,32,1]{2,1,3,0:T(8,128)S(1)}, u32[]{:S(2)}, u32[]{:S(2)}) collective-permute-start(f32[3,32,32,1]{2,1,3,0:T(8,128)S(1)} %copy.75), channel_id=1, source_target_pairs={{1,0},{2,1},{3,2},{4,3},{5,4},{6,5},{7,6},{9,8},{10,9},{11,10},{12... | collective-permute-start | bytes 36872 | tf_op jit(solution)/shard_map/ppermute | solution.py:24
  125.2 0.7 copy-start.4
  125.2 0.7 copy-start.5
  146.0 6.1 %copy-start.1 = (f32[3,32,32,512]{3,2,1,0:T(8,128)}, f32[3,32,32,512]{3,2,1,0:T(8,128)S(1)}, u32[]{:S(2)}) copy-start(f32[3,32,32,512]{3,2,1,0:T(8,128)S(1)} %multiply_subtract_fusion.1) | copy-start | bytes 18874372
  158.0 21.0 %copy-start.3 = (f32[32,32,512]{2,1,0:T(8,128)S(1)}, f32[32,32,512]{2,1,0:T(8,128)}, u32[]{:S(2)}) copy-start(f32[32,32,512]{2,1,0:T(8,128)} %get-tuple-element.24) | copy-start | bytes 6291460
  158.0 21.0 %collective-permute-start.5 = (f32[3,32,1,512]{3,2,1,0:T(1,128)S(1)}, f32[3,32,1,512]{3,2,1,0:T(1,128)S(1)}, u32[]{:S(2)}, u32[]{:S(2)}) collective-permute-start(f32[3,32,1,512]{3,2,1,0:T(1,128)S(1)} %get-tuple-element.18), channel_id=1, source_target_pairs={{0,8},{8,16},{16,24},{24,32},{32,40},{40,48},{48,56},{56,64},{64,7... | collective-permute-start | bytes 589832 | tf_op jit(solution)/shard_map/ppermute | solution.py:23
  162.4 16.6 %collective-permute-start.4 = (f32[3,32,1,512]{3,2,1,0:T(1,128)S(1)}, f32[3,32,1,512]{3,2,1,0:T(1,128)S(1)}, u32[]{:S(2)}, u32[]{:S(2)}) collective-permute-start(f32[3,32,1,512]{3,2,1,0:T(1,128)S(1)} %get-tuple-element.19), channel_id=1, source_target_pairs={{8,0},{16,8},{24,16},{32,24},{40,32},{48,40},{56,48},{64,56},{72,6... | collective-permute-start | bytes 589832 | tf_op jit(solution)/shard_map/ppermute | solution.py:24
  167.8 9.4 %collective-permute-start.7 = (f32[3,32,32,1]{2,1,3,0:T(8,128)S(1)}, f32[3,32,32,1]{2,1,3,0:T(8,128)S(1)}, u32[]{:S(2)}, u32[]{:S(2)}) collective-permute-start(f32[3,32,32,1]{2,1,3,0:T(8,128)S(1)} %copy.81), channel_id=1, source_target_pairs={{0,1},{1,2},{2,3},{3,4},{4,5},{5,6},{6,7},{8,9},{9,10},{10,11},{11... | collective-permute-start | bytes 36872 | tf_op jit(solution)/shard_map/ppermute | solution.py:23
  170.0 5.4 %collective-permute-start.6 = (f32[3,32,32,1]{2,1,3,0:T(8,128)S(1)}, f32[3,32,32,1]{2,1,3,0:T(8,128)S(1)}, u32[]{:S(2)}, u32[]{:S(2)}) collective-permute-start(f32[3,32,32,1]{2,1,3,0:T(8,128)S(1)} %copy.79), channel_id=1, source_target_pairs={{1,0},{2,1},{3,2},{4,3},{5,4},{6,5},{7,6},{9,8},{10,9},{11,10},{12... | collective-permute-start | bytes 36872 | tf_op jit(solution)/shard_map/ppermute | solution.py:24
where the time goes:
time: 237 us; the launch traced here: 236 us
  local copies, waits for them, and re-layouts  73.4 us (31%)
  other arithmetic  50.3 us (21%)
  starting transfers between devices  39.9 us (17%)
  waiting for transfers between devices  27.3 us (12%)
  blocking collectives  26.9 us (11%)
  matrix products  17.4 us (7%)
    all_to_all x1, blocking collectives, shards(): lax.all_to_all(replies.reshape(device_count, per_owner, 3, patch), ('gx',...  26.9 us
    all_to_all x1, waiting for transfers between devices, shards(): lax.all_to_all(outgoing.reshape(device_count, per_owner, 3, patch), ('gx'...  23.7 us
    convert_element_type x1, other arithmetic, shards(): fluid_bf = moving.astype(jnp.bfloat16).reshape(3, patch_count, patch)  20.8 us
    sub x1, other arithmetic, advance(): return middle + viscosity * laplace - transport_rate * transport  20.1 us
    gather x3, local copies, waits for them, and re-layouts, shards(): partner_points = jnp.take_along_axis(fiber_points, partner_full, axis=2)  18.5 us
    slice x4, local copies, waits for them, and re-layouts, advance(): above_cells = jnp.roll(middle, -1, axis=1)  14.1 us
    all_to_all x1, starting transfers between devices, shards(): lax.all_to_all(slot_patch.reshape(device_count, per_owner), ('gx', 'gy'),...  11.5 us
    ppermute x4, starting transfers between devices, extended_2(): lax.ppermute(last, axis, up)  10.9 us
  transfers between devices with their start and end apart: 10, of which 3 were waited for; matrix products, arithmetic and copies ran while one was open for 18% of the time, Pallas kernels for 0%

commit v1 on v0

v1 whole, which is shorter than its diff:
```python
import functools

import jax
import jax.numpy as jnp
from jax import lax
from jax.experimental import pallas as pl
from jax.experimental.pallas import tpu as pltpu
from jax.sharding import PartitionSpec as P

viscosity = 0.1
transport_rate = 0.1
force_step = 0.5
fiber_step = 0.25

F32 = jnp.float32
BF16 = jnp.bfloat16
LANES = 128
BELOW, ABOVE = 2, 10


def dot(a, b):
    return jnp.dot(a, b, preferred_element_type=F32)


def iota(shape, axis):
    return lax.broadcasted_iota(jnp.int32, shape, axis)


def spread_kernel(gy_size, slots, pts, stiff, links, owners, patch_slots, dw, out, dest_out, force, rows):
    b = pl.program_id(0)
    blocks, points = links.shape
    inter = owners.shape[1]
    entries = blocks * inter

    @pl.when(b == 0)
    def _():
        partner = lax.rem(iota((blocks, points), 1) + links[...], points)
        for c in range(3):
            own = pts[c]
            force[c] = jnp.take_along_axis(own, partner, axis=1) - own

    stiffness = stiff[b]
    group = iota((inter, inter * points), 0)
    column = iota((inter, inter * points), 1) // points
    parts = []
    for c in range(3):
        row = (stiffness * force[c, pl.ds(b, 1), :]).astype(BF16).astype(F32)
        wide = jnp.concatenate([jnp.broadcast_to(row, (inter, points))] * inter, axis=1)
        parts.append(jnp.where(group == column, wide, 0.0))
    parts.append(jnp.zeros_like(parts[0]))
    spread = dot(jnp.concatenate(parts, axis=0).astype(BF16), dw[0])
    for c in range(3):
        rows[c, pl.ds(pl.multiple_of(b * inter, inter), inter), :] = spread[c * inter : (c + 1) * inter]

    @pl.when(b == blocks - 1)
    def _():
        pick_block = (iota((entries, blocks), 0) // inter == iota((entries, blocks), 1)).astype(BF16)
        pick_k = lax.rem(iota((entries, inter), 0), inter) == iota((entries, inter), 1)

        def as_column(table):
            spread_rows = dot(pick_block, table.astype(F32).astype(BF16))
            return jnp.sum(jnp.where(pick_k, spread_rows, 0.0), axis=1, keepdims=True)

        owner = as_column(owners[...])
        code = patch_slots[...] + 1
        high, low = as_column(code // 32), as_column(lax.rem(code, 32))
        owner_wide = jnp.broadcast_to(owner, (entries, LANES))
        owner_row = jnp.transpose(
            jnp.concatenate([owner_wide, jnp.zeros((LANES - entries, LANES), F32)], axis=0)
        )[:entries, :entries]
        same = (owner_wide[:, :entries] == owner_row) & (iota((entries, entries), 1) < iota((entries, entries), 0))
        rank = jnp.sum(jnp.where(same, 1.0, 0.0), axis=1, keepdims=True)
        dest = owner * 2.0 + rank
        dest_wide = jnp.broadcast_to(dest, (entries, LANES))
        dest_out[...] = dest_wide
        padded = jnp.concatenate([dest_wide, jnp.full((LANES - entries, LANES), -8.0, F32)], axis=0)
        dest_row = jnp.transpose(padded)[0:1, :entries].astype(jnp.int32)
        position = lax.rem(dest_row // 2, gy_size)
        slot = iota((slots, entries), 0)
        here = (slot == dest_row).astype(F32).astype(BF16)
        to_above = ((slot == dest_row + 2) & (position < gy_size - 1)).astype(F32).astype(BF16)
        to_below = ((slot == dest_row - 2) & (position > 0)).astype(F32).astype(BF16)
        lane = iota((entries, LANES), 1)

        def digits(at):
            return jnp.where(lane == at, high, 0.0) + jnp.where(lane == at + 1, low, 0.0)

        own_head, above_head, below_head = digits(0), digits(BELOW), digits(ABOVE)
        patch = rows.shape[2]
        for c in range(3):
            tail = pltpu.roll(rows[c, :, patch - LANES :], BELOW + 4 + 2 * c, axis=1)
            at = BELOW + 2 + 2 * c
            above_head += jnp.where((lane == at) | (lane == at + 1), tail, 0.0)
            at = ABOVE + 2 + 2 * c
            start = pltpu.roll(rows[c, :, :LANES], at, axis=1)
            below_head += jnp.where((lane == at) | (lane == at + 1), start, 0.0)
            out[:, c * patch : (c + 1) * patch] = dot(here, rows[c].astype(BF16)).astype(BF16)
        head = dot(here, own_head.astype(BF16))
        head += dot(to_above, above_head.astype(BF16))
        head += dot(to_below, below_head.astype(BF16))
        out[:, 3 * patch : 3 * patch + LANES] = head.astype(BF16)
        out[:, 3 * patch + LANES :] = jnp.zeros((slots, patch - LANES), BF16)


def place_kernel(layer_rows, velocity, edge, received, out, low_rows, high_rows, low_f, high_f):
    step = pl.program_id(0)
    rows, patch = velocity.shape[1], velocity.shape[2]
    slots = received.shape[0]
    layers = rows // layer_rows
    head = received[:, 3 * patch : 3 * patch + LANES].astype(F32)
    head_t = jnp.transpose(head)
    lane = iota((slots, LANES), 1)

    def onehot(at):
        slot = (head_t[at : at + 1] * 32.0 + head_t[at + 1 : at + 2] - 1.0).astype(jnp.int32)
        return (iota((rows, slots), 0) + step * rows == slot).astype(F32).astype(BF16)

    here, below, above = onehot(0), onehot(BELOW), onehot(ABOVE)
    for c in range(3):
        placed = dot(here, received[:, c * patch : (c + 1) * patch])
        out[c, :, :patch] = velocity[c] + force_step * placed
        tail = pltpu.roll(head, LANES - 4 - BELOW - 2 * c, axis=1)
        tail = jnp.where(lane >= LANES - 2, tail, 0.0).astype(BF16)
        start = pltpu.roll(head, LANES - (ABOVE + 2 + 2 * c), axis=1)
        start = jnp.where(lane < 2, start, 0.0).astype(BF16)
        out[c, :, patch:] = edge[c] + force_step * (dot(below, tail) + dot(above, start))
        for j in range(2):
            for z in range(layers):
                at = pl.ds(step * layers + z, 1)
                low_f[c, j, at, :] = out[c, z * layer_rows + j : z * layer_rows + j + 1, :]
                top = (z + 1) * layer_rows - 2 + j
                high_f[c, j, at, :] = out[c, top : top + 1, :]

    @pl.when(step == pl.num_programs(0) - 1)
    def _():
        low_rows[...] = low_f[...].astype(BF16)
        high_rows[...] = high_f[...].astype(BF16)


def update(centre, weights, c, east, west, north, south, up, down):
    (px, mx), (py, my), (pz, mz) = weights
    keep = 1.0 - 6.0 * viscosity
    return keep * centre[c] + px * east + mx * west + py * north + my * south + pz * up + mz * down


def mix(centre):
    return [(viscosity - transport_rate * v, viscosity + transport_rate * v) for v in centre]


def sweep_kernel(sides, u0, below_x, above_x, head, fluid, replies, u1, halo, mid):
    layers, rows, wide = u0.shape[1:]
    patch = wide - LANES
    slots = head.shape[0]
    lane = iota((8, LANES), 1)
    mask = jnp.where(lane == 0, sides[3], 0.0) + jnp.where(lane == LANES - 1, sides[2], 0.0)
    sub = iota((8, wide), 0)

    for c in range(3):
        for j in range(2):
            halo[0, c, j] = below_x[c, j].astype(F32)
            halo[1, c, j] = above_x[c, j].astype(F32)
    mask_all = mask[0:1]
    for side in range(2):
        near = 1 - side
        centre = [halo[side, c, near] for c in range(3)]
        weights = mix(centre)
        for c in range(3):
            inner = u0[c, :, 0 if side == 0 else rows - 1, :]
            outer = halo[side, c, 1 - near]
            east, west = (inner, outer) if side == 0 else (outer, inner)
            v = centre[c]
            new = update(
                centre, weights, c, east, west,
                pltpu.roll(v, wide - 1, axis=1), pltpu.roll(v, 1, axis=1),
                pltpu.roll(v, layers - 1, axis=0), pltpu.roll(v, 1, axis=0),
            ) * sides[side]
            mid[side, c, :, :patch] = new[:, :patch]
            mid[side, c, :, patch:] = new[:, patch:] * mask_all

    def sweep(source, low_row, high_row, store, keep):
        @pl.loop(0, layers)
        def _(z):
            z_up = jnp.where(z == layers - 1, 0, z + 1)
            z_down = jnp.where(z == 0, layers - 1, z - 1)
            for x in range(0, rows, 8):
                centre = [source[c, z, x : x + 8, :] for c in range(3)]
                weights = mix([v[:, :keep] for v in centre])
                for c in range(3):
                    v = centre[c]
                    if x + 8 < rows:
                        east = source[c, z, x + 1 : x + 9, :keep]
                    else:
                        east = jnp.where(sub[:, :keep] == 7, high_row(c, z), pltpu.roll(v[:, :keep], 7, axis=0))
                    if x > 0:
                        west = source[c, z, x - 1 : x + 7, :keep]
                    else:
                        west = jnp.where(sub[:, :keep] == 0, low_row(c, z), pltpu.roll(v[:, :keep], 1, axis=0))
                    new = update(
                        [w[:, :keep] for w in centre], weights, c, east, west,
                        pltpu.roll(v, wide - 1, axis=1)[:, :keep], pltpu.roll(v, 1, axis=1)[:, :keep],
                        source[c, z_up, x : x + 8, :keep], source[c, z_down, x : x + 8, :keep],
                    )
                    store(c, z, x, new)

    def store_first(c, z, x, new):
        u1[c, z, x : x + 8, :patch] = new[:, :patch]
        u1[c, z, x : x + 8, patch:] = new[:, patch:] * mask

    def store_last(c, z, x, new):
        fluid[c, pl.ds(pl.multiple_of(z * rows + x, 8), 8), :] = new

    sweep(
        u0,
        lambda c, z: halo[0, c, 1, pl.ds(z, 1), :],
        lambda c, z: halo[1, c, 0, pl.ds(z, 1), :],
        store_first,
        wide,
    )
    sweep(
        u1,
        lambda c, z: mid[0, c, pl.ds(z, 1), :patch],
        lambda c, z: mid[1, c, pl.ds(z, 1), :patch],
        store_last,
        patch,
    )

    heads = head[...].astype(F32)
    slot = (heads[:, 0:1] * 32.0 + heads[:, 1:2] - 1.0).astype(jnp.int32)
    chunk = 256
    for c in range(3):
        total = jnp.zeros((slots, patch), F32)
        for first in range(0, layers * rows, chunk):
            pick = (iota((slots, chunk), 1) + first == slot).astype(F32).astype(BF16)
            total += dot(pick, fluid[c, first : first + chunk, :].astype(BF16))
        replies[:, c * patch : (c + 1) * patch] = total.astype(BF16)


def gather_kernel(pts, dest, returned, dw, out, picked, moved):
    b = pl.program_id(0)
    entries, slots = dest.shape[0], returned.shape[0]
    inter = entries // pl.num_programs(0)
    patch, points = dw.shape[2], pts.shape[2]

    @pl.when(b == 0)
    def _():
        to = dest[:, 0:1].astype(jnp.int32)
        pick = (iota((entries, slots), 1) == to).astype(F32).astype(BF16)
        for c in range(3):
            picked[c] = dot(pick, returned[:, c * patch : (c + 1) * patch])

    at = pl.ds(pl.multiple_of(b * inter, inter), inter)
    parts = [picked[c, at, :] for c in range(3)]
    parts.append(jnp.zeros_like(parts[0]))
    every = lax.dot_general(
        jnp.concatenate(parts, axis=0).astype(BF16), dw[0], (((1,), (1,)), ((), ())), preferred_element_type=F32
    )
    group = iota((inter, inter * points), 0)
    column = iota((inter, inter * points), 1) // points
    for c in range(3):
        own = jnp.where(group == column, every[c * inter : (c + 1) * inter], 0.0)
        folded = own[:, :points]
        for k in range(1, inter):
            folded = folded + own[:, k * points : (k + 1) * points]
        moved[c, pl.ds(b, 1), :] = jnp.sum(folded, axis=0, keepdims=True)

    @pl.when(b == pl.num_programs(0) - 1)
    def _():
        for c in range(3):
            out[c] = pts[c] + fiber_step * moved[c]


def whole(shape):
    return pl.BlockSpec(shape, lambda *_: (0,) * len(shape))


def shards(velocity, fiber_points, stiffness, links, delta_weights, owners, patch_slots):
    blocks, inter, points, patch = delta_weights.shape
    layers, rows, columns = velocity.shape[1:]
    gx_size, gy_size = lax.axis_size("gx"), lax.axis_size("gy")
    devices = gx_size * gy_size
    entries, slots, cells = blocks * inter, devices * 2, layers * rows
    wide = patch + LANES
    mb = 1 << 20
    pts = fiber_points.transpose(1, 0, 2)
    dw = delta_weights.reshape(blocks, inter * points, patch)
    smem = pl.BlockSpec(memory_space=pltpu.SMEM)

    outgoing, dest = pl.pallas_call(
        functools.partial(spread_kernel, gy_size, slots),
        grid=(blocks,),
        in_specs=[
            whole((3, blocks, points)),
            smem,
            whole((blocks, points)),
            whole((blocks, inter)),
            whole((blocks, inter)),
            pl.BlockSpec((1, inter * points, patch), lambda b: (b, 0, 0)),
        ],
        out_specs=[whole((slots, 4 * patch)), whole((entries, LANES))],
        out_shape=[
            jax.ShapeDtypeStruct((slots, 4 * patch), BF16),
            jax.ShapeDtypeStruct((entries, LANES), F32),
        ],
        scratch_shapes=[pltpu.VMEM((3, blocks, points), F32), pltpu.VMEM((3, entries, patch), F32)],
        compiler_params=pltpu.CompilerParams(vmem_limit_bytes=16 * mb),
        cost_estimate=pl.CostEstimate(flops=10**9, bytes_accessed=9 * mb, transcendentals=0),
        name="spread",
    )(pts, stiffness, links, owners.reshape(blocks, inter), patch_slots, dw)

    def exchange(rows_out):
        width = rows_out.shape[1]
        return lax.all_to_all(
            rows_out.reshape(devices, 2, width), ("gx", "gy"), split_axis=0, concat_axis=0, tiled=True
        ).reshape(slots, width)

    received = exchange(outgoing)

    ahead = [(i + 1, i) for i in range(gy_size - 1)]
    behind = [(i, i + 1) for i in range(gy_size - 1)]
    flat = velocity.reshape(3, cells, columns)
    first = lax.ppermute(flat[:, :, :2].transpose(0, 2, 1), "gy", ahead)
    last = lax.ppermute(flat[:, :, columns - 2 :].transpose(0, 2, 1), "gy", behind)
    edge = jnp.concatenate(
        [first.transpose(0, 2, 1), jnp.zeros((3, cells, LANES - 4), F32), last.transpose(0, 2, 1)], axis=2
    )

    steps = 4
    part = cells // steps
    u0, low_rows, high_rows = pl.pallas_call(
        functools.partial(place_kernel, rows),
        grid=(steps,),
        in_specs=[
            pl.BlockSpec((3, part, patch), lambda s: (0, s, 0)),
            pl.BlockSpec((3, part, LANES), lambda s: (0, s, 0)),
            whole((slots, 4 * patch)),
        ],
        out_specs=[
            pl.BlockSpec((3, part, wide), lambda s: (0, s, 0)),
            whole((3, 2, layers, wide)),
            whole((3, 2, layers, wide)),
        ],
        out_shape=[
            jax.ShapeDtypeStruct((3, cells, wide), F32),
            jax.ShapeDtypeStruct((3, 2, layers, wide), BF16),
            jax.ShapeDtypeStruct((3, 2, layers, wide), BF16),
        ],
        scratch_shapes=[pltpu.VMEM((3, 2, layers, wide), F32)] * 2,
        compiler_params=pltpu.CompilerParams(vmem_limit_bytes=24 * mb),
        cost_estimate=pl.CostEstimate(flops=10**9, bytes_accessed=17 * mb, transcendentals=0),
        name="place",
    )(flat, edge, received)

    up = [(i, i + 1) for i in range(gx_size - 1)]
    below_x = lax.ppermute(high_rows, "gx", up)
    above_x = lax.ppermute(low_rows, "gx", [(b, a) for a, b in up])

    gx, gy = lax.axis_index("gx"), lax.axis_index("gy")
    sides = jnp.stack([gx > 0, gx < gx_size - 1, gy > 0, gy < gy_size - 1]).astype(F32)
    vmem = pl.BlockSpec(memory_space=pltpu.VMEM)
    fluid, replies = pl.pallas_call(
        sweep_kernel,
        in_specs=[smem, vmem, vmem, vmem, vmem],
        out_specs=[vmem, vmem],
        out_shape=[
            jax.ShapeDtypeStruct((3, cells, patch), F32),
            jax.ShapeDtypeStruct((slots, 3 * patch), BF16),
        ],
        scratch_shapes=[
            pltpu.VMEM((3, layers, rows, wide), F32),
            pltpu.VMEM((2, 3, 2, layers, wide), F32),
            pltpu.VMEM((2, 3, layers, wide), F32),
        ],
        compiler_params=pltpu.CompilerParams(vmem_limit_bytes=48 * mb),
        cost_estimate=pl.CostEstimate(flops=2 * 10**9, bytes_accessed=16 * mb, transcendentals=0),
        name="sweeps",
    )(sides, u0.reshape(3, layers, rows, wide), below_x, above_x, received[:, 3 * patch : 3 * patch + LANES])

    returned = exchange(replies)
    moved = pl.pallas_call(
        gather_kernel,
        grid=(blocks,),
        in_specs=[
            whole((3, blocks, points)),
            whole((entries, LANES)),
            whole((slots, 3 * patch)),
            pl.BlockSpec((1, inter * points, patch), lambda b: (b, 0, 0)),
        ],
        out_specs=whole((3, blocks, points)),
        out_shape=jax.ShapeDtypeStruct((3, blocks, points), F32),
        scratch_shapes=[pltpu.VMEM((3, entries, patch), F32), pltpu.VMEM((3, blocks, points), F32)],
        compiler_params=pltpu.CompilerParams(vmem_limit_bytes=16 * mb),
        cost_estimate=pl.CostEstimate(flops=10**9, bytes_accessed=9 * mb, transcendentals=0),
        name="interp",
    )(pts, dest, returned, dw)
    return fluid.reshape(3, layers, rows, columns), moved.transpose(1, 0, 2)


def solution(mesh):
    placed = (
        P(None, None, "gx", "gy"),
        P(("gx", "gy"), None, None),
        P(("gx", "gy")),
        P(("gx", "gy"), None),
        P(("gx", "gy"), None, None, None),
        P(("gx", "gy"), None, None),
        P(("gx", "gy"), None),
    )
    return jax.shard_map(
        shards,
        mesh=mesh,
        in_specs=placed,
        out_specs=(P(None, None, "gx", "gy"), P(("gx", "gy"), None, None)),
        check_vma=False,
    )
```

time: 237 us -> 124 us (0.52)
  other arithmetic: 50.3 us -> 2.43 us
  local copies, waits for them, and re-layouts: 73.4 us -> 28.9 us
  Pallas kernels: 0 us -> 32.9 us
  waiting for transfers between devices: 27.3 us -> 8.56 us
  starting transfers between devices: 39.9 us -> 21.7 us
  matrix products: 17.4 us -> 0 us
    pallas_call x0 -> x4, Pallas kernels: none -> 32.9 us  [the longest x1 20.6 us: shards(): pl.pallas_call(sweep_kernel, in_specs=[smem, vmem, vmem, vmem, vmem], out...]
    slice x12 -> x1, local copies, waits for them, and re-layouts: 27.3 us -> 0.02 us  [shards(): received[:, 3 * patch:3 * patch + LANES]]
    all_to_all x2 -> x1, waiting for transfers between devices: 23.7 us -> 1.52 us  [exchange(): lax.all_to_all(rows_out.reshape(devices, 2, width), ('gx', 'gy'), split_a...]
    convert_element_type x1, other arithmetic: 20.8 us -> 0.08 us  [shards(): jnp.stack([gx > 0, gx < gx_size - 1, gy > 0, gy < gy_size - 1]).astype(F32)]
    sub x1 -> x0, other arithmetic: 20.1 us -> none  [advance(): return middle + viscosity * laplace - transport_rate * transport]
    gather x3 -> x0, local copies, waits for them, and re-layouts: 18.5 us -> none  [shards(): partner_points = jnp.take_along_axis(fiber_points, partner_full, axis=2)]
    dot_general x6 -> x0, matrix products: 17.4 us -> none  [the longest x1 5.66 us: shards(): jnp.einsum('bkcq,bkpq->bcp', picked, delta_weights, preferred_element_typ...]
    unnamed x16 -> x20, local copies, waits for them, and re-layouts: 1.88 us -> 16 us
  transfers between devices with their start and end apart: 10 -> 5, of which waited for: 3 -> 3; matrix products, arithmetic and copies ran while one was open for 18% -> 10% of each run, Pallas kernels for 0% -> 0%
where the time goes in v1:
time: 124 us; the launch traced here: 123 us
  Pallas kernels  32.9 us (27%)
  local copies, waits for them, and re-layouts  28.9 us (23%)
  blocking collectives  28 us (23%)
  starting transfers between devices  21.7 us (18%)
  waiting for transfers between devices  8.56 us (7%)
  other arithmetic  2.43 us (2%)
    all_to_all x1, blocking collectives, exchange(): lax.all_to_all(rows_out.reshape(devices, 2, width), ('gx', 'gy'), split_a...  28 us
    pallas_call x1, Pallas kernels, shards(): pl.pallas_call(sweep_kernel, in_specs=[smem, vmem, vmem, vmem, vmem], out...  20.6 us
    unnamed x20, local copies, waits for them, and re-layouts  16 us
    all_to_all x1, starting transfers between devices, exchange(): lax.all_to_all(rows_out.reshape(devices, 2, width), ('gx', 'gy'), split_a...  12 us
    transpose x2, local copies, waits for them, and re-layouts, shards(): first = lax.ppermute(flat[:, :, :2].transpose(0, 2, 1), 'gy', ahead)  5.41 us
    pallas_call x1, Pallas kernels, shards(): pl.pallas_call(gather_kernel, grid=(blocks,), in_specs=[whole((3, blocks,...  4.36 us
    pallas_call x1, Pallas kernels, shards(): pl.pallas_call(functools.partial(place_kernel, rows), grid=(steps,), in_s...  4.11 us
    pallas_call x1, Pallas kernels, shards(): pl.pallas_call(functools.partial(spread_kernel, gy_size, slots), grid=(bl...  3.82 us
  transfers between devices with their start and end apart: 5, of which 3 were waited for; matrix products, arithmetic and copies ran while one was open for 10% of the time, Pallas kernels for 0%

profile of v1, /device:TPU:1, one launch (start us, length us, event | category | flops | bytes accessed | tf_op | source)
XLA Modules:
  0.0 123.3 jit_solution(504409606300180835)
XLA Ops:
  0.6 3.4 %copy-done = bf16[8,8,128,512]{3,2,1,0:T(8,128)(2,1)S(1)} copy-done((bf16[8,8,128,512]{3,2,1,0:T(8,128)(2,1)S(1)}, bf16[8,8,128,512]{3,2,1,0:T(8,128)(2,1)}, u32[]{:S(2)}) %copy-start) | copy-done | bytes 8388632
  7.4 3.8 %spread.1 = (bf16[256,2048]{1,0:T(8,128)(2,1)S(1)}, f32[64,128]{1,0:T(8,128)S(1)}) custom-call(f32[3,8,128]{2,1,0:T(8,128)S(1)} %bitcast.22, f32[8]{0:T(128)S(1)} %copy-done.9, s32[8,128]{1,0:T(8,128)S(1)} %copy-done.6, s32[8,8]{1,0:T(8,128)S(1)} %bitcast.24, s32[8,8]{1,0:T(8,128)S(1)} %copy-done.8, bf16[8,1024,512]{2,1,0:T(8,128)(2,1)S(1)} %bitcast.17), custom_call_target="tpu_custom_call" | custom-call | flops 1000000000 | bytes 9437184 | tf_op jit(solution)/shard_map/spread/pallas_call | solution.py:288
  11.3 1.5 %reshape.34 = bf16[128,2,2048]{2,1,0:T(2,128)(2,1)} reshape(bf16[256,2048]{1,0:T(8,128)(2,1)S(1)} %get-tuple-element.9) | data formatting | bytes 2097152 | tf_op jit(solution)/shard_map/reshape | solution.py:313
  12.8 12.0 %all-to-all-start = ((bf16[128,2,2048]{2,1,0:T(2,128)(2,1)}), bf16[128,2,2048]{2,1,0:T(2,128)(2,1)}, u32[]{:S(2)}, u32[]{:S(2)}) async-start(bf16[128,2,2048]{2,1,0:T(2,128)(2,1)} %reshape.34), calls=%async_computation | async-start | bytes 2097152 | tf_op jit(solution)/shard_map/all_to_all | solution.py:312
  24.7 3.5 %slice_bitcast_fusion.1 = (f32[3,2,1024]{1,2,0:T(8,128)}, f32[3,2,1024]{1,2,0:T(8,128)S(1)}) fusion(f32[3,1024,512]{2,1,0:T(8,128)} %bitcast.19), kind=kLoop, calls=%fused_computation.1 | loop fusion | bytes 98304 | tf_op jit(solution)/shard_map/transpose | solution.py:321
  28.3 1.9 %copy.9 = f32[3,2,1024]{2,1,0:T(2,128)S(1)} copy(f32[3,2,1024]{1,2,0:T(8,128)} %get-tuple-element.16) | data formatting | bytes 49152 | tf_op jit(solution)/shard_map/transpose | solution.py:321
  30.1 3.1 %collective-permute-start = (f32[3,2,1024]{2,1,0:T(2,128)S(1)}, f32[3,2,1024]{2,1,0:T(2,128)S(1)}, u32[]{:S(2)}, u32[]{:S(2)}) collective-permute-start(f32[3,2,1024]{2,1,0:T(2,128)S(1)} %copy.9), channel_id=1, source_target_pairs={{1,0},{2,1},{3,2},{4,3},{5,4},{6,5},{7,6},{9,8},{10,9},{11,10},{12... | collective-permute-start | bytes 73736 | tf_op jit(solution)/shard_map/ppermute | solution.py:321
  33.7 2.5 %collective-permute-start.1 = (f32[3,2,1024]{2,1,0:T(2,128)S(1)}, f32[3,2,1024]{2,1,0:T(2,128)S(1)}, u32[]{:S(2)}, u32[]{:S(2)}) collective-permute-start(f32[3,2,1024]{2,1,0:T(2,128)S(1)} %copy.11), channel_id=1, source_target_pairs={{0,1},{1,2},{2,3},{3,4},{4,5},{5,6},{6,7},{8,9},{9,10},{10,11},{11... | collective-permute-start | bytes 73736 | tf_op jit(solution)/shard_map/ppermute | solution.py:322
  36.3 1.7 %copy.10 = f32[3,2,1024]{1,2,0:T(8,128)} copy(f32[3,2,1024]{2,1,0:T(2,128)S(1)} %collective-permute-done) | data formatting | bytes 49152 | tf_op jit(solution)/shard_map/ppermute | solution.py:321
  38.0 1.7 %copy.12 = f32[3,2,1024]{1,2,0:T(8,128)} copy(f32[3,2,1024]{2,1,0:T(2,128)S(1)} %collective-permute-done.1) | data formatting | bytes 49152 | tf_op jit(solution)/shard_map/ppermute | solution.py:322
  39.7 2.4 %pad_maximum_fusion.edge = f32[3,1024,128]{2,1,0:T(8,128)S(1)} fusion(f32[3,1024,2]{2,1,0:T(8,128)} %bitcast.26, f32[3,1024,2]{2,1,0:T(8,128)} %bitcast.25, f32[128]{0:T(128)S(1)} %pad.1.clone), kind=kLoop, calls=%fused_computation.2 | loop fusion | flops 786432 | bytes 1622528 | tf_op jit(solution)/shard_map/concatenate | solution.py:323
  42.0 1.5 %all-to-all-done = bf16[128,2,2048]{2,1,0:T(2,128)(2,1)} async-done(((bf16[128,2,2048]{2,1,0:T(2,128)(2,1)}), bf16[128,2,2048]{2,1,0:T(2,128)(2,1)}, u32[]{:S(2)}, u32[]{:S(2)}) %all-to-all-start) | async-done | bytes 1048608 | tf_op jit(solution)/shard_map/all_to_all | solution.py:312
  43.5 1.5 %reshape.35.received = bf16[256,2048]{1,0:T(8,128)(2,1)S(1)} reshape(bf16[128,2,2048]{2,1,0:T(2,128)(2,1)} %all-to-all-done) | data formatting | bytes 2097152 | tf_op jit(solution)/shard_map/reshape | solution.py:314
  45.0 2.8 %copy-done.2 = f32[3,32,32,512]{3,2,1,0:T(8,128)S(1)} copy-done((f32[3,32,32,512]{3,2,1,0:T(8,128)S(1)}, f32[3,32,32,512]{3,2,1,0:T(8,128)}, u32[]{:S(2)}) %copy-start.2) | copy-done | bytes 6291480
  47.8 4.1 %place.1 = (f32[3,1024,640]{2,1,0:T(8,128)S(1)}, bf16[3,2,32,640]{3,2,1,0:T(8,128)(2,1)S(1)}, bf16[3,2,32,640]{3,2,1,0:T(8,128)(2,1)S(1)}) custom-call(f32[3,1024,512]{2,1,0:T(8,128)S(1)} %bitcast.20, f32[3,1024,128]{2,1,0:T(8,128)S(1)} %pad_maximum_fusion.edge, bf16[256,2048]{1,0:T(8,128)(2,1)S(1)} %reshape.35.received), custom_call_target="tpu_custom_call" | custom-call | flops 1000000000 | bytes 17825792 | tf_op jit(solution)/shard_map/place/pallas_call | solution.py:329
  51.9 3.0 %copy-done.3 = f32[3,1024,640]{2,1,0:T(8,128)} copy-done((f32[3,1024,640]{2,1,0:T(8,128)}, f32[3,1024,640]{2,1,0:T(8,128)S(1)}, u32[]{:S(2)}) %copy-start.3) | copy-done | bytes 7864344
  55.0 2.9 %collective-permute-start.2 = (bf16[3,2,32,640]{3,2,1,0:T(8,128)(2,1)S(1)}, bf16[3,2,32,640]{3,2,1,0:T(8,128)(2,1)S(1)}, u32[]{:S(2)}, u32[]{:S(2)}) collective-permute-start(bf16[3,2,32,640]{3,2,1,0:T(8,128)(2,1)S(1)} %get-tuple-element.11), channel_id=1, source_target_pairs={{0,8},{8,16},{16,24},{24,32},{32,40},{40,48},{48,56},{56,64},{64,7... | collective-permute-start | bytes 737288 | tf_op jit(solution)/shard_map/ppermute | solution.py:354
  57.8 1.3 %collective-permute-start.3 = (bf16[3,2,32,640]{3,2,1,0:T(8,128)(2,1)S(1)}, bf16[3,2,32,640]{3,2,1,0:T(8,128)(2,1)S(1)}, u32[]{:S(2)}, u32[]{:S(2)}) collective-permute-start(bf16[3,2,32,640]{3,2,1,0:T(8,128)(2,1)S(1)} %get-tuple-element.12), channel_id=1, source_target_pairs={{8,0},{16,8},{24,16},{32,24},{40,32},{48,40},{56,48},{64,56},{72,6... | collective-permute-start | bytes 737288 | tf_op jit(solution)/shard_map/ppermute | solution.py:355
  59.3 3.2 %collective-permute-done.2.below_x = bf16[3,2,32,640]{3,2,1,0:T(8,128)(2,1)S(1)} collective-permute-done((bf16[3,2,32,640]{3,2,1,0:T(8,128)(2,1)S(1)}, bf16[3,2,32,640]{3,2,1,0:T(8,128)(2,1)S(1)}, u32[]{:S(2)}, u32[]{:S(2)}) %collective-permute-start.2) | collective-permute-done | bytes 245792 | tf_op jit(solution)/shard_map/ppermute | solution.py:354
  62.5 3.8 %collective-permute-done.3.above_x = bf16[3,2,32,640]{3,2,1,0:T(8,128)(2,1)S(1)} collective-permute-done((bf16[3,2,32,640]{3,2,1,0:T(8,128)(2,1)S(1)}, bf16[3,2,32,640]{3,2,1,0:T(8,128)(2,1)S(1)}, u32[]{:S(2)}, u32[]{:S(2)}) %collective-permute-start.3) | collective-permute-done | bytes 245792 | tf_op jit(solution)/shard_map/ppermute | solution.py:355
  66.3 20.6 %sweeps.1 = (f32[3,1024,512]{2,1,0:T(8,128)}, bf16[256,1536]{1,0:T(8,128)(2,1)S(1)}) custom-call(f32[4]{0:T(128)S(1)} %add_convert_fusion.sides, f32[3,32,32,640]{3,2,1,0:T(8,128)} %bitcast.21, bf16[3,2,32,640]{3,2,1,0:T(8,128)(2,1)S(1)} %collective-permute-done.2.below_x, bf16[3,2,32,640]{3,2,1,0:T(8,128)(2,1)S(1)} %collective-permute-done.3.above_x, ...), custom_call_target="tpu_custom_call" | custom-call | flops 2000000000 | bytes 16777216 | tf_op jit(solution)/shard_map/sweeps/pallas_call | solution.py:360
  87.3 28.0 %all_to_all.10 = bf16[128,2,1536]{2,1,0:T(2,128)(2,1)S(1)} all-to-all(bf16[128,2,1536]{2,1,0:T(2,128)(2,1)S(1)} %reshape.38), channel_id=1, replica_groups=mesh['gx'=16,'gy'=8] {'gx','gy'}, dimensions={0} | all-to-all | bytes 1572864 | tf_op jit(solution)/shard_map/all_to_all | solution.py:312
  115.6 3.4 %copy-done.1 = bf16[8,8,128,512]{3,2,1,0:T(8,128)(2,1)S(1)} copy-done((bf16[8,8,128,512]{3,2,1,0:T(8,128)(2,1)S(1)}, bf16[8,8,128,512]{3,2,1,0:T(8,128)(2,1)}, u32[]{:S(2)}) %copy-start.1) | copy-done | bytes 8388632
  119.0 4.4 %interp.1 = f32[3,8,128]{2,1,0:T(8,128)} custom-call(f32[3,8,128]{2,1,0:T(8,128)S(1)} %bitcast.23, f32[64,128]{1,0:T(8,128)S(1)} %get-tuple-element.14.dest, bf16[256,1536]{1,0:T(8,128)(2,1)S(1)} %reshape.39.returned, bf16[8,1024,512]{2,1,0:T(8,128)(2,1)S(1)} %bitcast.18), custom_call_target="tpu_custom_call" | custom-call | flops 1000000000 | bytes 9437184 | tf_op jit(solution)/shard_map/interp/pallas_call | solution.py:379
  (25 shorter events, 4.7 us)
Async XLA Ops:
  0.6 3.4 %copy-start = (bf16[8,8,128,512]{3,2,1,0:T(8,128)(2,1)S(1)}, bf16[8,8,128,512]{3,2,1,0:T(8,128)(2,1)}, u32[]{:S(2)}) copy-start(bf16[8,8,128,512]{3,2,1,0:T(8,128)(2,1)} %param.11) | copy-start | bytes 25165828
  4.0 0.7 copy-start.4
  4.7 0.7 copy-start.6
  5.4 0.7 copy-start.7
  6.1 0.7 copy-start.8
  6.8 0.7 copy-start.9
  12.8 30.8 %all-to-all-start = ((bf16[128,2,2048]{2,1,0:T(2,128)(2,1)}), bf16[128,2,2048]{2,1,0:T(2,128)(2,1)}, u32[]{:S(2)}, u32[]{:S(2)}) async-start(bf16[128,2,2048]{2,1,0:T(2,128)(2,1)} %reshape.34), calls=%async_computation | async-start | bytes 2097152 | tf_op jit(solution)/shard_map/all_to_all | solution.py:312
  30.1 6.2 %collective-permute-start = (f32[3,2,1024]{2,1,0:T(2,128)S(1)}, f32[3,2,1024]{2,1,0:T(2,128)S(1)}, u32[]{:S(2)}, u32[]{:S(2)}) collective-permute-start(f32[3,2,1024]{2,1,0:T(2,128)S(1)} %copy.9), channel_id=1, source_target_pairs={{1,0},{2,1},{3,2},{4,3},{5,4},{6,5},{7,6},{9,8},{10,9},{11,10},{12... | collective-permute-start | bytes 73736 | tf_op jit(solution)/shard_map/ppermute | solution.py:321
  33.7 4.3 %collective-permute-start.1 = (f32[3,2,1024]{2,1,0:T(2,128)S(1)}, f32[3,2,1024]{2,1,0:T(2,128)S(1)}, u32[]{:S(2)}, u32[]{:S(2)}) collective-permute-start(f32[3,2,1024]{2,1,0:T(2,128)S(1)} %copy.11), channel_id=1, source_target_pairs={{0,1},{1,2},{2,3},{3,4},{4,5},{5,6},{6,7},{8,9},{9,10},{10,11},{11... | collective-permute-start | bytes 73736 | tf_op jit(solution)/shard_map/ppermute | solution.py:322
  45.0 2.8 %copy-start.2 = (f32[3,32,32,512]{3,2,1,0:T(8,128)S(1)}, f32[3,32,32,512]{3,2,1,0:T(8,128)}, u32[]{:S(2)}) copy-start(f32[3,32,32,512]{3,2,1,0:T(8,128)} %param.7) | copy-start | bytes 18874372
  51.9 3.1 %copy-start.3 = (f32[3,1024,640]{2,1,0:T(8,128)}, f32[3,1024,640]{2,1,0:T(8,128)S(1)}, u32[]{:S(2)}) copy-start(f32[3,1024,640]{2,1,0:T(8,128)S(1)} %get-tuple-element.10) | copy-start | bytes 23592964
  55.0 7.5 %collective-permute-start.2 = (bf16[3,2,32,640]{3,2,1,0:T(8,128)(2,1)S(1)}, bf16[3,2,32,640]{3,2,1,0:T(8,128)(2,1)S(1)}, u32[]{:S(2)}, u32[]{:S(2)}) collective-permute-start(bf16[3,2,32,640]{3,2,1,0:T(8,128)(2,1)S(1)} %get-tuple-element.11), channel_id=1, source_target_pairs={{0,8},{8,16},{16,24},{24,32},{32,40},{40,48},{48,56},{56,64},{64,7... | collective-permute-start | bytes 737288 | tf_op jit(solution)/shard_map/ppermute | solution.py:354
  57.8 8.5 %collective-permute-start.3 = (bf16[3,2,32,640]{3,2,1,0:T(8,128)(2,1)S(1)}, bf16[3,2,32,640]{3,2,1,0:T(8,128)(2,1)S(1)}, u32[]{:S(2)}, u32[]{:S(2)}) collective-permute-start(bf16[3,2,32,640]{3,2,1,0:T(8,128)(2,1)S(1)} %get-tuple-element.12), channel_id=1, source_target_pairs={{8,0},{16,8},{24,16},{32,24},{40,32},{48,40},{56,48},{64,56},{72,6... | collective-permute-start | bytes 737288 | tf_op jit(solution)/shard_map/ppermute | solution.py:355
  87.2 28.3 %copy-start.5 = (f32[8,3,128]{2,0,1:T(8,128)S(1)}, f32[8,3,128]{2,0,1:T(8,128)}, u32[]{:S(2)}) copy-start(f32[8,3,128]{2,0,1:T(8,128)} %param.8) | copy-start | bytes 36868
  115.6 3.4 %copy-start.1 = (bf16[8,8,128,512]{3,2,1,0:T(8,128)(2,1)S(1)}, bf16[8,8,128,512]{3,2,1,0:T(8,128)(2,1)}, u32[]{:S(2)}) copy-start(bf16[8,8,128,512]{3,2,1,0:T(8,128)(2,1)} %param.11) | copy-start | bytes 25165828

commit v2 on v0

v2 whole, which is shorter than its diff:
```python
import functools

import jax
import jax.numpy as jnp
from jax import lax
from jax.experimental import pallas as pl
from jax.experimental.pallas import tpu as pltpu
from jax.sharding import PartitionSpec as P

viscosity = 0.1
transport_rate = 0.1
force_step = 0.5
fiber_step = 0.25

F32 = jnp.float32
BF16 = jnp.bfloat16
LANES = 128
BELOW, ABOVE = 2, 10


def dot(a, b):
    return jnp.dot(a, b, preferred_element_type=F32)


def iota(shape, axis):
    return lax.broadcasted_iota(jnp.int32, shape, axis)


def spread_kernel(
    gy_size, slots, pts_hbm, stiff, links_hbm, owners_hbm, patch_slots_hbm, dw_hbm, out, dest_out, dw,
    force, rows, pts, links, owners, patch_slots, sems,
):
    blocks, points = links.shape
    inter = owners.shape[1]
    entries = blocks * inter
    loads = [
        pltpu.make_async_copy(dw_hbm.at[b], dw.at[b], sems.at[b]) for b in range(blocks)
    ]
    small = [(pts_hbm, pts), (links_hbm, links), (owners_hbm, owners), (patch_slots_hbm, patch_slots)]
    small = [pltpu.make_async_copy(a, b, sems.at[blocks + i]) for i, (a, b) in enumerate(small)]
    for copy in small + loads:
        copy.start()
    for copy in small:
        copy.wait()
    partner = lax.rem(iota((blocks, points), 1) + links[...], points)
    for c in range(3):
        own = pts[c]
        force[c] = jnp.take_along_axis(own, partner, axis=1) - own
    group = iota((inter, inter * points), 0)
    column = iota((inter, inter * points), 1) // points

    @pl.loop(0, blocks)
    def _(b):
        stiffness = stiff[b]
        parts = []
        for c in range(3):
            row = (stiffness * force[c, pl.ds(b, 1), :]).astype(BF16).astype(F32)
            wide = jnp.concatenate([jnp.broadcast_to(row, (inter, points))] * inter, axis=1)
            parts.append(jnp.where(group == column, wide, 0.0))
        parts.append(jnp.zeros_like(parts[0]))
        pltpu.make_async_copy(dw_hbm.at[b], dw.at[b], sems.at[b]).wait()
        spread = dot(jnp.concatenate(parts, axis=0).astype(BF16), dw[b])
        for c in range(3):
            rows[c, pl.ds(pl.multiple_of(b * inter, inter), inter), :] = spread[c * inter : (c + 1) * inter]

    pick_block = (iota((entries, blocks), 0) // inter == iota((entries, blocks), 1)).astype(BF16)
    pick_k = lax.rem(iota((entries, inter), 0), inter) == iota((entries, inter), 1)

    def as_column(table):
        spread_rows = dot(pick_block, table.astype(F32).astype(BF16))
        return jnp.sum(jnp.where(pick_k, spread_rows, 0.0), axis=1, keepdims=True)

    owner = as_column(owners[...])
    code = patch_slots[...] + 1
    high, low = as_column(code // 32), as_column(lax.rem(code, 32))
    owner_wide = jnp.broadcast_to(owner, (entries, LANES))
    owner_row = jnp.transpose(
        jnp.concatenate([owner_wide, jnp.zeros((LANES - entries, LANES), F32)], axis=0)
    )[:entries, :entries]
    same = (owner_wide[:, :entries] == owner_row) & (iota((entries, entries), 1) < iota((entries, entries), 0))
    rank = jnp.sum(jnp.where(same, 1.0, 0.0), axis=1, keepdims=True)
    dest = owner * 2.0 + rank
    dest_wide = jnp.broadcast_to(dest, (entries, LANES))
    dest_out[...] = dest_wide
    padded = jnp.concatenate([dest_wide, jnp.full((LANES - entries, LANES), -8.0, F32)], axis=0)
    dest_row = jnp.transpose(padded)[0:1, :entries].astype(jnp.int32)
    position = lax.rem(dest_row // 2, gy_size)
    slot = iota((slots, entries), 0)
    here = (slot == dest_row).astype(F32).astype(BF16)
    to_above = ((slot == dest_row + 2) & (position < gy_size - 1)).astype(F32).astype(BF16)
    to_below = ((slot == dest_row - 2) & (position > 0)).astype(F32).astype(BF16)
    lane = iota((entries, LANES), 1)

    def digits(at):
        return jnp.where(lane == at, high, 0.0) + jnp.where(lane == at + 1, low, 0.0)

    own_head, above_head, below_head = digits(0), digits(BELOW), digits(ABOVE)
    patch = rows.shape[2]
    for c in range(3):
        tail = pltpu.roll(rows[c, :, patch - LANES :], BELOW + 4 + 2 * c, axis=1)
        at = BELOW + 2 + 2 * c
        above_head += jnp.where((lane == at) | (lane == at + 1), tail, 0.0)
        at = ABOVE + 2 + 2 * c
        start = pltpu.roll(rows[c, :, :LANES], at, axis=1)
        below_head += jnp.where((lane == at) | (lane == at + 1), start, 0.0)
        out[:, c * patch : (c + 1) * patch] = dot(here, rows[c].astype(BF16)).astype(BF16)
    head = dot(here, own_head.astype(BF16))
    head += dot(to_above, above_head.astype(BF16))
    head += dot(to_below, below_head.astype(BF16))
    out[:, 3 * patch :] = head.astype(BF16)


def stage_kernel(velocity, edge, out, sems):
    patch = velocity.shape[2]
    main = pltpu.make_async_copy(velocity, out.at[:, :, :patch], sems.at[0])
    side = pltpu.make_async_copy(edge, out.at[:, :, patch:], sems.at[1])
    main.start()
    side.start()
    main.wait()
    side.wait()


def place_kernel(layer_rows, staged, received, out, low_rows, high_rows, low_f, high_f):
    cells, wide = staged.shape[1:]
    patch = wide - LANES
    slots = received.shape[0]
    part = 256
    layers = part // layer_rows
    head = received[:, 3 * patch :].astype(F32)
    head_t = jnp.transpose(head)
    lane = iota((slots, LANES), 1)
    tails, starts = [], []
    for c in range(3):
        tail = pltpu.roll(head, LANES - 4 - BELOW - 2 * c, axis=1)
        tails.append(jnp.where(lane >= LANES - 2, tail, 0.0).astype(BF16))
        start = pltpu.roll(head, LANES - (ABOVE + 2 + 2 * c), axis=1)
        starts.append(jnp.where(lane < 2, start, 0.0).astype(BF16))

    def slot_at(at):
        return (head_t[at : at + 1] * 32.0 + head_t[at + 1 : at + 2] - 1.0).astype(jnp.int32)

    slot_here, slot_below, slot_above = slot_at(0), slot_at(BELOW), slot_at(ABOVE)

    @pl.loop(0, cells // part)
    def _(step):
        row = iota((part, slots), 0) + step * part
        here = (row == slot_here).astype(F32).astype(BF16)
        below = (row == slot_below).astype(F32).astype(BF16)
        above = (row == slot_above).astype(F32).astype(BF16)
        at = pl.ds(pl.multiple_of(step * part, part), part)
        for c in range(3):
            main = staged[c, at, :patch] + force_step * dot(here, received[:, c * patch : (c + 1) * patch])
            edge = staged[c, at, patch:] + force_step * (dot(below, tails[c]) + dot(above, starts[c]))
            out[c, at, :patch] = main
            out[c, at, patch:] = edge
            to = pl.ds(pl.multiple_of(step * layers, layers), layers)
            for j in range(2):
                for side, offset in ((low_f, j), (high_f, layer_rows - 2 + j)):
                    picks = range(offset, part, layer_rows)
                    side[c, j, to, :patch] = jnp.concatenate([main[i : i + 1] for i in picks], axis=0)
                    side[c, j, to, patch:] = jnp.concatenate([edge[i : i + 1] for i in picks], axis=0)

    low_rows[...] = low_f[...].astype(BF16)
    high_rows[...] = high_f[...].astype(BF16)


def update(centre, weights, c, east, west, north, south, up, down):
    (px, mx), (py, my), (pz, mz) = weights
    keep = 1.0 - 6.0 * viscosity
    return keep * centre[c] + px * east + mx * west + py * north + my * south + pz * up + mz * down


def mix(centre):
    return [(viscosity - transport_rate * v, viscosity + transport_rate * v) for v in centre]


def edge_mask(sides):
    lane = iota((8, LANES), 1)
    return jnp.where(lane == 0, sides[3], 0.0) + jnp.where(lane == LANES - 1, sides[2], 0.0)


def sweep(source, low_row, high_row, store, keep):
    layers, rows, wide = source.shape[1:]
    sub = iota((8, keep), 0)

    @pl.loop(0, layers)
    def _(z):
        z_up = jnp.where(z == layers - 1, 0, z + 1)
        z_down = jnp.where(z == 0, layers - 1, z - 1)
        for x in range(0, rows, 8):
            centre = [source[c, z, x : x + 8, :] for c in range(3)]
            weights = mix([v[:, :keep] for v in centre])
            for c in range(3):
                v = centre[c]
                if x + 8 < rows:
                    east = source[c, z, x + 1 : x + 9, :keep]
                else:
                    east = jnp.where(sub == 7, high_row(c, z), pltpu.roll(v[:, :keep], 7, axis=0))
                if x > 0:
                    west = source[c, z, x - 1 : x + 7, :keep]
                else:
                    west = jnp.where(sub == 0, low_row(c, z), pltpu.roll(v[:, :keep], 1, axis=0))
                new = update(
                    [w[:, :keep] for w in centre], weights, c, east, west,
                    pltpu.roll(v, wide - 1, axis=1)[:, :keep], pltpu.roll(v, 1, axis=1)[:, :keep],
                    source[c, z_up, x : x + 8, :keep], source[c, z_down, x : x + 8, :keep],
                )
                store(c, z, x, new)


def first_kernel(sides, u0, u1):
    patch = u0.shape[3] - LANES
    mask = edge_mask(sides)

    def store(c, z, x, new):
        u1[c, z, x : x + 8, :patch] = new[:, :patch]
        u1[c, z, x : x + 8, patch:] = new[:, patch:] * mask

    sweep(u0, lambda c, z: 0.0, lambda c, z: 0.0, store, u0.shape[3])


def last_kernel(sides, u1_in, low_f, high_f, below_x, above_x, received, fluid_hbm, replies, u1, mid, fluid, sems):
    layers, rows, wide = u1.shape[1:]
    patch = wide - LANES
    slots = received.shape[0]
    mask = edge_mask(sides)[0:1]

    for side in range(2):
        halo, inner, row = (below_x, low_f, 0) if side == 0 else (above_x, high_f, rows - 1)
        near = 1 - side
        centre = [halo[c, near].astype(F32) for c in range(3)]
        weights = mix(centre)
        slope = transport_rate if side == 0 else -transport_rate
        own = viscosity + slope * inner[0, side]
        for c in range(3):
            outer = halo[c, side].astype(F32)
            inside = inner[c, side]
            east, west = (inside, outer) if side == 0 else (outer, inside)
            v = centre[c]
            new = update(
                centre, weights, c, east, west,
                pltpu.roll(v, wide - 1, axis=1), pltpu.roll(v, 1, axis=1),
                pltpu.roll(v, layers - 1, axis=0), pltpu.roll(v, 1, axis=0),
            ) * sides[side]
            mid[side, c, :, :patch] = new[:, :patch]
            mid[side, c, :, patch:] = new[:, patch:] * mask
            term = own * v
            tail = term[:, patch:] * mask
            for z in range(layers):
                u1[c, z, row : row + 1, :patch] += term[z : z + 1, :patch]
                u1[c, z, row : row + 1, patch:] += tail[z : z + 1]

    def store(c, z, x, new):
        fluid[c, pl.ds(pl.multiple_of(z * rows + x, 8), 8), :] = new

    sweep(
        u1,
        lambda c, z: mid[0, c, pl.ds(z, 1), :patch],
        lambda c, z: mid[1, c, pl.ds(z, 1), :patch],
        store,
        patch,
    )
    write = pltpu.make_async_copy(fluid, fluid_hbm, sems.at[0])
    write.start()

    heads = received[:, 3 * patch :].astype(F32)
    slot = (heads[:, 0:1] * 32.0 + heads[:, 1:2] - 1.0).astype(jnp.int32)
    chunk = 256
    for c in range(3):
        total = jnp.zeros((slots, patch), F32)
        for first in range(0, layers * rows, chunk):
            pick = (iota((slots, chunk), 1) + first == slot).astype(F32).astype(BF16)
            total += dot(pick, fluid[c, first : first + chunk, :].astype(BF16))
        replies[:, c * patch : (c + 1) * patch] = total.astype(BF16)
    write.wait()


def gather_kernel(pts, dest, returned, dw, out, picked, moved):
    entries, slots = dest.shape[0], returned.shape[0]
    blocks, patch, points = dw.shape[0], dw.shape[2], pts.shape[2]
    inter = entries // blocks
    to = dest[:, 0:1].astype(jnp.int32)
    pick = (iota((entries, slots), 1) == to).astype(F32).astype(BF16)
    for c in range(3):
        picked[c] = dot(pick, returned[:, c * patch : (c + 1) * patch])
    group = iota((inter, inter * points), 0)
    column = iota((inter, inter * points), 1) // points

    @pl.loop(0, blocks)
    def _(b):
        at = pl.ds(pl.multiple_of(b * inter, inter), inter)
        parts = [picked[c, at, :] for c in range(3)]
        parts.append(jnp.zeros_like(parts[0]))
        every = lax.dot_general(
            jnp.concatenate(parts, axis=0).astype(BF16), dw[b], (((1,), (1,)), ((), ())), preferred_element_type=F32
        )
        for c in range(3):
            own = jnp.where(group == column, every[c * inter : (c + 1) * inter], 0.0)
            folded = own[:, :points]
            for k in range(1, inter):
                folded = folded + own[:, k * points : (k + 1) * points]
            moved[c, pl.ds(b, 1), :] = jnp.sum(folded, axis=0, keepdims=True)

    for c in range(3):
        out[c] = pts[c] + fiber_step * moved[c]


def shards(velocity, fiber_points, stiffness, links, delta_weights, owners, patch_slots):
    blocks, inter, points, patch = delta_weights.shape
    layers, rows, columns = velocity.shape[1:]
    gx_size, gy_size = lax.axis_size("gx"), lax.axis_size("gy")
    devices = gx_size * gy_size
    entries, slots, cells = blocks * inter, devices * 2, layers * rows
    wide, width = patch + LANES, 3 * patch + LANES
    mb = 1 << 20
    pts = fiber_points.transpose(1, 0, 2)
    dw = delta_weights.reshape(blocks, inter * points, patch)
    smem = pl.BlockSpec(memory_space=pltpu.SMEM)
    vmem = pl.BlockSpec(memory_space=pltpu.VMEM)
    hbm = pl.BlockSpec(memory_space=pltpu.HBM)
    anywhere = pl.BlockSpec(memory_space=pl.ANY)

    def params(limit):
        return pltpu.CompilerParams(vmem_limit_bytes=limit * mb)

    def cost(flops, size):
        return pl.CostEstimate(flops=flops, bytes_accessed=size * mb, transcendentals=0)

    outgoing, dest, dw_near = pl.pallas_call(
        functools.partial(spread_kernel, gy_size, slots),
        in_specs=[hbm, smem, hbm, hbm, hbm, hbm],
        out_specs=[vmem, vmem, vmem],
        out_shape=[
            jax.ShapeDtypeStruct((slots, width), BF16),
            jax.ShapeDtypeStruct((entries, LANES), F32),
            jax.ShapeDtypeStruct(dw.shape, BF16),
        ],
        scratch_shapes=[
            pltpu.VMEM((3, blocks, points), F32),
            pltpu.VMEM((3, entries, patch), F32),
            pltpu.VMEM((3, blocks, points), F32),
            pltpu.VMEM((blocks, points), jnp.int32),
            pltpu.VMEM((blocks, inter), jnp.int32),
            pltpu.VMEM((blocks, inter), jnp.int32),
            pltpu.SemaphoreType.DMA((blocks + 4,)),
        ],
        compiler_params=params(16),
        cost_estimate=cost(10**9, 9),
        name="spread",
    )(pts, stiffness, links, owners.reshape(blocks, inter), patch_slots, dw)

    def exchange(rows_out):
        size = rows_out.shape[1]
        return lax.all_to_all(
            rows_out.reshape(devices, 2, size), ("gx", "gy"), split_axis=0, concat_axis=0, tiled=True
        ).reshape(slots, size)

    received = exchange(outgoing)

    ahead = [(i + 1, i) for i in range(gy_size - 1)]
    behind = [(i, i + 1) for i in range(gy_size - 1)]
    flat = velocity.reshape(3, cells, columns)
    first = lax.ppermute(flat[:, :, :2].transpose(0, 2, 1), "gy", ahead)
    last = lax.ppermute(flat[:, :, columns - 2 :].transpose(0, 2, 1), "gy", behind)
    edge = jnp.concatenate(
        [first.transpose(0, 2, 1), jnp.zeros((3, cells, LANES - 4), F32), last.transpose(0, 2, 1)], axis=2
    )
    staged = pl.pallas_call(
        stage_kernel,
        in_specs=[hbm, anywhere],
        out_specs=vmem,
        out_shape=jax.ShapeDtypeStruct((3, cells, wide), F32),
        scratch_shapes=[pltpu.SemaphoreType.DMA((2,))],
        compiler_params=params(16),
        cost_estimate=cost(0, 8),
        name="stage",
    )(flat, edge)

    side = (3, 2, layers, wide)
    u0, low_rows, high_rows, low_f, high_f = pl.pallas_call(
        functools.partial(place_kernel, rows),
        in_specs=[vmem, vmem],
        out_specs=[vmem] * 5,
        out_shape=[
            jax.ShapeDtypeStruct((3, cells, wide), F32),
            jax.ShapeDtypeStruct(side, BF16),
            jax.ShapeDtypeStruct(side, BF16),
            jax.ShapeDtypeStruct(side, F32),
            jax.ShapeDtypeStruct(side, F32),
        ],
        input_output_aliases={0: 0},
        compiler_params=params(24),
        cost_estimate=cost(10**9, 10),
        name="place",
    )(staged, received)

    up = [(i, i + 1) for i in range(gx_size - 1)]
    below_x = lax.ppermute(high_rows, "gx", up)
    above_x = lax.ppermute(low_rows, "gx", [(b, a) for a, b in up])

    gx, gy = lax.axis_index("gx"), lax.axis_index("gy")
    sides = jnp.stack([gx > 0, gx < gx_size - 1, gy > 0, gy < gy_size - 1]).astype(F32)
    u1 = pl.pallas_call(
        first_kernel,
        in_specs=[smem, vmem],
        out_specs=vmem,
        out_shape=jax.ShapeDtypeStruct((3, layers, rows, wide), F32),
        compiler_params=params(24),
        cost_estimate=cost(2 * 10**9, 16),
        name="sweep_first",
    )(sides, u0.reshape(3, layers, rows, wide))
    fluid, replies, _ = pl.pallas_call(
        last_kernel,
        in_specs=[smem] + [vmem] * 6,
        out_specs=[hbm, vmem, vmem],
        out_shape=[
            jax.ShapeDtypeStruct((3, cells, patch), F32),
            jax.ShapeDtypeStruct((slots, 3 * patch), BF16),
            jax.ShapeDtypeStruct((3, layers, rows, wide), F32),
        ],
        scratch_shapes=[
            pltpu.VMEM((2, 3, layers, wide), F32),
            pltpu.VMEM((3, cells, patch), F32),
            pltpu.SemaphoreType.DMA((1,)),
        ],
        input_output_aliases={1: 2},
        compiler_params=params(24),
        cost_estimate=cost(2 * 10**9, 16),
        name="sweep_last",
    )(sides, u1, low_f, high_f, below_x, above_x, received)

    returned = exchange(replies)
    moved = pl.pallas_call(
        gather_kernel,
        in_specs=[vmem] * 4,
        out_specs=vmem,
        out_shape=jax.ShapeDtypeStruct((3, blocks, points), F32),
        scratch_shapes=[pltpu.VMEM((3, entries, patch), F32), pltpu.VMEM((3, blocks, points), F32)],
        compiler_params=params(16),
        cost_estimate=cost(10**9, 9),
        name="interp",
    )(pts, dest, returned, dw_near)
    return fluid.reshape(3, layers, rows, columns), moved.transpose(1, 0, 2)


def solution(mesh):
    placed = (
        P(None, None, "gx", "gy"),
        P(("gx", "gy"), None, None),
        P(("gx", "gy")),
        P(("gx", "gy"), None),
        P(("gx", "gy"), None, None, None),
        P(("gx", "gy"), None, None),
        P(("gx", "gy"), None),
    )
    return jax.shard_map(
        shards,
        mesh=mesh,
        in_specs=placed,
        out_specs=(P(None, None, "gx", "gy"), P(("gx", "gy"), None, None)),
        check_vma=False,
    )
```

time: 237 us -> 115 us (0.49)
  other arithmetic: 50.3 us -> 0.56 us
  local copies, waits for them, and re-layouts: 73.4 us -> 31.1 us
  Pallas kernels: 0 us -> 31.4 us
  waiting for transfers between devices: 27.3 us -> 0.79 us
  starting transfers between devices: 39.9 us -> 22.1 us
  matrix products: 17.4 us -> 0 us
    pallas_call x0 -> x6, Pallas kernels: none -> 31.4 us  [the longest x1 10.7 us: shards(): pl.pallas_call(last_kernel, in_specs=[smem] + [vmem] * 6, out_specs=[hbm,...]
    slice x12 -> x0, local copies, waits for them, and re-layouts: 27.3 us -> none  [the longest x4 14.1 us: advance(): above_cells = jnp.roll(middle, -1, axis=1)]
    all_to_all x2 -> x1, waiting for transfers between devices: 23.7 us -> 0.01 us  [exchange(): lax.all_to_all(rows_out.reshape(devices, 2, size), ('gx', 'gy'), split_ax...]
    convert_element_type x1, other arithmetic: 20.8 us -> 0.08 us  [shards(): jnp.stack([gx > 0, gx < gx_size - 1, gy > 0, gy < gy_size - 1]).astype(F32)]
    unnamed x16 -> x24, local copies, waits for them, and re-layouts: 1.88 us -> 22.5 us
    sub x1 -> x0, other arithmetic: 20.1 us -> none  [advance(): return middle + viscosity * laplace - transport_rate * transport]
    gather x3 -> x0, local copies, waits for them, and re-layouts: 18.5 us -> none  [shards(): partner_points = jnp.take_along_axis(fiber_points, partner_full, axis=2)]
    dot_general x6 -> x0, matrix products: 17.4 us -> none  [the longest x1 5.66 us: shards(): jnp.einsum('bkcq,bkpq->bcp', picked, delta_weights, preferred_element_typ...]
  transfers between devices with their start and end apart: 10 -> 5, of which waited for: 3 -> 2; matrix products, arithmetic and copies ran while one was open for 18% -> 4% of each run, Pallas kernels for 0% -> 8%
where the time goes in v2:
time: 115 us
  Pallas kernels  31.4 us (27%)
  local copies, waits for them, and re-layouts  31.1 us (27%)
  blocking collectives  28 us (24%)
  starting transfers between devices  22.1 us (19%)
    all_to_all x1, blocking collectives, exchange(): lax.all_to_all(rows_out.reshape(devices, 2, size), ('gx', 'gy'), split_ax...  28 us
    unnamed x24, local copies, waits for them, and re-layouts  22.5 us
    all_to_all x1, starting transfers between devices, exchange(): lax.all_to_all(rows_out.reshape(devices, 2, size), ('gx', 'gy'), split_ax...  11.9 us
    pallas_call x1, Pallas kernels, shards(): pl.pallas_call(last_kernel, in_specs=[smem] + [vmem] * 6, out_specs=[hbm,...  10.7 us
    pallas_call x1, Pallas kernels, shards(): pl.pallas_call(first_kernel, in_specs=[smem, vmem], out_specs=vmem, out_s...  7.74 us
    pallas_call x1, Pallas kernels, shards(): pl.pallas_call(functools.partial(spread_kernel, gy_size, slots), in_specs...  4.49 us
    pallas_call x1, Pallas kernels, shards(): pl.pallas_call(gather_kernel, in_specs=[vmem] * 4, out_specs=vmem, out_sh...  4.31 us
    ppermute x1, starting transfers between devices, shards(): below_x = lax.ppermute(high_rows, 'gx', up)  3.29 us
  transfers between devices with their start and end apart: 5, of which 2 were waited for; matrix products, arithmetic and copies ran while one was open for 4% of the time, Pallas kernels for 8%

profile of v2, /device:TPU:1, one launch (start us, length us, event | category | flops | bytes accessed | tf_op | source)
XLA Modules:
  0.0 114.7 jit_solution(15212420599090538448)
XLA Ops:
  0.6 3.4 %copy-done.3 = bf16[8,8,128,512]{3,2,1,0:T(8,128)(2,1)S(1)} copy-done((bf16[8,8,128,512]{3,2,1,0:T(8,128)(2,1)S(1)}, bf16[8,8,128,512]{3,2,1,0:T(8,128)(2,1)}, u32[]{:S(2)}) %copy-start.3) | copy-done | bytes 8388632
  4.0 0.7 copy-done.6
  4.7 0.7 copy-done.8
  5.4 0.7 copy-done.9
  7.4 4.5 %spread.1 = (bf16[256,1664]{1,0:T(8,128)(2,1)S(1)}, f32[64,128]{1,0:T(8,128)S(1)}, bf16[8,1024,512]{2,1,0:T(8,128)(2,1)S(1)}) custom-call(f32[3,8,128]{2,1,0:T(8,128)S(1)} %bitcast.21, f32[8]{0:T(128)S(1)} %copy-done.11, s32[8,128]{1,0:T(8,128)S(1)} %copy-done.8, s32[8,8]{1,0:T(8,128)S(1)} %bitcast.23, s32[8,8]{1,0:T(8,128)S(1)} %copy-done.10, ...), custom_call_target="tpu_custom_call" | custom-call | flops 1000000000 | bytes 9437184 | tf_op jit(solution)/shard_map/spread/pallas_call | solution.py:329
  11.9 3.2 %copy-done.4 = bf16[8,1024,512]{2,1,0:T(8,128)(2,1)} copy-done((bf16[8,1024,512]{2,1,0:T(8,128)(2,1)}, bf16[8,1024,512]{2,1,0:T(8,128)(2,1)S(1)}, u32[]{:S(2)}) %copy-start.4) | copy-done | bytes 8388632
  15.2 1.2 %reshape.34 = bf16[128,2,1664]{2,1,0:T(2,128)(2,1)} reshape(bf16[256,1664]{1,0:T(8,128)(2,1)S(1)} %get-tuple-element.12) | data formatting | bytes 1703936 | tf_op jit(solution)/shard_map/reshape | solution.py:355
  16.4 11.9 %all-to-all-start = ((bf16[128,2,1664]{2,1,0:T(2,128)(2,1)}), bf16[128,2,1664]{2,1,0:T(2,128)(2,1)}, u32[]{:S(2)}, u32[]{:S(2)}) async-start(bf16[128,2,1664]{2,1,0:T(2,128)(2,1)} %reshape.34), calls=%async_computation | async-start | bytes 1703936 | tf_op jit(solution)/shard_map/all_to_all | solution.py:354
  28.3 2.4 %slice_bitcast_fusion.1 = (f32[3,2,1024]{1,2,0:T(8,128)S(1)}, f32[3,2,1024]{1,2,0:T(8,128)S(1)}) fusion(f32[3,1024,512]{2,1,0:T(8,128)} %bitcast.18), kind=kLoop, calls=%fused_computation.1 | loop fusion | bytes 98304 | tf_op jit(solution)/shard_map/transpose | solution.py:363
  31.2 3.0 %collective-permute-start = (f32[3,2,1024]{2,1,0:T(2,128)S(1)}, f32[3,2,1024]{2,1,0:T(2,128)S(1)}, u32[]{:S(2)}, u32[]{:S(2)}) collective-permute-start(f32[3,2,1024]{2,1,0:T(2,128)S(1)} %copy.11), channel_id=1, source_target_pairs={{1,0},{2,1},{3,2},{4,3},{5,4},{6,5},{7,6},{9,8},{10,9},{11,10},{12... | collective-permute-start | bytes 73736 | tf_op jit(solution)/shard_map/ppermute | solution.py:363
  34.7 2.5 %collective-permute-start.1 = (f32[3,2,1024]{2,1,0:T(2,128)S(1)}, f32[3,2,1024]{2,1,0:T(2,128)S(1)}, u32[]{:S(2)}, u32[]{:S(2)}) collective-permute-start(f32[3,2,1024]{2,1,0:T(2,128)S(1)} %copy.13), channel_id=1, source_target_pairs={{0,1},{1,2},{2,3},{3,4},{4,5},{5,6},{6,7},{8,9},{9,10},{10,11},{11... | collective-permute-start | bytes 73736 | tf_op jit(solution)/shard_map/ppermute | solution.py:364
  39.6 2.8 %copy-done.2 = f32[3,32,32,512]{3,2,1,0:T(8,128)S(1)} copy-done((f32[3,32,32,512]{3,2,1,0:T(8,128)S(1)}, f32[3,32,32,512]{3,2,1,0:T(8,128)}, u32[]{:S(2)}) %copy-start.2) | copy-done | bytes 6291480
  42.3 0.9 stage.1.staged
  43.3 3.1 %copy-done = f32[3,1024,640]{2,1,0:T(8,128)} copy-done((f32[3,1024,640]{2,1,0:T(8,128)}, f32[3,1024,640]{2,1,0:T(8,128)S(1)}, u32[]{:S(2)}) %copy-start) | copy-done | bytes 7864344
  46.4 2.4 %reshape.35.received = bf16[256,1664]{1,0:T(8,128)(2,1)S(1)} reshape(bf16[128,2,1664]{2,1,0:T(2,128)(2,1)} %all-to-all-done) | data formatting | bytes 1703936 | tf_op jit(solution)/shard_map/reshape | solution.py:356
  48.7 3.2 %copy-done.1 = f32[3,1024,640]{2,1,0:T(8,128)S(1)} copy-done((f32[3,1024,640]{2,1,0:T(8,128)S(1)}, f32[3,1024,640]{2,1,0:T(8,128)}, u32[]{:S(2)}) %copy-start.1) | copy-done | bytes 7864344
  52.0 3.2 %place.1 = (f32[3,1024,640]{2,1,0:T(8,128)S(1)}, bf16[3,2,32,640]{3,2,1,0:T(8,128)(2,1)S(1)}, bf16[3,2,32,640]{3,2,1,0:T(8,128)(2,1)S(1)}, f32[3,2,32,640]{3,2,1,0:T(8,128)S(1)}, f32[3,2,32,640]{3,2,1,0:T(8,128)S(1)}) custom-call(f32[3,1024,640]{2,1,0:T(8,128)S(1)} %copy-done.1, bf16[256,1664]{1,0:T(8,128)(2,1)S(1)} %reshape.35.received), custom_call_target="tpu_custom_call", output_to_operand_aliasing={{0}: (0, {})} | custom-call | flops 1000000000 | bytes 10485760 | tf_op jit(solution)/shard_map/place/pallas_call | solution.py:380
  55.2 3.3 %collective-permute-start.2 = (bf16[3,2,32,640]{3,2,1,0:T(8,128)(2,1)S(1)}, bf16[3,2,32,640]{3,2,1,0:T(8,128)(2,1)S(1)}, u32[]{:S(2)}, u32[]{:S(2)}) collective-permute-start(bf16[3,2,32,640]{3,2,1,0:T(8,128)(2,1)S(1)} %get-tuple-element.16), channel_id=1, source_target_pairs={{0,8},{8,16},{16,24},{24,32},{32,40},{40,48},{48,56},{56,64},{64,7... | collective-permute-start | bytes 737288 | tf_op jit(solution)/shard_map/ppermute | solution.py:398
  58.5 1.3 %collective-permute-start.3 = (bf16[3,2,32,640]{3,2,1,0:T(8,128)(2,1)S(1)}, bf16[3,2,32,640]{3,2,1,0:T(8,128)(2,1)S(1)}, u32[]{:S(2)}, u32[]{:S(2)}) collective-permute-start(bf16[3,2,32,640]{3,2,1,0:T(8,128)(2,1)S(1)} %get-tuple-element.17), channel_id=1, source_target_pairs={{8,0},{16,8},{24,16},{32,24},{40,32},{48,40},{56,48},{64,56},{72,6... | collective-permute-start | bytes 737288 | tf_op jit(solution)/shard_map/ppermute | solution.py:399
  59.9 7.7 %sweep_first.1.u1_in = f32[3,32,32,640]{3,2,1,0:T(8,128)S(1)} custom-call(f32[4]{0:T(128)S(1)} %add_convert_fusion.sides, f32[3,32,32,640]{3,2,1,0:T(8,128)S(1)} %bitcast.17), custom_call_target="tpu_custom_call" | custom-call | flops 2000000000 | bytes 16777216 | tf_op jit(solution)/shard_map/sweep_first/pallas_call | solution.py:403
  67.7 10.7 %sweep_last.1 = (f32[3,1024,512]{2,1,0:T(8,128)}, bf16[256,1536]{1,0:T(8,128)(2,1)S(1)}, f32[3,32,32,640]{3,2,1,0:T(8,128)S(1)}) custom-call(f32[4]{0:T(128)S(1)} %add_convert_fusion.sides, f32[3,32,32,640]{3,2,1,0:T(8,128)S(1)} %sweep_first.1.u1_in, f32[3,2,32,640]{3,2,1,0:T(8,128)S(1)} %get-tuple-element.14.low_f, ...), custom_call_target="tpu_custom_call", output_to_operand_aliasing={{2}: (1, {})} | custom-call | flops 2000000000 | bytes 16777216 | tf_op jit(solution)/shard_map/sweep_last/pallas_call | solution.py:412
  78.7 28.0 %all_to_all.10 = bf16[128,2,1536]{2,1,0:T(2,128)(2,1)S(1)} all-to-all(bf16[128,2,1536]{2,1,0:T(2,128)(2,1)S(1)} %reshape.38), channel_id=1, replica_groups=mesh['gx'=16,'gy'=8] {'gx','gy'}, dimensions={0} | all-to-all | bytes 1572864 | tf_op jit(solution)/shard_map/all_to_all | solution.py:354
  107.0 3.4 %copy-done.5 = bf16[8,1024,512]{2,1,0:T(8,128)(2,1)S(1)} copy-done((bf16[8,1024,512]{2,1,0:T(8,128)(2,1)S(1)}, bf16[8,1024,512]{2,1,0:T(8,128)(2,1)}, u32[]{:S(2)}) %copy-start.5) | copy-done | bytes 8388632
  110.4 4.3 %interp.1 = f32[3,8,128]{2,1,0:T(8,128)} custom-call(f32[3,8,128]{2,1,0:T(8,128)S(1)} %bitcast.22, f32[64,128]{1,0:T(8,128)S(1)} %get-tuple-element.19.dest, bf16[256,1536]{1,0:T(8,128)(2,1)S(1)} %reshape.39.returned, bf16[8,1024,512]{2,1,0:T(8,128)(2,1)S(1)} %copy-done.5), custom_call_target="tpu_custom_call" | custom-call | flops 1000000000 | bytes 9437184 | tf_op jit(solution)/shard_map/interp/pallas_call | solution.py:433
  (30 shorter events, 5.3 us)
Async XLA Ops:
  0.6 3.4 %copy-start.3 = (bf16[8,8,128,512]{3,2,1,0:T(8,128)(2,1)S(1)}, bf16[8,8,128,512]{3,2,1,0:T(8,128)(2,1)}, u32[]{:S(2)}) copy-start(bf16[8,8,128,512]{3,2,1,0:T(8,128)(2,1)} %param.11) | copy-start | bytes 25165828
  4.0 0.7 copy-start.6
  4.7 0.7 copy-start.8
  5.4 0.7 copy-start.9
  6.1 0.7 copy-start.10
  6.8 0.7 copy-start.11
  11.9 3.2 %copy-start.4 = (bf16[8,1024,512]{2,1,0:T(8,128)(2,1)}, bf16[8,1024,512]{2,1,0:T(8,128)(2,1)S(1)}, u32[]{:S(2)}) copy-start(bf16[8,1024,512]{2,1,0:T(8,128)(2,1)S(1)} %get-tuple-element.21.dw) | copy-start | bytes 25165828
  16.4 29.9 %all-to-all-start = ((bf16[128,2,1664]{2,1,0:T(2,128)(2,1)}), bf16[128,2,1664]{2,1,0:T(2,128)(2,1)}, u32[]{:S(2)}, u32[]{:S(2)}) async-start(bf16[128,2,1664]{2,1,0:T(2,128)(2,1)} %reshape.34), calls=%async_computation | async-start | bytes 1703936 | tf_op jit(solution)/shard_map/all_to_all | solution.py:354
  31.2 6.8 %collective-permute-start = (f32[3,2,1024]{2,1,0:T(2,128)S(1)}, f32[3,2,1024]{2,1,0:T(2,128)S(1)}, u32[]{:S(2)}, u32[]{:S(2)}) collective-permute-start(f32[3,2,1024]{2,1,0:T(2,128)S(1)} %copy.11), channel_id=1, source_target_pairs={{1,0},{2,1},{3,2},{4,3},{5,4},{6,5},{7,6},{9,8},{10,9},{11,10},{12... | collective-permute-start | bytes 73736 | tf_op jit(solution)/shard_map/ppermute | solution.py:363
  34.7 3.8 %collective-permute-start.1 = (f32[3,2,1024]{2,1,0:T(2,128)S(1)}, f32[3,2,1024]{2,1,0:T(2,128)S(1)}, u32[]{:S(2)}, u32[]{:S(2)}) collective-permute-start(f32[3,2,1024]{2,1,0:T(2,128)S(1)} %copy.13), channel_id=1, source_target_pairs={{0,1},{1,2},{2,3},{3,4},{4,5},{5,6},{6,7},{8,9},{9,10},{10,11},{11... | collective-permute-start | bytes 73736 | tf_op jit(solution)/shard_map/ppermute | solution.py:364
  39.5 2.8 %copy-start.2 = (f32[3,32,32,512]{3,2,1,0:T(8,128)S(1)}, f32[3,32,32,512]{3,2,1,0:T(8,128)}, u32[]{:S(2)}) copy-start(f32[3,32,32,512]{3,2,1,0:T(8,128)} %param.7) | copy-start | bytes 18874372
  43.3 3.1 %copy-start = (f32[3,1024,640]{2,1,0:T(8,128)}, f32[3,1024,640]{2,1,0:T(8,128)S(1)}, u32[]{:S(2)}) copy-start(f32[3,1024,640]{2,1,0:T(8,128)S(1)} %stage.1.staged) | copy-start | bytes 23592964
  48.7 3.2 %copy-start.1 = (f32[3,1024,640]{2,1,0:T(8,128)S(1)}, f32[3,1024,640]{2,1,0:T(8,128)}, u32[]{:S(2)}) copy-start(f32[3,1024,640]{2,1,0:T(8,128)} %copy-done) | copy-start | bytes 23592964
  55.2 12.4 %collective-permute-start.2 = (bf16[3,2,32,640]{3,2,1,0:T(8,128)(2,1)S(1)}, bf16[3,2,32,640]{3,2,1,0:T(8,128)(2,1)S(1)}, u32[]{:S(2)}, u32[]{:S(2)}) collective-permute-start(bf16[3,2,32,640]{3,2,1,0:T(8,128)(2,1)S(1)} %get-tuple-element.16), channel_id=1, source_target_pairs={{0,8},{8,16},{16,24},{24,32},{32,40},{40,48},{48,56},{56,64},{64,7... | collective-permute-start | bytes 737288 | tf_op jit(solution)/shard_map/ppermute | solution.py:398
  58.5 9.2 %collective-permute-start.3 = (bf16[3,2,32,640]{3,2,1,0:T(8,128)(2,1)S(1)}, bf16[3,2,32,640]{3,2,1,0:T(8,128)(2,1)S(1)}, u32[]{:S(2)}, u32[]{:S(2)}) collective-permute-start(bf16[3,2,32,640]{3,2,1,0:T(8,128)(2,1)S(1)} %get-tuple-element.17), channel_id=1, source_target_pairs={{8,0},{16,8},{24,16},{32,24},{40,32},{48,40},{56,48},{64,56},{72,6... | collective-permute-start | bytes 737288 | tf_op jit(solution)/shard_map/ppermute | solution.py:399
  78.7 28.3 %copy-start.7 = (f32[8,3,128]{2,0,1:T(8,128)S(1)}, f32[8,3,128]{2,0,1:T(8,128)}, u32[]{:S(2)}) copy-start(f32[8,3,128]{2,0,1:T(8,128)} %param.8) | copy-start | bytes 36868
  107.0 3.4 %copy-start.5 = (bf16[8,1024,512]{2,1,0:T(8,128)(2,1)S(1)}, bf16[8,1024,512]{2,1,0:T(8,128)(2,1)}, u32[]{:S(2)}) copy-start(bf16[8,1024,512]{2,1,0:T(8,128)(2,1)} %copy-done.4) | copy-start | bytes 25165828

commit v3 on v2

--- a/solution.py
+++ b/solution.py
@@ -27,8 +27,8 @@
 
 
 def spread_kernel(
-    gy_size, slots, pts_hbm, stiff, links_hbm, owners_hbm, patch_slots_hbm, dw_hbm, out, dest_out, dw,
-    force, rows, pts, links, owners, patch_slots, sems,
+    gy_size, slots, pts_hbm, stiff, links_hbm, owners_hbm, patch_slots_hbm, dw_hbm, out, dest_out,
+    dw, force, rows, pts, links, owners, patch_slots, sems,
 ):
     blocks, points = links.shape
     inter = owners.shape[1]
@@ -110,58 +110,50 @@
     out[:, 3 * patch :] = head.astype(BF16)
 
 
-def stage_kernel(velocity, edge, out, sems):
-    patch = velocity.shape[2]
-    main = pltpu.make_async_copy(velocity, out.at[:, :, :patch], sems.at[0])
-    side = pltpu.make_async_copy(edge, out.at[:, :, patch:], sems.at[1])
-    main.start()
-    side.start()
-    main.wait()
-    side.wait()
-
-
-def place_kernel(layer_rows, staged, received, out, low_rows, high_rows, low_f, high_f):
-    cells, wide = staged.shape[1:]
-    patch = wide - LANES
+class Arrived:
+    def __init__(self, received, patch):
+        self.received, self.patch = received, patch
+        slots = received.shape[0]
+        head = received[:, 3 * patch :].astype(F32)
+        head_t = jnp.transpose(head)
+        lane = iota((slots, LANES), 1)
+        self.tails, self.starts = [], []
+        for c in range(3):
+            tail = pltpu.roll(head, LANES - 4 - BELOW - 2 * c, axis=1)
+            self.tails.append(jnp.where(lane >= LANES - 2, tail, 0.0).astype(BF16))
+            start = pltpu.roll(head, LANES - (ABOVE + 2 + 2 * c), axis=1)
+            self.starts.append(jnp.where(lane < 2, start, 0.0).astype(BF16))
+        self.slots = [
+            (head_t[at : at + 1] * 32.0 + head_t[at + 1 : at + 2] - 1.0).astype(jnp.int32) for at in (0, BELOW, ABOVE)
+        ]
+
+    def choose(self, row):
+        return [(row == slot).astype(F32).astype(BF16) for slot in self.slots]
+
+    def force(self, chosen, c):
+        here, below, above = chosen
+        main = dot(here, self.received[:, c * self.patch : (c + 1) * self.patch])
+        return force_step * main, force_step * (dot(below, self.tails[c]) + dot(above, self.starts[c]))
+
+
+def rim_kernel(layer_rows, velocity, edges, received, low_rows, high_rows, rim):
+    layers, patch = low_rows.shape[2], velocity.shape[2]
     slots = received.shape[0]
-    part = 256
-    layers = part // layer_rows
-    head = received[:, 3 * patch :].astype(F32)
-    head_t = jnp.transpose(head)
-    lane = iota((slots, LANES), 1)
-    tails, starts = [], []
-    for c in range(3):
-        tail = pltpu.roll(head, LANES - 4 - BELOW - 2 * c, axis=1)
-        tails.append(jnp.where(lane >= LANES - 2, tail, 0.0).astype(BF16))
-        start = pltpu.roll(head, LANES - (ABOVE + 2 + 2 * c), axis=1)
-        starts.append(jnp.where(lane < 2, start, 0.0).astype(BF16))
-
-    def slot_at(at):
-        return (head_t[at : at + 1] * 32.0 + head_t[at + 1 : at + 2] - 1.0).astype(jnp.int32)
-
-    slot_here, slot_below, slot_above = slot_at(0), slot_at(BELOW), slot_at(ABOVE)
-
-    @pl.loop(0, cells // part)
-    def _(step):
-        row = iota((part, slots), 0) + step * part
-        here = (row == slot_here).astype(F32).astype(BF16)
-        below = (row == slot_below).astype(F32).astype(BF16)
-        above = (row == slot_above).astype(F32).astype(BF16)
-        at = pl.ds(pl.multiple_of(step * part, part), part)
-        for c in range(3):
-            main = staged[c, at, :patch] + force_step * dot(here, received[:, c * patch : (c + 1) * patch])
-            edge = staged[c, at, patch:] + force_step * (dot(below, tails[c]) + dot(above, starts[c]))
-            out[c, at, :patch] = main
-            out[c, at, patch:] = edge
-            to = pl.ds(pl.multiple_of(step * layers, layers), layers)
-            for j in range(2):
-                for side, offset in ((low_f, j), (high_f, layer_rows - 2 + j)):
-                    picks = range(offset, part, layer_rows)
-                    side[c, j, to, :patch] = jnp.concatenate([main[i : i + 1] for i in picks], axis=0)
-                    side[c, j, to, patch:] = jnp.concatenate([edge[i : i + 1] for i in picks], axis=0)
-
-    low_rows[...] = low_f[...].astype(BF16)
-    high_rows[...] = high_f[...].astype(BF16)
+    arrived = Arrived(received, patch)
+    row = iota((4 * layers, slots), 0)
+    line, z = row // layers, lax.rem(row, layers)
+    chosen = arrived.choose(z * layer_rows + jnp.where(line < 2, line, layer_rows - 4 + line))
+    for c in range(3):
+        main, edge = arrived.force(chosen, c)
+        main, edge = velocity[c] + main, edges[c] + edge
+        for j in range(4):
+            at = slice(j * layers, (j + 1) * layers)
+            to = low_rows if j < 2 else high_rows
+            to[c, j % 2, :, :patch] = main[at].astype(BF16)
+            to[c, j % 2, :, patch:] = edge[at].astype(BF16)
+        for side, at in ((0, slice(0, layers)), (1, slice(3 * layers, 4 * layers))):
+            rim[side, c, :, :patch] = main[at]
+            rim[side, c, :, patch:] = edge[at]
 
 
 def update(centre, weights, c, east, west, north, south, up, down):
@@ -179,7 +171,7 @@
     return jnp.where(lane == 0, sides[3], 0.0) + jnp.where(lane == LANES - 1, sides[2], 0.0)
 
 
-def sweep(source, low_row, high_row, store, keep):
+def sweep(source, low_row, high_row, store, keep, after=None):
     layers, rows, wide = source.shape[1:]
     sub = iota((8, keep), 0)
 
@@ -206,35 +198,59 @@
                     source[c, z_up, x : x + 8, :keep], source[c, z_down, x : x + 8, :keep],
                 )
                 store(c, z, x, new)
-
-
-def first_kernel(sides, u0, u1):
-    patch = u0.shape[3] - LANES
+        if after is not None:
+            after(z)
+
+
+def first_kernel(sides, velocity, edges, received, u1, u0, sems):
+    layers, rows, wide = u0.shape[1:]
+    patch = wide - LANES
+    part = 8
+    slots = received.shape[0]
+
+    def load(step):
+        at = pl.ds(step * part, part)
+        return pltpu.make_async_copy(velocity.at[:, at], u0.at[:, at, :, pl.ds(0, patch)], sems.at[step])
+
+    for step in range(layers // part):
+        load(step).start()
+    arrived = Arrived(received, patch)
+
+    @pl.loop(0, layers // part)
+    def _(step):
+        at = pl.ds(step * part, part)
+        chosen = arrived.choose(iota((part * rows, slots), 0) + step * (part * rows))
+        load(step).wait()
+        for c in range(3):
+            main, edge = arrived.force(chosen, c)
+            u0[c, at, :, :patch] += main.reshape(part, rows, patch)
+            u0[c, at, :, patch:] = edges[c, at] + edge.reshape(part, rows, LANES)
+
     mask = edge_mask(sides)
 
     def store(c, z, x, new):
         u1[c, z, x : x + 8, :patch] = new[:, :patch]
         u1[c, z, x : x + 8, patch:] = new[:, patch:] * mask
 
-    sweep(u0, lambda c, z: 0.0, lambda c, z: 0.0, store, u0.shape[3])
-
-
-def last_kernel(sides, u1_in, low_f, high_f, below_x, above_x, received, fluid_hbm, replies, u1, mid, fluid, sems):
+    sweep(u0, lambda c, z: 0.0, lambda c, z: 0.0, store, wide)
+
+
+def last_kernel(sides, u1_in, rim, below_x, above_x, received, fluid_hbm, replies, u1, mid, fluid, sems):
     layers, rows, wide = u1.shape[1:]
     patch = wide - LANES
     slots = received.shape[0]
     mask = edge_mask(sides)[0:1]
 
     for side in range(2):
-        halo, inner, row = (below_x, low_f, 0) if side == 0 else (above_x, high_f, rows - 1)
+        halo, row = (below_x, 0) if side == 0 else (above_x, rows - 1)
         near = 1 - side
         centre = [halo[c, near].astype(F32) for c in range(3)]
         weights = mix(centre)
         slope = transport_rate if side == 0 else -transport_rate
-        own = viscosity + slope * inner[0, side]
+        own = viscosity + slope * rim[side, 0]
         for c in range(3):
             outer = halo[c, side].astype(F32)
-            inside = inner[c, side]
+            inside = rim[side, c]
             east, west = (inside, outer) if side == 0 else (outer, inside)
             v = centre[c]
             new = update(
@@ -250,6 +266,17 @@
                 u1[c, z, row : row + 1, :patch] += term[z : z + 1, :patch]
                 u1[c, z, row : row + 1, patch:] += tail[z : z + 1]
 
+    part = 8
+
+    def write(step):
+        at = pl.ds(pl.multiple_of(step * part * rows, part * rows), part * rows)
+        return pltpu.make_async_copy(fluid.at[:, at], fluid_hbm.at[:, at], sems.at[step])
+
+    def after(z):
+        @pl.when(lax.rem(z, part) == part - 1)
+        def _():
+            write(z // part).start()
+
     def store(c, z, x, new):
         fluid[c, pl.ds(pl.multiple_of(z * rows + x, 8), 8), :] = new
 
@@ -259,9 +286,8 @@
         lambda c, z: mid[1, c, pl.ds(z, 1), :patch],
         store,
         patch,
+        after,
     )
-    write = pltpu.make_async_copy(fluid, fluid_hbm, sems.at[0])
-    write.start()
 
     heads = received[:, 3 * patch :].astype(F32)
     slot = (heads[:, 0:1] * 32.0 + heads[:, 1:2] - 1.0).astype(jnp.int32)
@@ -272,13 +298,16 @@
             pick = (iota((slots, chunk), 1) + first == slot).astype(F32).astype(BF16)
             total += dot(pick, fluid[c, first : first + chunk, :].astype(BF16))
         replies[:, c * patch : (c + 1) * patch] = total.astype(BF16)
-    write.wait()
-
-
-def gather_kernel(pts, dest, returned, dw, out, picked, moved):
+    for step in range(layers // part):
+        write(step).wait()
+
+
+def gather_kernel(pts, dest, returned, dw_hbm, out, dw, picked, moved, sems):
     entries, slots = dest.shape[0], returned.shape[0]
     blocks, patch, points = dw.shape[0], dw.shape[2], pts.shape[2]
     inter = entries // blocks
+    for b in range(blocks):
+        pltpu.make_async_copy(dw_hbm.at[b], dw.at[b], sems.at[b]).start()
     to = dest[:, 0:1].astype(jnp.int32)
     pick = (iota((entries, slots), 1) == to).astype(F32).astype(BF16)
     for c in range(3):
@@ -291,6 +320,7 @@
         at = pl.ds(pl.multiple_of(b * inter, inter), inter)
         parts = [picked[c, at, :] for c in range(3)]
         parts.append(jnp.zeros_like(parts[0]))
+        pltpu.make_async_copy(dw_hbm.at[b], dw.at[b], sems.at[b]).wait()
         every = lax.dot_general(
             jnp.concatenate(parts, axis=0).astype(BF16), dw[b], (((1,), (1,)), ((), ())), preferred_element_type=F32
         )
@@ -326,16 +356,16 @@
     def cost(flops, size):
         return pl.CostEstimate(flops=flops, bytes_accessed=size * mb, transcendentals=0)
 
-    outgoing, dest, dw_near = pl.pallas_call(
+    outgoing, dest = pl.pallas_call(
         functools.partial(spread_kernel, gy_size, slots),
         in_specs=[hbm, smem, hbm, hbm, hbm, hbm],
-        out_specs=[vmem, vmem, vmem],
+        out_specs=[vmem, vmem],
         out_shape=[
             jax.ShapeDtypeStruct((slots, width), BF16),
             jax.ShapeDtypeStruct((entries, LANES), F32),
-            jax.ShapeDtypeStruct(dw.shape, BF16),
         ],
         scratch_shapes=[
+            pltpu.VMEM(dw.shape, BF16),
             pltpu.VMEM((3, blocks, points), F32),
             pltpu.VMEM((3, entries, patch), F32),
             pltpu.VMEM((3, blocks, points), F32),
@@ -344,7 +374,7 @@
             pltpu.VMEM((blocks, inter), jnp.int32),
             pltpu.SemaphoreType.DMA((blocks + 4,)),
         ],
-        compiler_params=params(16),
+        compiler_params=params(60),
         cost_estimate=cost(10**9, 9),
         name="spread",
     )(pts, stiffness, links, owners.reshape(blocks, inter), patch_slots, dw)
@@ -365,34 +395,25 @@
     edge = jnp.concatenate(
         [first.transpose(0, 2, 1), jnp.zeros((3, cells, LANES - 4), F32), last.transpose(0, 2, 1)], axis=2
     )
-    staged = pl.pallas_call(
-        stage_kernel,
-        in_specs=[hbm, anywhere],
-        out_specs=vmem,
-        out_shape=jax.ShapeDtypeStruct((3, cells, wide), F32),
-        scratch_shapes=[pltpu.SemaphoreType.DMA((2,))],
-        compiler_params=params(16),
-        cost_estimate=cost(0, 8),
-        name="stage",
-    )(flat, edge)
+    lines = (0, 1, rows - 2, rows - 1)
+    rim_velocity = jnp.stack([velocity[:, :, x, :] for x in lines], axis=1).reshape(3, 4 * layers, patch)
+    edge = edge.reshape(3, layers, rows, LANES)
+    rim_edge = jnp.stack([edge[:, :, x, :] for x in lines], axis=1).reshape(3, 4 * layers, LANES)
 
     side = (3, 2, layers, wide)
-    u0, low_rows, high_rows, low_f, high_f = pl.pallas_call(
-        functools.partial(place_kernel, rows),
-        in_specs=[vmem, vmem],
-        out_specs=[vmem] * 5,
+    low_rows, high_rows, rim = pl.pallas_call(
+        functools.partial(rim_kernel, rows),
+        in_specs=[vmem] * 3,
+        out_specs=[vmem] * 3,
         out_shape=[
-            jax.ShapeDtypeStruct((3, cells, wide), F32),
             jax.ShapeDtypeStruct(side, BF16),
             jax.ShapeDtypeStruct(side, BF16),
-            jax.ShapeDtypeStruct(side, F32),
-            jax.ShapeDtypeStruct(side, F32),
-        ],
-        input_output_aliases={0: 0},
+            jax.ShapeDtypeStruct((2, 3, layers, wide), F32),
+        ],
         compiler_params=params(24),
-        cost_estimate=cost(10**9, 10),
-        name="place",
-    )(staged, received)
+        cost_estimate=cost(10**8, 3),
+        name="rim",
+    )(rim_velocity, rim_edge, received)
 
     up = [(i, i + 1) for i in range(gx_size - 1)]
     below_x = lax.ppermute(high_rows, "gx", up)
@@ -402,16 +423,17 @@
     sides = jnp.stack([gx > 0, gx < gx_size - 1, gy > 0, gy < gy_size - 1]).astype(F32)
     u1 = pl.pallas_call(
         first_kernel,
-        in_specs=[smem, vmem],
+        in_specs=[smem, hbm, vmem, vmem],
         out_specs=vmem,
         out_shape=jax.ShapeDtypeStruct((3, layers, rows, wide), F32),
+        scratch_shapes=[pltpu.VMEM((3, layers, rows, wide), F32), pltpu.SemaphoreType.DMA((layers // 8,))],
         compiler_params=params(24),
-        cost_estimate=cost(2 * 10**9, 16),
+        cost_estimate=cost(2 * 10**9, 24),
         name="sweep_first",
-    )(sides, u0.reshape(3, layers, rows, wide))
+    )(sides, pltpu.with_memory_space_constraint(velocity, pltpu.HBM), edge, received)
     fluid, replies, _ = pl.pallas_call(
         last_kernel,
-        in_specs=[smem] + [vmem] * 6,
+        in_specs=[smem] + [vmem] * 5,
         out_specs=[hbm, vmem, vmem],
         out_shape=[
             jax.ShapeDtypeStruct((3, cells, patch), F32),
@@ -421,25 +443,30 @@
         scratch_shapes=[
             pltpu.VMEM((2, 3, layers, wide), F32),
             pltpu.VMEM((3, cells, patch), F32),
-            pltpu.SemaphoreType.DMA((1,)),
+            pltpu.SemaphoreType.DMA((layers // 8,)),
         ],
         input_output_aliases={1: 2},
         compiler_params=params(24),
         cost_estimate=cost(2 * 10**9, 16),
         name="sweep_last",
-    )(sides, u1, low_f, high_f, below_x, above_x, received)
+    )(sides, u1, rim, below_x, above_x, received)
 
     returned = exchange(replies)
     moved = pl.pallas_call(
         gather_kernel,
-        in_specs=[vmem] * 4,
+        in_specs=[vmem] * 3 + [hbm],
         out_specs=vmem,
         out_shape=jax.ShapeDtypeStruct((3, blocks, points), F32),
-        scratch_shapes=[pltpu.VMEM((3, entries, patch), F32), pltpu.VMEM((3, blocks, points), F32)],
-        compiler_params=params(16),
+        scratch_shapes=[
+            pltpu.VMEM(dw.shape, BF16),
+            pltpu.VMEM((3, entries, patch), F32),
+            pltpu.VMEM((3, blocks, points), F32),
+            pltpu.SemaphoreType.DMA((blocks,)),
+        ],
+        compiler_params=params(56),
         cost_estimate=cost(10**9, 9),
         name="interp",
-    )(pts, dest, returned, dw_near)
+    )(pts, dest, returned, dw)
     return fluid.reshape(3, layers, rows, columns), moved.transpose(1, 0, 2)
 
 

time: 115 us -> 106 us (0.922)
  local copies, waits for them, and re-layouts: 31.1 us -> 17.8 us
  Pallas kernels: 31.4 us -> 34.2 us
  other arithmetic: 0.56 us -> 3.2 us
    unnamed x24 -> x0, local copies, waits for them, and re-layouts: 22.5 us -> none
    another operation x0 -> x3, local copies, waits for them, and re-layouts: none -> 4.09 us  [the longest x2 4.07 us: shards(): jnp.stack([velocity[:, :, x, :] for x in lines], axis=1)]
    transpose x0 -> x2, local copies, waits for them, and re-layouts: none -> 3.33 us  [the longest x1 1.67 us: shards(): first.transpose(0, 2, 1)]
    concatenate x1, other arithmetic: 0.48 us -> 2.35 us  [shards(): jnp.concatenate([first.transpose(0, 2, 1), jnp.zeros((3, cells, LANES - 4...]
    reshape x2, local copies, waits for them, and re-layouts: 1.52 us -> 3.26 us  [exchange(): rows_out.reshape(devices, 2, size)]
    pallas_call x1, Pallas kernels: 4.49 us -> 6.23 us  [shards(): pl.pallas_call(functools.partial(spread_kernel, gy_size, slots), in_specs...]
    pallas_call x5 -> x4, Pallas kernels: 26.9 us -> 27.9 us  [the longest x1 11.8 us: shards(): pl.pallas_call(first_kernel, in_specs=[smem, hbm, vmem, vmem], out_specs=...]
  transfers between devices with their start and end apart: 5 -> 5, of which waited for: 2 -> 0; matrix products, arithmetic and copies ran while one was open for 4% -> 13% of each run, Pallas kernels for 8% -> 11%
where the time goes in v3:
time: 106 us; the launch traced here: 105 us
  Pallas kernels  34.2 us (32%)
  blocking collectives  27.3 us (26%)
  starting transfers between devices  21.9 us (21%)
  local copies, waits for them, and re-layouts  17.8 us (17%)
  other arithmetic  3.2 us (3%)
    all_to_all x1, blocking collectives, exchange(): lax.all_to_all(rows_out.reshape(devices, 2, size), ('gx', 'gy'), split_ax...  27.3 us
    all_to_all x1, starting transfers between devices, exchange(): lax.all_to_all(rows_out.reshape(devices, 2, size), ('gx', 'gy'), split_ax...  11.9 us
    pallas_call x1, Pallas kernels, shards(): pl.pallas_call(first_kernel, in_specs=[smem, hbm, vmem, vmem], out_specs=...  11.8 us
    pallas_call x1, Pallas kernels, shards(): pl.pallas_call(last_kernel, in_specs=[smem] + [vmem] * 5, out_specs=[hbm,...  9.18 us
    pallas_call x1, Pallas kernels, shards(): pl.pallas_call(gather_kernel, in_specs=[vmem] * 3 + [hbm], out_specs=vmem...  6.51 us
    pallas_call x1, Pallas kernels, shards(): pl.pallas_call(functools.partial(spread_kernel, gy_size, slots), in_specs...  6.23 us
    another operation x2, local copies, waits for them, and re-layouts, shards(): jnp.stack([velocity[:, :, x, :] for x in lines], axis=1)  4.07 us
    ppermute x1, starting transfers between devices, shards(): lax.ppermute(flat[:, :, columns - 2:].transpose(0, 2, 1), 'gy', behind)  3.66 us
  transfers between devices with their start and end apart: 5, of which 0 were waited for; matrix products, arithmetic and copies ran while one was open for 13% of the time, Pallas kernels for 11%

profile of v3, /device:TPU:1, one launch (start us, length us, event | category | flops | bytes accessed | tf_op | source)
XLA Modules:
  0.0 105.2 jit_solution(9054046418184119226)
XLA Ops:
  0.6 6.2 %spread.1 = (bf16[256,1664]{1,0:T(8,128)(2,1)}, f32[64,128]{1,0:T(8,128)}) custom-call(f32[3,8,128]{2,1,0:T(8,128)} %bitcast.48, f32[8]{0:T(128)} %stiff.1, s32[8,128]{1,0:T(8,128)} %links_hbm.1, s32[8,8]{1,0:T(8,128)} %bitcast.53, s32[8,8]{1,0:T(8,128)} %patch_slots_hbm.1, bf16[8,1024,512]{2,1,0:T(8,128)(2,1)} %bitcast.41), custom_call_target="tpu_custom_call" | custom-call | flops 1000000000 | bytes 9437184 | tf_op jit(solution)/shard_map/spread/pallas_call | solution.py:359
  6.9 3.0 %reshape.41 = bf16[128,2,1664]{2,1,0:T(2,128)(2,1)} reshape(bf16[256,1664]{1,0:T(8,128)(2,1)} %get-tuple-element.9) | data formatting | bytes 1703936 | tf_op jit(solution)/shard_map/reshape | solution.py:385
  9.8 11.9 %all-to-all-start = ((bf16[128,2,1664]{2,1,0:T(2,128)(2,1)}), bf16[128,2,1664]{2,1,0:T(2,128)(2,1)}, u32[]{:S(2)}, u32[]{:S(2)}) async-start(bf16[128,2,1664]{2,1,0:T(2,128)(2,1)} %reshape.41), calls=%async_computation | async-start | bytes 1703936 | tf_op jit(solution)/shard_map/all_to_all | solution.py:384
  21.7 2.4 %slice_bitcast_fusion.1 = (f32[3,2,1024]{1,2,0:T(8,128)S(1)}, f32[3,2,1024]{1,2,0:T(8,128)S(1)}) fusion(f32[3,1024,512]{2,1,0:T(8,128)} %bitcast.43), kind=kLoop, calls=%fused_computation.1 | loop fusion | bytes 98304 | tf_op jit(solution)/shard_map/transpose | solution.py:393
  24.1 0.5 copy.24
  24.6 3.7 %collective-permute-start.1 = (f32[3,2,1024]{2,1,0:T(2,128)S(1)}, f32[3,2,1024]{2,1,0:T(2,128)S(1)}, u32[]{:S(2)}, u32[]{:S(2)}) collective-permute-start(f32[3,2,1024]{2,1,0:T(2,128)S(1)} %copy.24), channel_id=1, source_target_pairs={{0,1},{1,2},{2,3},{3,4},{4,5},{5,6},{6,7},{8,9},{9,10},{10,11},{11... | collective-permute-start | bytes 73736 | tf_op jit(solution)/shard_map/ppermute | solution.py:394
  28.3 0.5 copy.23
  28.7 1.9 %collective-permute-start = (f32[3,2,1024]{2,1,0:T(2,128)S(1)}, f32[3,2,1024]{2,1,0:T(2,128)S(1)}, u32[]{:S(2)}, u32[]{:S(2)}) collective-permute-start(f32[3,2,1024]{2,1,0:T(2,128)S(1)} %copy.23), channel_id=1, source_target_pairs={{1,0},{2,1},{3,2},{4,3},{5,4},{6,5},{7,6},{9,8},{10,9},{11,10},{12... | collective-permute-start | bytes 73736 | tf_op jit(solution)/shard_map/ppermute | solution.py:393
  30.7 3.8 %slice_bitcast_fusion.5 = (f32[3,1,32,512]{3,1,2,0:T(1,128)S(1)}, f32[3,1,32,512]{3,1,2,0:T(1,128)S(1)}, f32[3,1,32,512]{3,1,2,0:T(1,128)S(1)}, f32[3,1,32,512]{3,1,2,0:T(1,128)S(1)}) fusion(f32[3,32,32,512]{3,2,1,0:T(8,128)} %velocity.1), kind=kLoop, calls=%fused_computation.8 | loop fusion | bytes 1572864 | tf_op jit(solution)/shard_map/stack;squeeze | solution.py:399
  34.5 0.7 pad_maximum_fusion.1
  35.3 0.3 copy.27
  35.6 1.7 %copy.25 = f32[3,1024,2]{2,1,0:T(8,128)} copy(f32[3,1024,2]{1,2,0:T(2,128)S(1)} %bitcast.51) | data formatting | bytes 49152 | tf_op jit(solution)/shard_map/transpose | solution.py:396
  37.3 1.7 %copy.26 = f32[3,1024,2]{2,1,0:T(8,128)} copy(f32[3,1024,2]{1,2,0:T(2,128)S(1)} %bitcast.50) | data formatting | bytes 49152 | tf_op jit(solution)/shard_map/transpose | solution.py:396
  39.0 2.4 %pad_maximum_fusion = f32[3,1024,128]{2,1,0:T(8,128)S(1)} fusion(f32[3,1024,2]{2,1,0:T(8,128)} %copy.26, f32[3,1024,2]{2,1,0:T(8,128)} %copy.25, f32[128]{0:T(128)S(1)} %pad.9.clone), kind=kLoop, calls=%fused_computation.2 | loop fusion | flops 786432 | bytes 1622528 | tf_op jit(solution)/shard_map/concatenate | solution.py:395
  41.5 2.4 %reshape.42.received = bf16[256,1664]{1,0:T(8,128)(2,1)S(1)} reshape(bf16[128,2,1664]{2,1,0:T(2,128)(2,1)} %all-to-all-done) | data formatting | bytes 1703936 | tf_op jit(solution)/shard_map/reshape | solution.py:386
  43.9 0.5 rim.1
  44.4 3.1 %collective-permute-start.2 = (bf16[3,2,32,640]{3,2,1,0:T(8,128)(2,1)S(1)}, bf16[3,2,32,640]{3,2,1,0:T(8,128)(2,1)S(1)}, u32[]{:S(2)}, u32[]{:S(2)}) collective-permute-start(bf16[3,2,32,640]{3,2,1,0:T(8,128)(2,1)S(1)} %get-tuple-element.11), channel_id=1, source_target_pairs={{0,8},{8,16},{16,24},{24,32},{32,40},{40,48},{48,56},{56,64},{64,7... | collective-permute-start | bytes 737288 | tf_op jit(solution)/shard_map/ppermute | solution.py:419
  47.5 1.3 %collective-permute-start.3 = (bf16[3,2,32,640]{3,2,1,0:T(8,128)(2,1)S(1)}, bf16[3,2,32,640]{3,2,1,0:T(8,128)(2,1)S(1)}, u32[]{:S(2)}, u32[]{:S(2)}) collective-permute-start(bf16[3,2,32,640]{3,2,1,0:T(8,128)(2,1)S(1)} %get-tuple-element.12), channel_id=1, source_target_pairs={{8,0},{16,8},{24,16},{32,24},{40,32},{48,40},{56,48},{64,56},{72,6... | collective-permute-start | bytes 737288 | tf_op jit(solution)/shard_map/ppermute | solution.py:420
  48.9 11.8 %sweep_first.1.u1_in = f32[3,32,32,640]{3,2,1,0:T(8,128)S(1)} custom-call(f32[4]{0:T(128)S(1)} %add_convert_fusion.sides, f32[3,32,32,512]{3,2,1,0:T(8,128)} %velocity.1, f32[3,32,32,128]{3,2,1,0:T(8,128)S(1)} %bitcast.38, bf16[256,1664]{1,0:T(8,128)(2,1)S(1)} %reshape.42.received), custom_call_target="tpu_custom_call" | custom-call | flops 2000000000 | bytes 25165824 | tf_op jit(solution)/shard_map/sweep_first/pallas_call | solution.py:424
  60.7 9.2 %sweep_last.1 = (f32[3,1024,512]{2,1,0:T(8,128)}, bf16[256,1536]{1,0:T(8,128)(2,1)S(1)}, f32[3,32,32,640]{3,2,1,0:T(8,128)S(1)}) custom-call(f32[4]{0:T(128)S(1)} %add_convert_fusion.sides, f32[3,32,32,640]{3,2,1,0:T(8,128)S(1)} %sweep_first.1.u1_in, f32[2,3,32,640]{3,2,1,0:T(8,128)S(1)} %get-tuple-element.10.rim, ...), custom_call_target="tpu_custom_call", output_to_operand_aliasing={{2}: (1, {})} | custom-call | flops 2000000000 | bytes 16777216 | tf_op jit(solution)/shard_map/sweep_last/pallas_call | solution.py:434
  69.9 0.3 reshape.46
  70.2 27.3 %all_to_all.10 = bf16[128,2,1536]{2,1,0:T(2,128)(2,1)S(1)} all-to-all(bf16[128,2,1536]{2,1,0:T(2,128)(2,1)S(1)} %reshape.46), channel_id=1, replica_groups=mesh['gx'=16,'gy'=8] {'gx','gy'}, dimensions={0} | all-to-all | bytes 1572864 | tf_op jit(solution)/shard_map/all_to_all | solution.py:384
  97.5 1.2 %reshape.47.returned = bf16[256,1536]{1,0:T(8,128)(2,1)} reshape(bf16[128,2,1536]{2,1,0:T(2,128)(2,1)S(1)} %all_to_all.10) | data formatting | bytes 1572864 | tf_op jit(solution)/shard_map/reshape | solution.py:386
  98.7 6.5 %interp.1 = f32[3,8,128]{2,1,0:T(8,128)} custom-call(f32[3,8,128]{2,1,0:T(8,128)} %bitcast.49, f32[64,128]{1,0:T(8,128)} %get-tuple-element.14.dest, bf16[256,1536]{1,0:T(8,128)(2,1)} %reshape.47.returned, bf16[8,1024,512]{2,1,0:T(8,128)(2,1)} %bitcast.42), custom_call_target="tpu_custom_call" | custom-call | flops 1000000000 | bytes 9437184 | tf_op jit(solution)/shard_map/interp/pallas_call | solution.py:455
  (11 shorter events, 0.3 us)
Async XLA Ops:
  9.8 31.7 %all-to-all-start = ((bf16[128,2,1664]{2,1,0:T(2,128)(2,1)}), bf16[128,2,1664]{2,1,0:T(2,128)(2,1)}, u32[]{:S(2)}, u32[]{:S(2)}) async-start(bf16[128,2,1664]{2,1,0:T(2,128)(2,1)} %reshape.41), calls=%async_computation | async-start | bytes 1703936 | tf_op jit(solution)/shard_map/all_to_all | solution.py:384
  24.6 12.7 %collective-permute-start.1 = (f32[3,2,1024]{2,1,0:T(2,128)S(1)}, f32[3,2,1024]{2,1,0:T(2,128)S(1)}, u32[]{:S(2)}, u32[]{:S(2)}) collective-permute-start(f32[3,2,1024]{2,1,0:T(2,128)S(1)} %copy.24), channel_id=1, source_target_pairs={{0,1},{1,2},{2,3},{3,4},{4,5},{5,6},{6,7},{8,9},{9,10},{10,11},{11... | collective-permute-start | bytes 73736 | tf_op jit(solution)/shard_map/ppermute | solution.py:394
  28.7 6.9 %collective-permute-start = (f32[3,2,1024]{2,1,0:T(2,128)S(1)}, f32[3,2,1024]{2,1,0:T(2,128)S(1)}, u32[]{:S(2)}, u32[]{:S(2)}) collective-permute-start(f32[3,2,1024]{2,1,0:T(2,128)S(1)} %copy.23), channel_id=1, source_target_pairs={{1,0},{2,1},{3,2},{4,3},{5,4},{6,5},{7,6},{9,8},{10,9},{11,10},{12... | collective-permute-start | bytes 73736 | tf_op jit(solution)/shard_map/ppermute | solution.py:393
  44.4 16.3 %collective-permute-start.2 = (bf16[3,2,32,640]{3,2,1,0:T(8,128)(2,1)S(1)}, bf16[3,2,32,640]{3,2,1,0:T(8,128)(2,1)S(1)}, u32[]{:S(2)}, u32[]{:S(2)}) collective-permute-start(bf16[3,2,32,640]{3,2,1,0:T(8,128)(2,1)S(1)} %get-tuple-element.11), channel_id=1, source_target_pairs={{0,8},{8,16},{16,24},{24,32},{32,40},{40,48},{48,56},{56,64},{64,7... | collective-permute-start | bytes 737288 | tf_op jit(solution)/shard_map/ppermute | solution.py:419
  47.5 13.2 %collective-permute-start.3 = (bf16[3,2,32,640]{3,2,1,0:T(8,128)(2,1)S(1)}, bf16[3,2,32,640]{3,2,1,0:T(8,128)(2,1)S(1)}, u32[]{:S(2)}, u32[]{:S(2)}) collective-permute-start(bf16[3,2,32,640]{3,2,1,0:T(8,128)(2,1)S(1)} %get-tuple-element.12), channel_id=1, source_target_pairs={{8,0},{16,8},{24,16},{32,24},{40,32},{48,40},{56,48},{64,56},{72,6... | collective-permute-start | bytes 737288 | tf_op jit(solution)/shard_map/ppermute | solution.py:420

commit v4 on v3

v4 whole, which is shorter than its diff:
```python
import functools

import jax
import jax.numpy as jnp
from jax import lax
from jax.experimental import pallas as pl
from jax.experimental.pallas import tpu as pltpu
from jax.sharding import PartitionSpec as P

viscosity = 0.1
transport_rate = 0.1
force_step = 0.5
fiber_step = 0.25

F32 = jnp.float32
BF16 = jnp.bfloat16
LANES = 128
BELOW, ABOVE = 2, 10


def dot(a, b):
    return jnp.dot(a, b, preferred_element_type=F32)


def iota(shape, axis):
    return lax.broadcasted_iota(jnp.int32, shape, axis)


def spread_kernel(
    gy_size, slots, pts_hbm, stiff_hbm, links_hbm, owners_hbm, patch_slots_hbm, dw_hbm, out, dest_out,
    dw, force, rows, choose, pts, stiff, links, owners, patch_slots, sems,
):
    blocks, points = links.shape
    inter = owners.shape[1]
    entries = blocks * inter
    patch = rows.shape[2]
    small = [
        (pts_hbm, pts), (stiff_hbm, stiff), (links_hbm, links), (owners_hbm, owners), (patch_slots_hbm, patch_slots)
    ]
    small = [pltpu.make_async_copy(a, b, sems.at[blocks + i]) for i, (a, b) in enumerate(small)]
    for copy in small + [pltpu.make_async_copy(dw_hbm.at[b], dw.at[b], sems.at[b]) for b in range(blocks)]:
        copy.start()
    for copy in small:
        copy.wait()
    partner = lax.rem(iota((blocks, points), 1) + links[...], points)
    for c in range(3):
        own = pts[c]
        force[c] = jnp.take_along_axis(own, partner, axis=1) - own

    pick_block = (iota((entries, blocks), 0) // inter == iota((entries, blocks), 1)).astype(F32).astype(BF16)
    pick_k = lax.rem(iota((entries, inter), 0), inter) == iota((entries, inter), 1)

    def as_column(table):
        spread_rows = dot(pick_block, table.astype(F32).astype(BF16))
        return jnp.sum(jnp.where(pick_k, spread_rows, 0.0), axis=1, keepdims=True)

    owner = as_column(owners[...])
    code = patch_slots[...] + 1
    high, low = as_column(code // 32), as_column(lax.rem(code, 32))
    owner_wide = jnp.broadcast_to(owner, (entries, LANES))
    owner_row = jnp.transpose(
        jnp.concatenate([owner_wide, jnp.zeros((LANES - entries, LANES), F32)], axis=0)
    )[:entries, :entries]
    same = (owner_wide[:, :entries] == owner_row) & (iota((entries, entries), 1) < iota((entries, entries), 0))
    rank = jnp.sum(jnp.where(same, 1.0, 0.0), axis=1, keepdims=True)
    dest_wide = jnp.broadcast_to(owner * 2.0 + rank, (entries, LANES))
    dest_out[...] = dest_wide
    padded = jnp.concatenate([dest_wide, jnp.full((LANES - entries, LANES), -8.0, F32)], axis=0)
    dest_row = jnp.transpose(padded)[0:1, :entries].astype(jnp.int32)
    position = lax.rem(dest_row // 2, gy_size)
    slot = iota((slots, entries), 0)
    choose[0] = (slot == dest_row).astype(F32).astype(BF16)
    choose[1] = ((slot == dest_row + 2) & (position < gy_size - 1)).astype(F32).astype(BF16)
    choose[2] = ((slot == dest_row - 2) & (position > 0)).astype(F32).astype(BF16)
    lane = iota((entries, LANES), 1)

    def digits(at):
        return jnp.where(lane == at, high, 0.0) + jnp.where(lane == at + 1, low, 0.0)

    own_head, above_head, below_head = digits(0), digits(BELOW), digits(ABOVE)
    group = iota((inter, inter * points), 0)
    column = iota((inter, inter * points), 1) // points

    @pl.loop(0, blocks)
    def _(b):
        stiffness = stiff[b]
        parts = []
        for c in range(3):
            row = (stiffness * force[c, pl.ds(b, 1), :]).astype(BF16).astype(F32)
            wide = jnp.concatenate([jnp.broadcast_to(row, (inter, points))] * inter, axis=1)
            parts.append(jnp.where(group == column, wide, 0.0))
        parts.append(jnp.zeros_like(parts[0]))
        pltpu.make_async_copy(dw_hbm.at[b], dw.at[b], sems.at[b]).wait()
        spread = dot(jnp.concatenate(parts, axis=0).astype(BF16), dw[b])
        for c in range(3):
            rows[c, pl.ds(pl.multiple_of(b * inter, inter), inter), :] = spread[c * inter : (c + 1) * inter]

    for c in range(3):
        tail = pltpu.roll(rows[c, :, patch - LANES :], BELOW + 4 + 2 * c, axis=1)
        at = BELOW + 2 + 2 * c
        above_head += jnp.where((lane == at) | (lane == at + 1), tail, 0.0)
        at = ABOVE + 2 + 2 * c
        start = pltpu.roll(rows[c, :, :LANES], at, axis=1)
        below_head += jnp.where((lane == at) | (lane == at + 1), start, 0.0)
        out[:, c * patch : (c + 1) * patch] = dot(choose[0], rows[c].astype(BF16)).astype(BF16)
    head = dot(choose[0], own_head.astype(BF16))
    head += dot(choose[1], above_head.astype(BF16))
    head += dot(choose[2], below_head.astype(BF16))
    out[:, 3 * patch :] = head.astype(BF16)


class Arrived:
    def __init__(self, received, patch):
        self.received, self.patch = received, patch
        slots = received.shape[0]
        head = received[:, 3 * patch :].astype(F32)
        head_t = jnp.transpose(head)
        lane = iota((slots, LANES), 1)
        self.tails, self.starts = [], []
        for c in range(3):
            tail = pltpu.roll(head, LANES - 4 - BELOW - 2 * c, axis=1)
            self.tails.append(jnp.where(lane >= LANES - 2, tail, 0.0).astype(BF16))
            start = pltpu.roll(head, LANES - (ABOVE + 2 + 2 * c), axis=1)
            self.starts.append(jnp.where(lane < 2, start, 0.0).astype(BF16))
        self.slots = [
            (head_t[at : at + 1] * 32.0 + head_t[at + 1 : at + 2] - 1.0).astype(jnp.int32) for at in (0, BELOW, ABOVE)
        ]

    def choose(self, row):
        return [(row == slot).astype(F32).astype(BF16) for slot in self.slots]

    def force(self, chosen, c):
        here, below, above = chosen
        main = dot(here, self.received[:, c * self.patch : (c + 1) * self.patch])
        return force_step * main, force_step * (dot(below, self.tails[c]) + dot(above, self.starts[c]))


def rim_kernel(layer_rows, velocity, edges, received, low_rows, high_rows, rim):
    layers, patch = low_rows.shape[2], velocity.shape[2]
    slots = received.shape[0]
    arrived = Arrived(received, patch)
    row = iota((4 * layers, slots), 0)
    line, z = row // layers, lax.rem(row, layers)
    chosen = arrived.choose(z * layer_rows + jnp.where(line < 2, line, layer_rows - 4 + line))
    for c in range(3):
        main, edge = arrived.force(chosen, c)
        main, edge = velocity[c] + main, edges[c] + edge
        for j in range(4):
            at = slice(j * layers, (j + 1) * layers)
            to = low_rows if j < 2 else high_rows
            to[c, j % 2, :, :patch] = main[at].astype(BF16)
            to[c, j % 2, :, patch:] = edge[at].astype(BF16)
        for side, at in ((0, slice(0, layers)), (1, slice(3 * layers, 4 * layers))):
            rim[side, c, :, :patch] = main[at]
            rim[side, c, :, patch:] = edge[at]


def update(centre, weights, c, east, west, north, south, up, down):
    (px, mx), (py, my), (pz, mz) = weights
    keep = 1.0 - 6.0 * viscosity
    return keep * centre[c] + px * east + mx * west + py * north + my * south + pz * up + mz * down


def mix(centre):
    return [(viscosity - transport_rate * v, viscosity + transport_rate * v) for v in centre]


def edge_mask(sides):
    lane = iota((8, LANES), 1)
    return jnp.where(lane == 0, sides[3], 0.0) + jnp.where(lane == LANES - 1, sides[2], 0.0)


def sweep(source, low_row, high_row, store, tiles, after=None):
    layers, rows, wide = source.shape[1:]
    count = wide // LANES
    sub, lane = iota((8, LANES), 0), iota((8, LANES), 1)
    first_sub, last_sub, first_lane, last_lane = sub == 0, sub == 7, lane == 0, lane == LANES - 1

    @pl.loop(0, layers, step=2)
    def _(even):
        for z, up, down in (
            (even, even + 1, jnp.where(even == 0, layers - 1, even - 1)),
            (even + 1, jnp.where(even == layers - 2, 0, even + 2), even),
        ):
            below = [low_row(c, z) for c in range(3)]
            above = [high_row(c, z) for c in range(3)]
            for x in range(0, rows, 8):
                for t in range(tiles):
                    at = slice(t * LANES, (t + 1) * LANES)
                    centre = [source[c, z, x : x + 8, at] for c in range(3)]
                    weights = mix(centre)
                    for c in range(3):
                        v = centre[c]
                        ahead = source[c, z, x + 8 : x + 16, at] if x + 8 < rows else above[c][:, at]
                        behind = source[c, z, x - 8 : x, at] if x > 0 else below[c][:, at]
                        right = (t + 1) % count * LANES
                        left = (t - 1) % count * LANES
                        right = source[c, z, x : x + 8, right : right + LANES]
                        left = source[c, z, x : x + 8, left : left + LANES]
                        new = update(
                            centre, weights, c,
                            pltpu.roll(jnp.where(first_sub, ahead, v), 7, axis=0),
                            pltpu.roll(jnp.where(last_sub, behind, v), 1, axis=0),
                            pltpu.roll(jnp.where(first_lane, right, v), LANES - 1, axis=1),
                            pltpu.roll(jnp.where(last_lane, left, v), 1, axis=1),
                            source[c, up, x : x + 8, at],
                            source[c, down, x : x + 8, at],
                        )
                        store(c, z, x, at, new)
        if after is not None:
            after(even + 1)


def first_kernel(sides, velocity, edges, received, u1, u0, sems):
    layers, rows, wide = u0.shape[1:]
    patch = wide - LANES
    part = 8
    slots = received.shape[0]

    def load(step):
        at = pl.ds(step * part, part)
        return pltpu.make_async_copy(velocity.at[:, at], u0.at[:, at, :, pl.ds(0, patch)], sems.at[step])

    for step in range(layers // part):
        load(step).start()
    arrived = Arrived(received, patch)

    @pl.loop(0, layers // part)
    def _(step):
        at = pl.ds(step * part, part)
        chosen = arrived.choose(iota((part * rows, slots), 0) + step * (part * rows))
        load(step).wait()
        for c in range(3):
            main, edge = arrived.force(chosen, c)
            u0[c, at, :, :patch] += main.reshape(part, rows, patch)
            u0[c, at, :, patch:] = edges[c, at] + edge.reshape(part, rows, LANES)

    mask = edge_mask(sides)

    def store(c, z, x, at, new):
        u1[c, z, x : x + 8, at] = new * mask if at.start == patch else new

    nothing = jnp.zeros((1, wide), F32)
    sweep(u0, lambda c, z: nothing, lambda c, z: nothing, store, wide // LANES)


def last_kernel(sides, u1_in, rim, below_x, above_x, received, fluid_hbm, replies, u1, mid, fluid, sems):
    layers, rows, wide = u1.shape[1:]
    patch = wide - LANES
    slots = received.shape[0]
    mask = edge_mask(sides)[0:1]

    for side in range(2):
        halo, row = (below_x, 0) if side == 0 else (above_x, rows - 1)
        near = 1 - side
        centre = [halo[c, near].astype(F32) for c in range(3)]
        weights = mix(centre)
        slope = transport_rate if side == 0 else -transport_rate
        own = viscosity + slope * rim[side, 0]
        for c in range(3):
            outer = halo[c, side].astype(F32)
            inside = rim[side, c]
            east, west = (inside, outer) if side == 0 else (outer, inside)
            v = centre[c]
            new = update(
                centre, weights, c, east, west,
                pltpu.roll(v, wide - 1, axis=1), pltpu.roll(v, 1, axis=1),
                pltpu.roll(v, layers - 1, axis=0), pltpu.roll(v, 1, axis=0),
            ) * sides[side]
            mid[side, c, :, :patch] = new[:, :patch]
            mid[side, c, :, patch:] = new[:, patch:] * mask
            term = own * v
            tail = term[:, patch:] * mask
            for z in range(layers):
                u1[c, z, row : row + 1, :patch] += term[z : z + 1, :patch]
                u1[c, z, row : row + 1, patch:] += tail[z : z + 1]

    part = 8

    def write(step):
        at = pl.ds(pl.multiple_of(step * part * rows, part * rows), part * rows)
        return pltpu.make_async_copy(fluid.at[:, at], fluid_hbm.at[:, at], sems.at[step])

    def after(z):
        @pl.when(lax.rem(z, part) == part - 1)
        def _():
            write(z // part).start()

    def store(c, z, x, at, new):
        fluid[c, pl.ds(pl.multiple_of(z * rows + x, 8), 8), at] = new

    sweep(
        u1,
        lambda c, z: mid[0, c, pl.ds(z, 1), :patch],
        lambda c, z: mid[1, c, pl.ds(z, 1), :patch],
        store,
        patch // LANES,
        after,
    )

    heads = received[:, 3 * patch :].astype(F32)
    slot = (heads[:, 0:1] * 32.0 + heads[:, 1:2] - 1.0).astype(jnp.int32)
    chunk = 256
    for c in range(3):
        total = jnp.zeros((slots, patch), F32)
        for first in range(0, layers * rows, chunk):
            pick = (iota((slots, chunk), 1) + first == slot).astype(F32).astype(BF16)
            total += dot(pick, fluid[c, first : first + chunk, :].astype(BF16))
        replies[:, c * patch : (c + 1) * patch] = total.astype(BF16)
    for step in range(layers // part):
        write(step).wait()


def gather_kernel(pts, dest, returned, dw_hbm, out, dw, picked, moved, sems):
    entries, slots = dest.shape[0], returned.shape[0]
    blocks, patch, points = dw.shape[0], dw.shape[2], pts.shape[2]
    inter = entries // blocks
    for b in range(blocks):
        pltpu.make_async_copy(dw_hbm.at[b], dw.at[b], sems.at[b]).start()
    to = dest[:, 0:1].astype(jnp.int32)
    pick = (iota((entries, slots), 1) == to).astype(F32).astype(BF16)
    for c in range(3):
        picked[c] = dot(pick, returned[:, c * patch : (c + 1) * patch])
    k_of_lane = lax.rem(iota((points, LANES), 1), inter)

    @pl.loop(0, blocks)
    def _(b):
        at = pl.ds(pl.multiple_of(b * inter, inter), inter)
        parts = [picked[c, at, :] for c in range(3)]
        parts.append(jnp.zeros((LANES - 3 * inter, patch), F32))
        cells = jnp.concatenate(parts, axis=0).astype(BF16)
        pltpu.make_async_copy(dw_hbm.at[b], dw.at[b], sems.at[b]).wait()
        every = lax.dot_general(dw[b], cells, (((1,), (1,)), ((), ())), preferred_element_type=F32)
        folded = jnp.zeros((points, LANES), F32)
        for k in range(inter):
            folded += jnp.where(k_of_lane == k, every[k * points : (k + 1) * points], 0.0)
        turned = jnp.transpose(folded)
        for c in range(3):
            moved[c, pl.ds(b, 1), :] = jnp.sum(turned[c * inter : (c + 1) * inter], axis=0, keepdims=True)

    for c in range(3):
        out[c] = pts[c] + fiber_step * moved[c]


def in_hbm(x):
    return pltpu.with_memory_space_constraint(x, pltpu.HBM)


def params(limit):
    return pltpu.CompilerParams(vmem_limit_bytes=limit << 20)


def cost(flops, size):
    return pl.CostEstimate(flops=flops, bytes_accessed=size << 20, transcendentals=0)


SMEM = pl.BlockSpec(memory_space=pltpu.SMEM)
VMEM = pl.BlockSpec(memory_space=pltpu.VMEM)
HBM = pl.BlockSpec(memory_space=pltpu.HBM)


def run_spread(gy_size, slots, pts, stiffness, links, owners, patch_slots, dw):
    blocks, points = links.shape
    inter, patch = owners.shape[1], dw.shape[2]
    entries = blocks * inter
    return pl.pallas_call(
        functools.partial(spread_kernel, gy_size, slots),
        in_specs=[HBM] * 6,
        out_specs=[VMEM, VMEM],
        out_shape=[
            jax.ShapeDtypeStruct((slots, 3 * patch + LANES), BF16),
            jax.ShapeDtypeStruct((entries, LANES), F32),
        ],
        scratch_shapes=[
            pltpu.VMEM(dw.shape, BF16),
            pltpu.VMEM((3, blocks, points), F32),
            pltpu.VMEM((3, entries, patch), F32),
            pltpu.VMEM((3, slots, entries), BF16),
            pltpu.VMEM((3, blocks, points), F32),
            pltpu.SMEM((blocks,), F32),
            pltpu.VMEM((blocks, points), jnp.int32),
            pltpu.VMEM((blocks, inter), jnp.int32),
            pltpu.VMEM((blocks, inter), jnp.int32),
            pltpu.SemaphoreType.DMA((blocks + 5,)),
        ],
        compiler_params=params(24),
        cost_estimate=cost(10**9, 9),
        name="spread",
    )(*[in_hbm(x) for x in (pts, stiffness, links, owners, patch_slots, dw)])


def run_rim(layer_rows, layers, rim_velocity, rim_edge, received):
    patch = rim_velocity.shape[2]
    wide = patch + LANES
    side = (3, 2, layers, wide)
    return pl.pallas_call(
        functools.partial(rim_kernel, layer_rows),
        in_specs=[VMEM] * 3,
        out_specs=[VMEM] * 3,
        out_shape=[
            jax.ShapeDtypeStruct(side, BF16),
            jax.ShapeDtypeStruct(side, BF16),
            jax.ShapeDtypeStruct((2, 3, layers, wide), F32),
        ],
        compiler_params=params(24),
        cost_estimate=cost(10**8, 3),
        name="rim",
    )(rim_velocity, rim_edge, received)


def run_first(sides, velocity, edge, received):
    layers, rows, patch = velocity.shape[1:]
    block = (3, layers, rows, patch + LANES)
    return pl.pallas_call(
        first_kernel,
        in_specs=[SMEM, HBM, VMEM, VMEM],
        out_specs=VMEM,
        out_shape=jax.ShapeDtypeStruct(block, F32),
        scratch_shapes=[pltpu.VMEM(block, F32), pltpu.SemaphoreType.DMA((layers // 8,))],
        compiler_params=params(24),
        cost_estimate=cost(2 * 10**9, 24),
        name="sweep_first",
    )(sides, in_hbm(velocity), edge, received)


def run_last(sides, u1, rim, below_x, above_x, received):
    layers, rows, wide = u1.shape[1:]
    patch, slots = wide - LANES, received.shape[0]
    return pl.pallas_call(
        last_kernel,
        in_specs=[SMEM] + [VMEM] * 5,
        out_specs=[HBM, VMEM, VMEM],
        out_shape=[
            jax.ShapeDtypeStruct((3, layers * rows, patch), F32),
            jax.ShapeDtypeStruct((slots, 3 * patch), BF16),
            jax.ShapeDtypeStruct(u1.shape, F32),
        ],
        scratch_shapes=[
            pltpu.VMEM((2, 3, layers, wide), F32),
            pltpu.VMEM((3, layers * rows, patch), F32),
            pltpu.SemaphoreType.DMA((layers // 8,)),
        ],
        input_output_aliases={1: 2},
        compiler_params=params(24),
        cost_estimate=cost(2 * 10**9, 16),
        name="sweep_last",
    )(sides, u1, rim, below_x, above_x, received)[:2]


def run_gather(pts, dest, returned, dw):
    blocks, patch = dw.shape[0], dw.shape[2]
    return pl.pallas_call(
        gather_kernel,
        in_specs=[VMEM] * 3 + [HBM],
        out_specs=VMEM,
        out_shape=jax.ShapeDtypeStruct(pts.shape, F32),
        scratch_shapes=[
            pltpu.VMEM(dw.shape, BF16),
            pltpu.VMEM((3, dest.shape[0], patch), F32),
            pltpu.VMEM(pts.shape, F32),
            pltpu.SemaphoreType.DMA((blocks,)),
        ],
        compiler_params=params(24),
        cost_estimate=cost(10**9, 9),
        name="interp",
    )(pts, dest, returned, in_hbm(dw))


def shards(velocity, fiber_points, stiffness, links, delta_weights, owners, patch_slots):
    blocks, inter, points, patch = delta_weights.shape
    layers, rows, columns = velocity.shape[1:]
    gx_size, gy_size = lax.axis_size("gx"), lax.axis_size("gy")
    devices = gx_size * gy_size
    slots, cells = devices * 2, layers * rows
    pts = fiber_points.transpose(1, 0, 2)
    dw = delta_weights.reshape(blocks, inter * points, patch)
    outgoing, dest = run_spread(
        gy_size, slots, pts, stiffness, links, owners.reshape(blocks, inter), patch_slots, dw
    )

    def exchange(rows_out):
        size = rows_out.shape[1]
        return lax.all_to_all(
            rows_out.reshape(devices, 2, size), ("gx", "gy"), split_axis=0, concat_axis=0, tiled=True
        ).reshape(slots, size)

    received = exchange(outgoing)

    ahead = [(i + 1, i) for i in range(gy_size - 1)]
    behind = [(i, i + 1) for i in range(gy_size - 1)]
    flat = velocity.reshape(3, cells, columns)
    first = lax.ppermute(flat[:, :, :2].transpose(0, 2, 1), "gy", ahead)
    last = lax.ppermute(flat[:, :, columns - 2 :].transpose(0, 2, 1), "gy", behind)
    edge = jnp.concatenate(
        [first.transpose(0, 2, 1), jnp.zeros((3, cells, LANES - 4), F32), last.transpose(0, 2, 1)], axis=2
    ).reshape(3, layers, rows, LANES)
    lines = (0, 1, rows - 2, rows - 1)
    rim_velocity = jnp.stack([velocity[:, :, x, :] for x in lines], axis=1).reshape(3, 4 * layers, patch)
    rim_edge = jnp.stack([edge[:, :, x, :] for x in lines], axis=1).reshape(3, 4 * layers, LANES)
    low_rows, high_rows, rim = run_rim(rows, layers, rim_velocity, rim_edge, received)

    up = [(i, i + 1) for i in range(gx_size - 1)]
    below_x = lax.ppermute(high_rows, "gx", up)
    above_x = lax.ppermute(low_rows, "gx", [(b, a) for a, b in up])
    gx, gy = lax.axis_index("gx"), lax.axis_index("gy")
    sides = jnp.stack([gx > 0, gx < gx_size - 1, gy > 0, gy < gy_size - 1]).astype(F32)
    u1 = run_first(sides, velocity, edge, received)
    fluid, replies = run_last(sides, u1, rim, below_x, above_x, received)
    moved = run_gather(pts, dest, exchange(replies), dw)
    return fluid.reshape(3, layers, rows, columns), moved.transpose(1, 0, 2)


def solution(mesh):
    placed = (
        P(None, None, "gx", "gy"),
        P(("gx", "gy"), None, None),
        P(("gx", "gy")),
        P(("gx", "gy"), None),
        P(("gx", "gy"), None, None, None),
        P(("gx", "gy"), None, None),
        P(("gx", "gy"), None),
    )
    return jax.shard_map(
        shards,
        mesh=mesh,
        in_specs=placed,
        out_specs=(P(None, None, "gx", "gy"), P(("gx", "gy"), None, None)),
        check_vma=False,
    )
```

time: 106 us -> 97 us (0.915)
  Pallas kernels: 34.2 us -> 28.2 us
  local copies, waits for them, and re-layouts: 17.8 us -> 15.2 us
    pallas_call x5, Pallas kernels: 34.2 us -> 28.2 us  [the longest x1 10.4 us: run_first(): pl.pallas_call(first_kernel, in_specs=[SMEM, HBM, VMEM, VMEM], out_specs=...]
    reshape x2, local copies, waits for them, and re-layouts: 3.26 us -> 1.52 us  [exchange(): rows_out.reshape(devices, 2, size)]
  transfers between devices with their start and end apart: 5 -> 5, of which waited for: 0 -> 0; matrix products, arithmetic and copies ran while one was open for 13% -> 15% of each run, Pallas kernels for 11% -> 11%
where the time goes in v4:
time: 97 us; the launch traced here: 96.7 us
  Pallas kernels  28.2 us (29%)
  blocking collectives  27.3 us (28%)
  starting transfers between devices  21.9 us (23%)
  local copies, waits for them, and re-layouts  15.2 us (16%)
  other arithmetic  3.2 us (3%)
    all_to_all x1, blocking collectives, exchange(): lax.all_to_all(rows_out.reshape(devices, 2, size), ('gx', 'gy'), split_ax...  27.3 us
    all_to_all x1, starting transfers between devices, exchange(): lax.all_to_all(rows_out.reshape(devices, 2, size), ('gx', 'gy'), split_ax...  11.9 us
    pallas_call x1, Pallas kernels, run_first(): pl.pallas_call(first_kernel, in_specs=[SMEM, HBM, VMEM, VMEM], out_specs=...  10.4 us
    pallas_call x1, Pallas kernels, run_last(): pl.pallas_call(last_kernel, in_specs=[SMEM] + [VMEM] * 5, out_specs=[HBM,...  7.4 us
    pallas_call x1, Pallas kernels, run_gather(): pl.pallas_call(gather_kernel, in_specs=[VMEM] * 3 + [HBM], out_specs=VMEM...  5.72 us
    pallas_call x1, Pallas kernels, run_spread(): pl.pallas_call(functools.partial(spread_kernel, gy_size, slots), in_specs...  4.28 us
    another operation x2, local copies, waits for them, and re-layouts, shards(): jnp.stack([velocity[:, :, x, :] for x in lines], axis=1)  4.07 us
    ppermute x1, starting transfers between devices, shards(): lax.ppermute(flat[:, :, columns - 2:].transpose(0, 2, 1), 'gy', behind)  3.66 us
  transfers between devices with their start and end apart: 5, of which 0 were waited for; matrix products, arithmetic and copies ran while one was open for 15% of the time, Pallas kernels for 11%

profile of v4, /device:TPU:1, one launch (start us, length us, event | category | flops | bytes accessed | tf_op | source)
XLA Modules:
  0.0 96.7 jit_solution(11188920468705439323)
XLA Ops:
  0.6 4.3 %spread.1 = (bf16[256,1664]{1,0:T(8,128)(2,1)S(1)}, f32[64,128]{1,0:T(8,128)S(1)}) custom-call(f32[3,8,128]{2,1,0:T(8,128)} %bitcast.41, f32[8]{0:T(128)} %stiff_hbm.1, s32[8,128]{1,0:T(8,128)} %links_hbm.1, s32[8,8]{1,0:T(8,128)} %bitcast.53, s32[8,8]{1,0:T(8,128)} %patch_slots_hbm.1, bf16[8,1024,512]{2,1,0:T(8,128)(2,1)} %bitcast.43), custom_call_target="tpu_custom_call" | custom-call | flops 1000000000 | bytes 9437184 | tf_op jit(solution)/shard_map/spread/pallas_call | solution.py:366
  4.9 1.2 %reshape.41 = bf16[128,2,1664]{2,1,0:T(2,128)(2,1)} reshape(bf16[256,1664]{1,0:T(8,128)(2,1)S(1)} %get-tuple-element.9) | data formatting | bytes 1703936 | tf_op jit(solution)/shard_map/reshape | solution.py:484
  6.1 11.9 %all-to-all-start = ((bf16[128,2,1664]{2,1,0:T(2,128)(2,1)}), bf16[128,2,1664]{2,1,0:T(2,128)(2,1)}, u32[]{:S(2)}, u32[]{:S(2)}) async-start(bf16[128,2,1664]{2,1,0:T(2,128)(2,1)} %reshape.41), calls=%async_computation | async-start | bytes 1703936 | tf_op jit(solution)/shard_map/all_to_all | solution.py:483
  18.1 2.4 %slice_bitcast_fusion.1 = (f32[3,2,1024]{1,2,0:T(8,128)S(1)}, f32[3,2,1024]{1,2,0:T(8,128)S(1)}) fusion(f32[3,1024,512]{2,1,0:T(8,128)} %bitcast.45), kind=kLoop, calls=%fused_computation.1 | loop fusion | bytes 98304 | tf_op jit(solution)/shard_map/transpose | solution.py:492
  20.5 0.5 copy.24
  20.9 3.7 %collective-permute-start.1 = (f32[3,2,1024]{2,1,0:T(2,128)S(1)}, f32[3,2,1024]{2,1,0:T(2,128)S(1)}, u32[]{:S(2)}, u32[]{:S(2)}) collective-permute-start(f32[3,2,1024]{2,1,0:T(2,128)S(1)} %copy.24), channel_id=1, source_target_pairs={{0,1},{1,2},{2,3},{3,4},{4,5},{5,6},{6,7},{8,9},{9,10},{10,11},{11... | collective-permute-start | bytes 73736 | tf_op jit(solution)/shard_map/ppermute | solution.py:493
  24.6 0.5 copy.23
  25.1 1.9 %collective-permute-start = (f32[3,2,1024]{2,1,0:T(2,128)S(1)}, f32[3,2,1024]{2,1,0:T(2,128)S(1)}, u32[]{:S(2)}, u32[]{:S(2)}) collective-permute-start(f32[3,2,1024]{2,1,0:T(2,128)S(1)} %copy.23), channel_id=1, source_target_pairs={{1,0},{2,1},{3,2},{4,3},{5,4},{6,5},{7,6},{9,8},{10,9},{11,10},{12... | collective-permute-start | bytes 73736 | tf_op jit(solution)/shard_map/ppermute | solution.py:492
  27.0 3.8 %slice_bitcast_fusion.5 = (f32[3,1,32,512]{3,1,2,0:T(1,128)S(1)}, f32[3,1,32,512]{3,1,2,0:T(1,128)S(1)}, f32[3,1,32,512]{3,1,2,0:T(1,128)S(1)}, f32[3,1,32,512]{3,1,2,0:T(1,128)S(1)}) fusion(f32[3,32,32,512]{3,2,1,0:T(8,128)} %velocity.1), kind=kLoop, calls=%fused_computation.8 | loop fusion | bytes 1572864 | tf_op jit(solution)/shard_map/stack;squeeze | solution.py:498
  30.8 0.7 pad_maximum_fusion.1
  31.6 0.3 copy.27
  31.9 1.7 %copy.25 = f32[3,1024,2]{2,1,0:T(8,128)} copy(f32[3,1024,2]{1,2,0:T(2,128)S(1)} %bitcast.51) | data formatting | bytes 49152 | tf_op jit(solution)/shard_map/transpose | solution.py:495
  33.6 1.7 %copy.26 = f32[3,1024,2]{2,1,0:T(8,128)} copy(f32[3,1024,2]{1,2,0:T(2,128)S(1)} %bitcast.50) | data formatting | bytes 49152 | tf_op jit(solution)/shard_map/transpose | solution.py:495
  35.3 2.4 %pad_maximum_fusion = f32[3,1024,128]{2,1,0:T(8,128)S(1)} fusion(f32[3,1024,2]{2,1,0:T(8,128)} %copy.26, f32[3,1024,2]{2,1,0:T(8,128)} %copy.25, f32[128]{0:T(128)S(1)} %pad.9.clone), kind=kLoop, calls=%fused_computation.2 | loop fusion | flops 786432 | bytes 1622528 | tf_op jit(solution)/shard_map/concatenate | solution.py:494
  37.8 2.4 %reshape.42.received = bf16[256,1664]{1,0:T(8,128)(2,1)S(1)} reshape(bf16[128,2,1664]{2,1,0:T(2,128)(2,1)} %all-to-all-done) | data formatting | bytes 1703936 | tf_op jit(solution)/shard_map/reshape | solution.py:485
  40.2 0.5 rim.1
  40.7 3.1 %collective-permute-start.2 = (bf16[3,2,32,640]{3,2,1,0:T(8,128)(2,1)S(1)}, bf16[3,2,32,640]{3,2,1,0:T(8,128)(2,1)S(1)}, u32[]{:S(2)}, u32[]{:S(2)}) collective-permute-start(bf16[3,2,32,640]{3,2,1,0:T(8,128)(2,1)S(1)} %get-tuple-element.11), channel_id=1, source_target_pairs={{0,8},{8,16},{16,24},{24,32},{32,40},{40,48},{48,56},{56,64},{64,7... | collective-permute-start | bytes 737288 | tf_op jit(solution)/shard_map/ppermute | solution.py:503
  43.8 1.3 %collective-permute-start.3 = (bf16[3,2,32,640]{3,2,1,0:T(8,128)(2,1)S(1)}, bf16[3,2,32,640]{3,2,1,0:T(8,128)(2,1)S(1)}, u32[]{:S(2)}, u32[]{:S(2)}) collective-permute-start(bf16[3,2,32,640]{3,2,1,0:T(8,128)(2,1)S(1)} %get-tuple-element.12), channel_id=1, source_target_pairs={{8,0},{16,8},{24,16},{32,24},{40,32},{48,40},{56,48},{64,56},{72,6... | collective-permute-start | bytes 737288 | tf_op jit(solution)/shard_map/ppermute | solution.py:504
  45.2 10.4 %sweep_first.1.u1_in = f32[3,32,32,640]{3,2,1,0:T(8,128)S(1)} custom-call(f32[4]{0:T(128)S(1)} %add_convert_fusion.sides, f32[3,32,32,512]{3,2,1,0:T(8,128)} %velocity.1, f32[3,32,32,128]{3,2,1,0:T(8,128)S(1)} %bitcast.38, bf16[256,1664]{1,0:T(8,128)(2,1)S(1)} %reshape.42.received), custom_call_target="tpu_custom_call" | custom-call | flops 2000000000 | bytes 25165824 | tf_op jit(solution)/shard_map/sweep_first/pallas_call | solution.py:414
  55.6 7.4 %sweep_last.1 = (f32[3,1024,512]{2,1,0:T(8,128)}, bf16[256,1536]{1,0:T(8,128)(2,1)S(1)}, f32[3,32,32,640]{3,2,1,0:T(8,128)S(1)}) custom-call(f32[4]{0:T(128)S(1)} %add_convert_fusion.sides, f32[3,32,32,640]{3,2,1,0:T(8,128)S(1)} %sweep_first.1.u1_in, f32[2,3,32,640]{3,2,1,0:T(8,128)S(1)} %get-tuple-element.10.rim, ...), custom_call_target="tpu_custom_call", output_to_operand_aliasing={{2}: (1, {})} | custom-call | flops 2000000000 | bytes 16777216 | tf_op jit(solution)/shard_map/sweep_last/pallas_call | solution.py:429
  63.0 0.3 reshape.46
  63.3 27.3 %all_to_all.10 = bf16[128,2,1536]{2,1,0:T(2,128)(2,1)S(1)} all-to-all(bf16[128,2,1536]{2,1,0:T(2,128)(2,1)S(1)} %reshape.46), channel_id=1, replica_groups=mesh['gx'=16,'gy'=8] {'gx','gy'}, dimensions={0} | all-to-all | bytes 1572864 | tf_op jit(solution)/shard_map/all_to_all | solution.py:483
  90.6 0.3 reshape.47.returned
  90.9 5.7 %interp.1 = f32[3,8,128]{2,1,0:T(8,128)} custom-call(f32[3,8,128]{2,1,0:T(8,128)S(1)} %bitcast.42, f32[64,128]{1,0:T(8,128)S(1)} %get-tuple-element.14.dest, bf16[256,1536]{1,0:T(8,128)(2,1)S(1)} %reshape.47.returned, bf16[8,1024,512]{2,1,0:T(8,128)(2,1)} %bitcast.44), custom_call_target="tpu_custom_call" | custom-call | flops 1000000000 | bytes 9437184 | tf_op jit(solution)/shard_map/interp/pallas_call | solution.py:452
  (13 shorter events, 0.4 us)
Async XLA Ops:
  6.1 31.7 %all-to-all-start = ((bf16[128,2,1664]{2,1,0:T(2,128)(2,1)}), bf16[128,2,1664]{2,1,0:T(2,128)(2,1)}, u32[]{:S(2)}, u32[]{:S(2)}) async-start(bf16[128,2,1664]{2,1,0:T(2,128)(2,1)} %reshape.41), calls=%async_computation | async-start | bytes 1703936 | tf_op jit(solution)/shard_map/all_to_all | solution.py:483
  20.9 12.7 %collective-permute-start.1 = (f32[3,2,1024]{2,1,0:T(2,128)S(1)}, f32[3,2,1024]{2,1,0:T(2,128)S(1)}, u32[]{:S(2)}, u32[]{:S(2)}) collective-permute-start(f32[3,2,1024]{2,1,0:T(2,128)S(1)} %copy.24), channel_id=1, source_target_pairs={{0,1},{1,2},{2,3},{3,4},{4,5},{5,6},{6,7},{8,9},{9,10},{10,11},{11... | collective-permute-start | bytes 73736 | tf_op jit(solution)/shard_map/ppermute | solution.py:493
  25.1 6.9 %collective-permute-start = (f32[3,2,1024]{2,1,0:T(2,128)S(1)}, f32[3,2,1024]{2,1,0:T(2,128)S(1)}, u32[]{:S(2)}, u32[]{:S(2)}) collective-permute-start(f32[3,2,1024]{2,1,0:T(2,128)S(1)} %copy.23), channel_id=1, source_target_pairs={{1,0},{2,1},{3,2},{4,3},{5,4},{6,5},{7,6},{9,8},{10,9},{11,10},{12... | collective-permute-start | bytes 73736 | tf_op jit(solution)/shard_map/ppermute | solution.py:492
  40.7 14.9 %collective-permute-start.2 = (bf16[3,2,32,640]{3,2,1,0:T(8,128)(2,1)S(1)}, bf16[3,2,32,640]{3,2,1,0:T(8,128)(2,1)S(1)}, u32[]{:S(2)}, u32[]{:S(2)}) collective-permute-start(bf16[3,2,32,640]{3,2,1,0:T(8,128)(2,1)S(1)} %get-tuple-element.11), channel_id=1, source_target_pairs={{0,8},{8,16},{16,24},{24,32},{32,40},{40,48},{48,56},{56,64},{64,7... | collective-permute-start | bytes 737288 | tf_op jit(solution)/shard_map/ppermute | solution.py:503
  43.8 11.8 %collective-permute-start.3 = (bf16[3,2,32,640]{3,2,1,0:T(8,128)(2,1)S(1)}, bf16[3,2,32,640]{3,2,1,0:T(8,128)(2,1)S(1)}, u32[]{:S(2)}, u32[]{:S(2)}) collective-permute-start(bf16[3,2,32,640]{3,2,1,0:T(8,128)(2,1)S(1)} %get-tuple-element.12), channel_id=1, source_target_pairs={{8,0},{16,8},{24,16},{32,24},{40,32},{48,40},{56,48},{64,56},{72,6... | collective-permute-start | bytes 737288 | tf_op jit(solution)/shard_map/ppermute | solution.py:504
  63.3 27.6 %copy-start = (f32[8,3,128]{2,0,1:T(8,128)S(1)}, f32[8,3,128]{2,0,1:T(8,128)}, u32[]{:S(2)}) copy-start(f32[8,3,128]{2,0,1:T(8,128)} %param.8) | copy-start | bytes 36868

commit v5 on v4

--- a/solution.py
+++ b/solution.py
@@ -151,8 +151,9 @@
             to[c, j % 2, :, :patch] = main[at].astype(BF16)
             to[c, j % 2, :, patch:] = edge[at].astype(BF16)
         for side, at in ((0, slice(0, layers)), (1, slice(3 * layers, 4 * layers))):
-            rim[side, c, :, :patch] = main[at]
-            rim[side, c, :, patch:] = edge[at]
+            for t in range(patch // LANES):
+                rim[side, c, t] = main[at, t * LANES : (t + 1) * LANES]
+            rim[side, c, patch // LANES] = edge[at]
 
 
 def update(centre, weights, c, east, west, north, south, up, down):
@@ -165,149 +166,162 @@
     return [(viscosity - transport_rate * v, viscosity + transport_rate * v) for v in centre]
 
 
+def beside():
+    flags = []
+    for axis in ("gx", "gy"):
+        at, size = lax.axis_index(axis), lax.axis_size(axis)
+        flags += [jnp.where(at > 0, 1.0, 0.0).astype(F32), jnp.where(at < size - 1, 1.0, 0.0).astype(F32)]
+    return flags
+
+
 def edge_mask(sides):
     lane = iota((8, LANES), 1)
     return jnp.where(lane == 0, sides[3], 0.0) + jnp.where(lane == LANES - 1, sides[2], 0.0)
 
 
-def sweep(source, low_row, high_row, store, tiles, after=None):
-    layers, rows, wide = source.shape[1:]
-    count = wide // LANES
-    sub, lane = iota((8, LANES), 0), iota((8, LANES), 1)
-    first_sub, last_sub, first_lane, last_lane = sub == 0, sub == 7, lane == 0, lane == LANES - 1
-
-    @pl.loop(0, layers, step=2)
-    def _(even):
-        for z, up, down in (
-            (even, even + 1, jnp.where(even == 0, layers - 1, even - 1)),
-            (even + 1, jnp.where(even == layers - 2, 0, even + 2), even),
-        ):
-            below = [low_row(c, z) for c in range(3)]
-            above = [high_row(c, z) for c in range(3)]
-            for x in range(0, rows, 8):
-                for t in range(tiles):
-                    at = slice(t * LANES, (t + 1) * LANES)
-                    centre = [source[c, z, x : x + 8, at] for c in range(3)]
-                    weights = mix(centre)
-                    for c in range(3):
-                        v = centre[c]
-                        ahead = source[c, z, x + 8 : x + 16, at] if x + 8 < rows else above[c][:, at]
-                        behind = source[c, z, x - 8 : x, at] if x > 0 else below[c][:, at]
-                        right = (t + 1) % count * LANES
-                        left = (t - 1) % count * LANES
-                        right = source[c, z, x : x + 8, right : right + LANES]
-                        left = source[c, z, x : x + 8, left : left + LANES]
-                        new = update(
-                            centre, weights, c,
-                            pltpu.roll(jnp.where(first_sub, ahead, v), 7, axis=0),
-                            pltpu.roll(jnp.where(last_sub, behind, v), 1, axis=0),
-                            pltpu.roll(jnp.where(first_lane, right, v), LANES - 1, axis=1),
-                            pltpu.roll(jnp.where(last_lane, left, v), 1, axis=1),
-                            source[c, up, x : x + 8, at],
-                            source[c, down, x : x + 8, at],
-                        )
-                        store(c, z, x, at, new)
-        if after is not None:
-            after(even + 1)
-
-
-def first_kernel(sides, velocity, edges, received, u1, u0, sems):
-    layers, rows, wide = u0.shape[1:]
-    patch = wide - LANES
-    part = 8
-    slots = received.shape[0]
-
-    def load(step):
-        at = pl.ds(step * part, part)
-        return pltpu.make_async_copy(velocity.at[:, at], u0.at[:, at, :, pl.ds(0, patch)], sems.at[step])
-
-    for step in range(layers // part):
-        load(step).start()
-    arrived = Arrived(received, patch)
-
-    @pl.loop(0, layers // part)
+def rows_at(z, x, rows):
+    return pl.ds(pl.multiple_of(z * rows + x, 8), 8)
+
+
+def shifted(v, ahead, behind, axis):
+    size = v.shape[axis]
+    at = iota(v.shape, axis)
+    return (
+        pltpu.roll(jnp.where(at == 0, ahead, v), size - 1, axis=axis),
+        pltpu.roll(jnp.where(at == size - 1, behind, v), 1, axis=axis),
+    )
+
+
+def sweep_pair(source, layers, z, low_row, high_row, store, tiles):
+    count, rows = source.shape[1], source.shape[2] // layers
+    z1 = lax.rem(z + 1, layers)
+    for z, up, down in ((z, z1, lax.rem(z + layers - 1, layers)), (z1, lax.rem(z + 2, layers), z)):
+        for x in range(0, rows, 8):
+            for t in range(tiles):
+                here = rows_at(z, x, rows)
+                centre = [source[c, t, here, :] for c in range(3)]
+                weights = mix(centre)
+                for c in range(3):
+                    v = centre[c]
+                    ahead = source[c, t, rows_at(z, x + 8, rows), :] if x + 8 < rows else high_row(c, t, z)
+                    behind = source[c, t, rows_at(z, x - 8, rows), :] if x > 0 else low_row(c, t, z)
+                    east, west = shifted(v, ahead, behind, 0)
+                    north, south = shifted(v, source[c, (t + 1) % count, here, :], source[c, (t - 1) % count, here, :], 1)
+                    above, below = source[c, t, rows_at(up, x, rows), :], source[c, t, rows_at(down, x, rows), :]
+                    store(c, t, here, update(centre, weights, c, east, west, north, south, above, below))
+
+
+def first_kernel(layers, velocity, edges, received, u1, u0, sems):
+    count, cells = u0.shape[1:3]
+    rows, tiles = cells // layers, count - 1
+    depth, slots = 8, received.shape[0]
+    part, steps = depth * rows, layers // depth
+
+    def load(step, t):
+        at = pl.ds(pl.multiple_of(step * part, part), part)
+        return pltpu.make_async_copy(
+            velocity.at[:, at, pl.ds(t * LANES, LANES)], u0.at[:, t, at], sems.at[step * tiles + t]
+        )
+
+    for step in range(steps):
+        for t in range(tiles):
+            load(step, t).start()
+    arrived = Arrived(received, tiles * LANES)
+    mask = edge_mask(beside())
+
+    def store(c, t, here, new):
+        u1[c, t, here, :] = new * mask if t == tiles else new
+
+    def nothing(c, t, z):
+        return 0.0
+
+    @pl.loop(0, steps)
     def _(step):
-        at = pl.ds(step * part, part)
-        chosen = arrived.choose(iota((part * rows, slots), 0) + step * (part * rows))
-        load(step).wait()
+        at = pl.ds(pl.multiple_of(step * part, part), part)
+        chosen = arrived.choose(iota((part, slots), 0) + step * part)
+        for t in range(tiles):
+            load(step, t).wait()
         for c in range(3):
             main, edge = arrived.force(chosen, c)
-            u0[c, at, :, :patch] += main.reshape(part, rows, patch)
-            u0[c, at, :, patch:] = edges[c, at] + edge.reshape(part, rows, LANES)
-
+            for t in range(tiles):
+                u0[c, t, at, :] += main[:, t * LANES : (t + 1) * LANES]
+            u0[c, tiles, at, :] = edges[c, at, :] + edge
+
+        @pl.loop(jnp.where(step == 0, 1, 0), jnp.where(step == steps - 1, depth // 2 + 1, depth // 2))
+        def _(i):
+            sweep_pair(u0, layers, step * depth - 1 + 2 * i, nothing, nothing, store, count)
+
+
+def last_kernel(layers, u1_in, rim, below_x, above_x, received, fluid_hbm, replies, u1, mid, halo, fluid, pick, sems):
+    count, cells = u1.shape[1:3]
+    rows, tiles = cells // layers, count - 1
+    patch, slots = tiles * LANES, received.shape[0]
+    sides = beside()
     mask = edge_mask(sides)
-
-    def store(c, z, x, at, new):
-        u1[c, z, x : x + 8, at] = new * mask if at.start == patch else new
-
-    nothing = jnp.zeros((1, wide), F32)
-    sweep(u0, lambda c, z: nothing, lambda c, z: nothing, store, wide // LANES)
-
-
-def last_kernel(sides, u1_in, rim, below_x, above_x, received, fluid_hbm, replies, u1, mid, fluid, sems):
-    layers, rows, wide = u1.shape[1:]
-    patch = wide - LANES
-    slots = received.shape[0]
-    mask = edge_mask(sides)[0:1]
-
-    for side in range(2):
-        halo, row = (below_x, 0) if side == 0 else (above_x, rows - 1)
-        near = 1 - side
-        centre = [halo[c, near].astype(F32) for c in range(3)]
-        weights = mix(centre)
-        slope = transport_rate if side == 0 else -transport_rate
-        own = viscosity + slope * rim[side, 0]
-        for c in range(3):
-            outer = halo[c, side].astype(F32)
-            inside = rim[side, c]
-            east, west = (inside, outer) if side == 0 else (outer, inside)
-            v = centre[c]
-            new = update(
-                centre, weights, c, east, west,
-                pltpu.roll(v, wide - 1, axis=1), pltpu.roll(v, 1, axis=1),
-                pltpu.roll(v, layers - 1, axis=0), pltpu.roll(v, 1, axis=0),
-            ) * sides[side]
-            mid[side, c, :, :patch] = new[:, :patch]
-            mid[side, c, :, patch:] = new[:, patch:] * mask
-            term = own * v
-            tail = term[:, patch:] * mask
-            for z in range(layers):
-                u1[c, z, row : row + 1, :patch] += term[z : z + 1, :patch]
-                u1[c, z, row : row + 1, patch:] += tail[z : z + 1]
-
-    part = 8
-
-    def write(step):
-        at = pl.ds(pl.multiple_of(step * part * rows, part * rows), part * rows)
-        return pltpu.make_async_copy(fluid.at[:, at], fluid_hbm.at[:, at], sems.at[step])
-
-    def after(z):
-        @pl.when(lax.rem(z, part) == part - 1)
-        def _():
-            write(z // part).start()
-
-    def store(c, z, x, at, new):
-        fluid[c, pl.ds(pl.multiple_of(z * rows + x, 8), 8), at] = new
-
-    sweep(
-        u1,
-        lambda c, z: mid[0, c, pl.ds(z, 1), :patch],
-        lambda c, z: mid[1, c, pl.ds(z, 1), :patch],
-        store,
-        patch // LANES,
-        after,
-    )
 
     heads = received[:, 3 * patch :].astype(F32)
     slot = (heads[:, 0:1] * 32.0 + heads[:, 1:2] - 1.0).astype(jnp.int32)
-    chunk = 256
+    for first in range(0, cells, 256):
+        pick[:, first : first + 256] = (iota((slots, 256), 1) + first == slot).astype(F32).astype(BF16)
+
+    for side, source in enumerate((below_x, above_x)):
+        for c in range(3):
+            for j in range(2):
+                for t in range(count):
+                    halo[side, c, j, t] = source[c, j, :, t * LANES : (t + 1) * LANES].astype(F32)
+    for side in range(2):
+        near, row = 1 - side, (rows - 1) * side
+        slope = -transport_rate if side else transport_rate
+        for t in range(count):
+            scale = sides[side] * mask if t == tiles else sides[side]
+            for g in range(0, layers, 8):
+                at = slice(g, g + 8)
+                after, before = (g + 8) % layers, (g - 8) % layers
+                centre = [halo[side, c, near, t, at, :] for c in range(3)]
+                weights = mix(centre)
+                own = viscosity + slope * rim[side, 0, t, at, :]
+                for c in range(3):
+                    v = centre[c]
+                    plane = halo.at[side, c, near]
+                    inner, outer = rim[side, c, t, at, :], halo[side, c, side, t, at, :]
+                    east, west = (outer, inner) if side else (inner, outer)
+                    north, south = shifted(v, plane[(t + 1) % count, at, :], plane[(t - 1) % count, at, :], 1)
+                    up, down = shifted(v, plane[t, after : after + 8, :], plane[t, before : before + 8, :], 0)
+                    mid[side, c, t, at, :] = scale * update(
+                        centre, weights, c, east, west, north, south, up, down
+                    )
+                    term = own * v
+                    strided = pl.ds(g * rows + row, 8, stride=rows)
+                    u1[c, t, strided, :] += term * mask if t == tiles else term
+
+    def store(c, t, here, new):
+        fluid[c, here, t * LANES : (t + 1) * LANES] = new
+
+    depth = 8
+
+    def write(step):
+        at = pl.ds(pl.multiple_of(step * depth * rows, depth * rows), depth * rows)
+        return pltpu.make_async_copy(fluid.at[:, at], fluid_hbm.at[:, at], sems.at[step])
+
+    @pl.loop(0, layers // depth)
+    def _(step):
+        @pl.loop(0, depth // 2)
+        def _(i):
+            sweep_pair(
+                u1,
+                layers,
+                step * depth + 2 * i,
+                lambda c, t, z: mid[0, c, t, pl.ds(z, 1), :],
+                lambda c, t, z: mid[1, c, t, pl.ds(z, 1), :],
+                store,
+                tiles,
+            )
+
+        write(step).start()
+
     for c in range(3):
-        total = jnp.zeros((slots, patch), F32)
-        for first in range(0, layers * rows, chunk):
-            pick = (iota((slots, chunk), 1) + first == slot).astype(F32).astype(BF16)
-            total += dot(pick, fluid[c, first : first + chunk, :].astype(BF16))
-        replies[:, c * patch : (c + 1) * patch] = total.astype(BF16)
-    for step in range(layers // part):
+        replies[:, c * patch : (c + 1) * patch] = dot(pick[...], fluid[c].astype(BF16)).astype(BF16)
+    for step in range(layers // depth):
         write(step).wait()
 
 
@@ -354,7 +368,6 @@
     return pl.CostEstimate(flops=flops, bytes_accessed=size << 20, transcendentals=0)
 
 
-SMEM = pl.BlockSpec(memory_space=pltpu.SMEM)
 VMEM = pl.BlockSpec(memory_space=pltpu.VMEM)
 HBM = pl.BlockSpec(memory_space=pltpu.HBM)
 
@@ -400,7 +413,7 @@
         out_shape=[
             jax.ShapeDtypeStruct(side, BF16),
             jax.ShapeDtypeStruct(side, BF16),
-            jax.ShapeDtypeStruct((2, 3, layers, wide), F32),
+            jax.ShapeDtypeStruct((2, 3, wide // LANES, layers, LANES), F32),
         ],
         compiler_params=params(24),
         cost_estimate=cost(10**8, 3),
@@ -408,43 +421,45 @@
     )(rim_velocity, rim_edge, received)
 
 
-def run_first(sides, velocity, edge, received):
-    layers, rows, patch = velocity.shape[1:]
-    block = (3, layers, rows, patch + LANES)
+def run_first(layers, velocity, edge, received):
+    cells, patch = velocity.shape[1:]
+    block = (3, patch // LANES + 1, cells, LANES)
     return pl.pallas_call(
-        first_kernel,
-        in_specs=[SMEM, HBM, VMEM, VMEM],
+        functools.partial(first_kernel, layers),
+        in_specs=[HBM, VMEM, VMEM],
         out_specs=VMEM,
         out_shape=jax.ShapeDtypeStruct(block, F32),
-        scratch_shapes=[pltpu.VMEM(block, F32), pltpu.SemaphoreType.DMA((layers // 8,))],
+        scratch_shapes=[pltpu.VMEM(block, F32), pltpu.SemaphoreType.DMA((layers // 8 * (patch // LANES),))],
         compiler_params=params(24),
         cost_estimate=cost(2 * 10**9, 24),
         name="sweep_first",
-    )(sides, in_hbm(velocity), edge, received)
-
-
-def run_last(sides, u1, rim, below_x, above_x, received):
-    layers, rows, wide = u1.shape[1:]
-    patch, slots = wide - LANES, received.shape[0]
+    )(in_hbm(velocity), edge, received)
+
+
+def run_last(layers, u1, rim, below_x, above_x, received):
+    count, cells = u1.shape[1:3]
+    patch, slots = (count - 1) * LANES, received.shape[0]
     return pl.pallas_call(
-        last_kernel,
-        in_specs=[SMEM] + [VMEM] * 5,
+        functools.partial(last_kernel, layers),
+        in_specs=[VMEM] * 5,
         out_specs=[HBM, VMEM, VMEM],
         out_shape=[
-            jax.ShapeDtypeStruct((3, layers * rows, patch), F32),
+            jax.ShapeDtypeStruct((3, cells, patch), F32),
             jax.ShapeDtypeStruct((slots, 3 * patch), BF16),
             jax.ShapeDtypeStruct(u1.shape, F32),
         ],
         scratch_shapes=[
-            pltpu.VMEM((2, 3, layers, wide), F32),
-            pltpu.VMEM((3, layers * rows, patch), F32),
+            pltpu.VMEM((2, 3, count, layers, LANES), F32),
+            pltpu.VMEM((2, 3, 2, count, layers, LANES), F32),
+            pltpu.VMEM((3, cells, patch), F32),
+            pltpu.VMEM((slots, cells), BF16),
             pltpu.SemaphoreType.DMA((layers // 8,)),
         ],
-        input_output_aliases={1: 2},
+        input_output_aliases={0: 2},
         compiler_params=params(24),
         cost_estimate=cost(2 * 10**9, 16),
         name="sweep_last",
-    )(sides, u1, rim, below_x, above_x, received)[:2]
+    )(u1, rim, below_x, above_x, received)[:2]
 
 
 def run_gather(pts, dest, returned, dw):
@@ -493,19 +508,18 @@
     last = lax.ppermute(flat[:, :, columns - 2 :].transpose(0, 2, 1), "gy", behind)
     edge = jnp.concatenate(
         [first.transpose(0, 2, 1), jnp.zeros((3, cells, LANES - 4), F32), last.transpose(0, 2, 1)], axis=2
-    ).reshape(3, layers, rows, LANES)
+    )
+    planes = edge.reshape(3, layers, rows, LANES)
     lines = (0, 1, rows - 2, rows - 1)
     rim_velocity = jnp.stack([velocity[:, :, x, :] for x in lines], axis=1).reshape(3, 4 * layers, patch)
-    rim_edge = jnp.stack([edge[:, :, x, :] for x in lines], axis=1).reshape(3, 4 * layers, LANES)
+    rim_edge = jnp.stack([planes[:, :, x, :] for x in lines], axis=1).reshape(3, 4 * layers, LANES)
     low_rows, high_rows, rim = run_rim(rows, layers, rim_velocity, rim_edge, received)
 
     up = [(i, i + 1) for i in range(gx_size - 1)]
     below_x = lax.ppermute(high_rows, "gx", up)
     above_x = lax.ppermute(low_rows, "gx", [(b, a) for a, b in up])
-    gx, gy = lax.axis_index("gx"), lax.axis_index("gy")
-    sides = jnp.stack([gx > 0, gx < gx_size - 1, gy > 0, gy < gy_size - 1]).astype(F32)
-    u1 = run_first(sides, velocity, edge, received)
-    fluid, replies = run_last(sides, u1, rim, below_x, above_x, received)
+    u1 = run_first(layers, flat, edge, received)
+    fluid, replies = run_last(layers, u1, rim, below_x, above_x, received)
     moved = run_gather(pts, dest, exchange(replies), dw)
     return fluid.reshape(3, layers, rows, columns), moved.transpose(1, 0, 2)
 

time: 97 us -> 96.6 us (level)
    ppermute x0 -> x2, local copies, waits for them, and re-layouts: none -> 3.35 us  [the longest x1 1.69 us: shards(): first = lax.ppermute(flat[:, :, :2].transpose(0, 2, 1), 'gy', ahead)]
    transpose x2 -> x0, local copies, waits for them, and re-layouts: 3.35 us -> none  [the longest x1 1.69 us: shards(): first.transpose(0, 2, 1)]
where the time goes in v5:
time: 96.6 us; the launch traced here: 96.3 us
  Pallas kernels  27.9 us (29%)
  blocking collectives  27.3 us (28%)
  starting transfers between devices  21.9 us (23%)
  local copies, waits for them, and re-layouts  15.2 us (16%)
  other arithmetic  3.11 us (3%)
    all_to_all x1, blocking collectives, exchange(): lax.all_to_all(rows_out.reshape(devices, 2, size), ('gx', 'gy'), split_ax...  27.3 us
    all_to_all x1, starting transfers between devices, exchange(): lax.all_to_all(rows_out.reshape(devices, 2, size), ('gx', 'gy'), split_ax...  11.9 us
    pallas_call x1, Pallas kernels, run_first(): pl.pallas_call(functools.partial(first_kernel, layers), in_specs=[HBM, VM...  10.2 us
    pallas_call x1, Pallas kernels, run_last(): pl.pallas_call(functools.partial(last_kernel, layers), in_specs=[VMEM] *...  7.3 us
    pallas_call x1, Pallas kernels, run_gather(): pl.pallas_call(gather_kernel, in_specs=[VMEM] * 3 + [HBM], out_specs=VMEM...  5.73 us
    pallas_call x1, Pallas kernels, run_spread(): pl.pallas_call(functools.partial(spread_kernel, gy_size, slots), in_specs...  4.28 us
    another operation x2, local copies, waits for them, and re-layouts, shards(): jnp.stack([velocity[:, :, x, :] for x in lines], axis=1)  4.07 us
    ppermute x1, starting transfers between devices, shards(): lax.ppermute(flat[:, :, columns - 2:].transpose(0, 2, 1), 'gy', behind)  3.66 us
  transfers between devices with their start and end apart: 5, of which 0 were waited for; matrix products, arithmetic and copies ran while one was open for 15% of the time, Pallas kernels for 11%

profile of v5, /device:TPU:1, one launch (start us, length us, event | category | flops | bytes accessed | tf_op | source)
XLA Modules:
  0.0 96.3 jit_solution(787280477926283212)
XLA Ops:
  0.6 4.3 %spread.1 = (bf16[256,1664]{1,0:T(8,128)(2,1)S(1)}, f32[64,128]{1,0:T(8,128)S(1)}) custom-call(f32[3,8,128]{2,1,0:T(8,128)} %bitcast.38, f32[8]{0:T(128)} %stiff_hbm.1, s32[8,128]{1,0:T(8,128)} %links_hbm.1, s32[8,8]{1,0:T(8,128)} %bitcast.51, s32[8,8]{1,0:T(8,128)} %patch_slots_hbm.1, bf16[8,1024,512]{2,1,0:T(8,128)(2,1)} %bitcast.40), custom_call_target="tpu_custom_call" | custom-call | flops 1000000000 | bytes 9437184 | tf_op jit(solution)/shard_map/spread/pallas_call | solution.py:379
  4.9 1.2 %reshape.40 = bf16[128,2,1664]{2,1,0:T(2,128)(2,1)} reshape(bf16[256,1664]{1,0:T(8,128)(2,1)S(1)} %get-tuple-element.9) | data formatting | bytes 1703936 | tf_op jit(solution)/shard_map/reshape | solution.py:499
  6.1 11.9 %all-to-all-start = ((bf16[128,2,1664]{2,1,0:T(2,128)(2,1)}), bf16[128,2,1664]{2,1,0:T(2,128)(2,1)}, u32[]{:S(2)}, u32[]{:S(2)}) async-start(bf16[128,2,1664]{2,1,0:T(2,128)(2,1)} %reshape.40), calls=%async_computation | async-start | bytes 1703936 | tf_op jit(solution)/shard_map/all_to_all | solution.py:498
  18.1 2.4 %slice_bitcast_fusion.1 = (f32[3,2,1024]{1,2,0:T(8,128)S(1)}, f32[3,2,1024]{1,2,0:T(8,128)S(1)}) fusion(f32[3,1024,512]{2,1,0:T(8,128)} %bitcast.42), kind=kLoop, calls=%fused_computation.1 | loop fusion | bytes 98304 | tf_op jit(solution)/shard_map/transpose | solution.py:507
  20.5 0.5 copy.17
  20.9 3.7 %collective-permute-start.1 = (f32[3,2,1024]{2,1,0:T(2,128)S(1)}, f32[3,2,1024]{2,1,0:T(2,128)S(1)}, u32[]{:S(2)}, u32[]{:S(2)}) collective-permute-start(f32[3,2,1024]{2,1,0:T(2,128)S(1)} %copy.17), channel_id=1, source_target_pairs={{0,1},{1,2},{2,3},{3,4},{4,5},{5,6},{6,7},{8,9},{9,10},{10,11},{11... | collective-permute-start | bytes 73736 | tf_op jit(solution)/shard_map/ppermute | solution.py:508
  24.6 0.5 copy.15
  25.1 1.9 %collective-permute-start = (f32[3,2,1024]{2,1,0:T(2,128)S(1)}, f32[3,2,1024]{2,1,0:T(2,128)S(1)}, u32[]{:S(2)}, u32[]{:S(2)}) collective-permute-start(f32[3,2,1024]{2,1,0:T(2,128)S(1)} %copy.15), channel_id=1, source_target_pairs={{1,0},{2,1},{3,2},{4,3},{5,4},{6,5},{7,6},{9,8},{10,9},{11,10},{12... | collective-permute-start | bytes 73736 | tf_op jit(solution)/shard_map/ppermute | solution.py:507
  27.0 3.8 %slice_bitcast_fusion.5 = (f32[3,1,32,512]{3,1,2,0:T(1,128)S(1)}, f32[3,1,32,512]{3,1,2,0:T(1,128)S(1)}, f32[3,1,32,512]{3,1,2,0:T(1,128)S(1)}, f32[3,1,32,512]{3,1,2,0:T(1,128)S(1)}) fusion(f32[3,32,32,512]{3,2,1,0:T(8,128)} %param.7), kind=kLoop, calls=%fused_computation.8 | loop fusion | bytes 1572864 | tf_op jit(solution)/shard_map/stack;squeeze | solution.py:514
  30.8 0.7 pad_maximum_fusion.1
  31.6 0.3 copy.19
  31.9 1.7 %copy.16 = f32[3,2,1024]{1,2,0:T(8,128)} copy(f32[3,2,1024]{2,1,0:T(2,128)S(1)} %collective-permute-done) | data formatting | bytes 49152 | tf_op jit(solution)/shard_map/ppermute | solution.py:507
  33.6 1.7 %copy.18 = f32[3,2,1024]{1,2,0:T(8,128)} copy(f32[3,2,1024]{2,1,0:T(2,128)S(1)} %collective-permute-done.1) | data formatting | bytes 49152 | tf_op jit(solution)/shard_map/ppermute | solution.py:508
  35.3 2.4 %pad_maximum_fusion.edges = f32[3,1024,128]{2,1,0:T(8,128)S(1)} fusion(f32[3,1024,2]{2,1,0:T(8,128)} %bitcast.45, f32[3,1024,2]{2,1,0:T(8,128)} %bitcast.44, f32[128]{0:T(128)S(1)} %pad.9.clone), kind=kLoop, calls=%fused_computation.2 | loop fusion | flops 786432 | bytes 1622528 | tf_op jit(solution)/shard_map/concatenate | solution.py:509
  37.8 2.4 %reshape.41.received = bf16[256,1664]{1,0:T(8,128)(2,1)S(1)} reshape(bf16[128,2,1664]{2,1,0:T(2,128)(2,1)} %all-to-all-done) | data formatting | bytes 1703936 | tf_op jit(solution)/shard_map/reshape | solution.py:500
  40.2 0.5 rim.1
  40.7 3.1 %collective-permute-start.2 = (bf16[3,2,32,640]{3,2,1,0:T(8,128)(2,1)S(1)}, bf16[3,2,32,640]{3,2,1,0:T(8,128)(2,1)S(1)}, u32[]{:S(2)}, u32[]{:S(2)}) collective-permute-start(bf16[3,2,32,640]{3,2,1,0:T(8,128)(2,1)S(1)} %get-tuple-element.11), channel_id=1, source_target_pairs={{0,8},{8,16},{16,24},{24,32},{32,40},{40,48},{48,56},{56,64},{64,7... | collective-permute-start | bytes 737288 | tf_op jit(solution)/shard_map/ppermute | solution.py:519
  43.8 1.3 %collective-permute-start.3 = (bf16[3,2,32,640]{3,2,1,0:T(8,128)(2,1)S(1)}, bf16[3,2,32,640]{3,2,1,0:T(8,128)(2,1)S(1)}, u32[]{:S(2)}, u32[]{:S(2)}) collective-permute-start(bf16[3,2,32,640]{3,2,1,0:T(8,128)(2,1)S(1)} %get-tuple-element.12), channel_id=1, source_target_pairs={{8,0},{16,8},{24,16},{32,24},{40,32},{48,40},{56,48},{64,56},{72,6... | collective-permute-start | bytes 737288 | tf_op jit(solution)/shard_map/ppermute | solution.py:520
  45.1 10.2 %sweep_first.1.u1_in = f32[3,5,1024,128]{3,2,1,0:T(8,128)S(1)} custom-call(f32[3,1024,512]{2,1,0:T(8,128)} %bitcast.43, f32[3,1024,128]{2,1,0:T(8,128)S(1)} %pad_maximum_fusion.edges, bf16[256,1664]{1,0:T(8,128)(2,1)S(1)} %reshape.41.received), custom_call_target="tpu_custom_call" | custom-call | flops 2000000000 | bytes 25165824 | tf_op jit(solution)/shard_map/sweep_first/pallas_call | solution.py:427
  55.3 7.3 %sweep_last.1 = (f32[3,1024,512]{2,1,0:T(8,128)}, bf16[256,1536]{1,0:T(8,128)(2,1)S(1)}, f32[3,5,1024,128]{3,2,1,0:T(8,128)S(1)}) custom-call(f32[3,5,1024,128]{3,2,1,0:T(8,128)S(1)} %sweep_first.1.u1_in, f32[2,3,5,32,128]{4,3,2,1,0:T(8,128)S(1)} %get-tuple-element.10.rim, ...), custom_call_target="tpu_custom_call", output_to_operand_aliasing={{2}: (0, {})} | custom-call | flops 2000000000 | bytes 16777216 | tf_op jit(solution)/shard_map/sweep_last/pallas_call | solution.py:442
  62.6 0.3 reshape.46
  62.9 27.3 %all_to_all.10 = bf16[128,2,1536]{2,1,0:T(2,128)(2,1)S(1)} all-to-all(bf16[128,2,1536]{2,1,0:T(2,128)(2,1)S(1)} %reshape.46), channel_id=1, replica_groups=mesh['gx'=16,'gy'=8] {'gx','gy'}, dimensions={0} | all-to-all | bytes 1572864 | tf_op jit(solution)/shard_map/all_to_all | solution.py:498
  90.2 0.3 reshape.47.returned
  90.5 5.7 %interp.1 = f32[3,8,128]{2,1,0:T(8,128)} custom-call(f32[3,8,128]{2,1,0:T(8,128)S(1)} %bitcast.39, f32[64,128]{1,0:T(8,128)S(1)} %get-tuple-element.14.dest, bf16[256,1536]{1,0:T(8,128)(2,1)S(1)} %reshape.47.returned, bf16[8,1024,512]{2,1,0:T(8,128)(2,1)} %bitcast.41), custom_call_target="tpu_custom_call" | custom-call | flops 1000000000 | bytes 9437184 | tf_op jit(solution)/shard_map/interp/pallas_call | solution.py:467
  (11 shorter events, 0.3 us)
Async XLA Ops:
  6.1 31.7 %all-to-all-start = ((bf16[128,2,1664]{2,1,0:T(2,128)(2,1)}), bf16[128,2,1664]{2,1,0:T(2,128)(2,1)}, u32[]{:S(2)}, u32[]{:S(2)}) async-start(bf16[128,2,1664]{2,1,0:T(2,128)(2,1)} %reshape.40), calls=%async_computation | async-start | bytes 1703936 | tf_op jit(solution)/shard_map/all_to_all | solution.py:498
  20.9 12.7 %collective-permute-start.1 = (f32[3,2,1024]{2,1,0:T(2,128)S(1)}, f32[3,2,1024]{2,1,0:T(2,128)S(1)}, u32[]{:S(2)}, u32[]{:S(2)}) collective-permute-start(f32[3,2,1024]{2,1,0:T(2,128)S(1)} %copy.17), channel_id=1, source_target_pairs={{0,1},{1,2},{2,3},{3,4},{4,5},{5,6},{6,7},{8,9},{9,10},{10,11},{11... | collective-permute-start | bytes 73736 | tf_op jit(solution)/shard_map/ppermute | solution.py:508
  25.1 6.9 %collective-permute-start = (f32[3,2,1024]{2,1,0:T(2,128)S(1)}, f32[3,2,1024]{2,1,0:T(2,128)S(1)}, u32[]{:S(2)}, u32[]{:S(2)}) collective-permute-start(f32[3,2,1024]{2,1,0:T(2,128)S(1)} %copy.15), channel_id=1, source_target_pairs={{1,0},{2,1},{3,2},{4,3},{5,4},{6,5},{7,6},{9,8},{10,9},{11,10},{12... | collective-permute-start | bytes 73736 | tf_op jit(solution)/shard_map/ppermute | solution.py:507
  40.7 14.6 %collective-permute-start.2 = (bf16[3,2,32,640]{3,2,1,0:T(8,128)(2,1)S(1)}, bf16[3,2,32,640]{3,2,1,0:T(8,128)(2,1)S(1)}, u32[]{:S(2)}, u32[]{:S(2)}) collective-permute-start(bf16[3,2,32,640]{3,2,1,0:T(8,128)(2,1)S(1)} %get-tuple-element.11), channel_id=1, source_target_pairs={{0,8},{8,16},{16,24},{24,32},{32,40},{40,48},{48,56},{56,64},{64,7... | collective-permute-start | bytes 737288 | tf_op jit(solution)/shard_map/ppermute | solution.py:519
  43.8 11.5 %collective-permute-start.3 = (bf16[3,2,32,640]{3,2,1,0:T(8,128)(2,1)S(1)}, bf16[3,2,32,640]{3,2,1,0:T(8,128)(2,1)S(1)}, u32[]{:S(2)}, u32[]{:S(2)}) collective-permute-start(bf16[3,2,32,640]{3,2,1,0:T(8,128)(2,1)S(1)} %get-tuple-element.12), channel_id=1, source_target_pairs={{8,0},{16,8},{24,16},{32,24},{40,32},{48,40},{56,48},{64,56},{72,6... | collective-permute-start | bytes 737288 | tf_op jit(solution)/shard_map/ppermute | solution.py:520
  62.9 27.6 %copy-start = (f32[8,3,128]{2,0,1:T(8,128)S(1)}, f32[8,3,128]{2,0,1:T(8,128)}, u32[]{:S(2)}) copy-start(f32[8,3,128]{2,0,1:T(8,128)} %param.8) | copy-start | bytes 36868

commit v6 on v5

--- a/solution.py
+++ b/solution.py
@@ -109,6 +109,44 @@
     out[:, 3 * patch :] = head.astype(BF16)
 
 
+def edge_kernel(velocity, first, last, start, end, sems):
+    patch = velocity.shape[2]
+    loads = []
+    for c in range(3):
+        for i, (to, lane) in enumerate(((start, 0), (end, patch - LANES))):
+            loads.append(pltpu.make_async_copy(velocity.at[c, :, pl.ds(lane, LANES)], to.at[c], sems.at[2 * c + i]))
+    for load in loads:
+        load.start()
+    row, lane = iota((16, LANES), 0), iota((16, LANES), 1)
+    across = (((1,), (1,)), ((), ()))
+    sums = [0.0, 0.0]
+    for c in range(3):
+        for i, (tile, at) in enumerate(((start, 0), (end, LANES - 2))):
+            loads[2 * c + i].wait()
+            pick = ((row - 2 * c == lane - at) & (lane >= at) & (lane < at + 2)).astype(F32).astype(BF16)
+            sums[i] += lax.dot_general(pick, tile[c].astype(BF16), across, preferred_element_type=F32)
+    first[...] = sums[0][:8]
+    last[...] = sums[1][:8]
+
+
+def line_kernel(velocity, out, lines, sems):
+    layers, rows, patch = velocity.shape[1:]
+    loads = []
+    for i, x in enumerate((0, rows - 8)):
+        for t in range(patch // LANES):
+            part = velocity.at[:, :, pl.ds(x, 8), pl.ds(t * LANES, LANES)]
+            loads.append(pltpu.make_async_copy(part, lines.at[i, t], sems.at[len(loads)]))
+    for load in loads:
+        load.start()
+    for i in range(2):
+        for t in range(patch // LANES):
+            loads[i * (patch // LANES) + t].wait()
+            for c in range(3):
+                for j in range(2):
+                    at = (2 * i + j) * layers
+                    out[c, at : at + layers, t * LANES : (t + 1) * LANES] = lines[i, t, c, :, 6 * i + j, :]
+
+
 class Arrived:
     def __init__(self, received, patch):
         self.received, self.patch = received, patch
@@ -135,25 +173,35 @@
         return force_step * main, force_step * (dot(below, self.tails[c]) + dot(above, self.starts[c]))
 
 
-def rim_kernel(layer_rows, velocity, edges, received, low_rows, high_rows, rim):
+def rim_kernel(layer_rows, velocity, ahead, behind, received, low_rows, high_rows, rim, edges):
     layers, patch = low_rows.shape[2], velocity.shape[2]
-    slots = received.shape[0]
+    slots, cells = received.shape[0], ahead.shape[1]
+
+    turned = jnp.transpose(jnp.concatenate([ahead[...], behind[...], jnp.zeros((LANES - 16, cells), F32)], axis=0))
+    turned = turned.astype(BF16)
+    row, lane = iota((LANES, LANES), 0), iota((LANES, LANES), 1)
+    for c in range(3):
+        put = ((lane < 2) & (row == lane + 2 * c)) | ((lane >= LANES - 2) & (row == lane - (LANES - 2) + 8 + 2 * c))
+        edges[c] = dot(turned, put.astype(F32).astype(BF16))
+
     arrived = Arrived(received, patch)
     row = iota((4 * layers, slots), 0)
     line, z = row // layers, lax.rem(row, layers)
     chosen = arrived.choose(z * layer_rows + jnp.where(line < 2, line, layer_rows - 4 + line))
     for c in range(3):
         main, edge = arrived.force(chosen, c)
-        main, edge = velocity[c] + main, edges[c] + edge
+        main = velocity[c] + main
         for j in range(4):
             at = slice(j * layers, (j + 1) * layers)
+            x = j if j < 2 else layer_rows - 4 + j
+            side = edges[c, pl.ds(x, layers, stride=layer_rows), :] + edge[at]
             to = low_rows if j < 2 else high_rows
             to[c, j % 2, :, :patch] = main[at].astype(BF16)
-            to[c, j % 2, :, patch:] = edge[at].astype(BF16)
-        for side, at in ((0, slice(0, layers)), (1, slice(3 * layers, 4 * layers))):
-            for t in range(patch // LANES):
-                rim[side, c, t] = main[at, t * LANES : (t + 1) * LANES]
-            rim[side, c, patch // LANES] = edge[at]
+            to[c, j % 2, :, patch:] = side.astype(BF16)
+            if j in (0, 3):
+                for t in range(patch // LANES):
+                    rim[j // 3, c, t] = main[at, t * LANES : (t + 1) * LANES]
+                rim[j // 3, c, patch // LANES] = side
 
 
 def update(centre, weights, c, east, west, north, south, up, down):
@@ -402,23 +450,53 @@
     )(*[in_hbm(x) for x in (pts, stiffness, links, owners, patch_slots, dw)])
 
 
-def run_rim(layer_rows, layers, rim_velocity, rim_edge, received):
-    patch = rim_velocity.shape[2]
+def run_edges(velocity):
+    cells = velocity.shape[1]
+    return pl.pallas_call(
+        edge_kernel,
+        in_specs=[HBM],
+        out_specs=[VMEM, VMEM],
+        out_shape=[jax.ShapeDtypeStruct((8, cells), F32)] * 2,
+        scratch_shapes=[pltpu.VMEM((3, cells, LANES), F32)] * 2 + [pltpu.SemaphoreType.DMA((6,))],
+        compiler_params=params(24),
+        cost_estimate=cost(10**8, 3),
+        name="edges",
+    )(in_hbm(velocity))
+
+
+def run_lines(velocity):
+    layers, patch = velocity.shape[1], velocity.shape[3]
+    tiles = patch // LANES
+    return pl.pallas_call(
+        line_kernel,
+        in_specs=[HBM],
+        out_specs=VMEM,
+        out_shape=jax.ShapeDtypeStruct((3, 4 * layers, patch), F32),
+        scratch_shapes=[pltpu.VMEM((2, tiles, 3, layers, 8, LANES), F32), pltpu.SemaphoreType.DMA((2 * tiles,))],
+        compiler_params=params(24),
+        cost_estimate=cost(10**8, 3),
+        name="lines",
+    )(in_hbm(velocity))
+
+
+def run_rim(layer_rows, layers, rim_velocity, ahead, behind, received):
+    patch, cells = rim_velocity.shape[2], ahead.shape[1]
     wide = patch + LANES
     side = (3, 2, layers, wide)
     return pl.pallas_call(
         functools.partial(rim_kernel, layer_rows),
-        in_specs=[VMEM] * 3,
-        out_specs=[VMEM] * 3,
+        in_specs=[VMEM] * 4,
+        out_specs=[VMEM] * 4,
         out_shape=[
             jax.ShapeDtypeStruct(side, BF16),
             jax.ShapeDtypeStruct(side, BF16),
             jax.ShapeDtypeStruct((2, 3, wide // LANES, layers, LANES), F32),
+            jax.ShapeDtypeStruct((3, cells, LANES), F32),
         ],
         compiler_params=params(24),
         cost_estimate=cost(10**8, 3),
         name="rim",
-    )(rim_velocity, rim_edge, received)
+    )(rim_velocity, ahead, behind, received)
 
 
 def run_first(layers, velocity, edge, received):
@@ -501,19 +579,11 @@
 
     received = exchange(outgoing)
 
-    ahead = [(i + 1, i) for i in range(gy_size - 1)]
-    behind = [(i, i + 1) for i in range(gy_size - 1)]
     flat = velocity.reshape(3, cells, columns)
-    first = lax.ppermute(flat[:, :, :2].transpose(0, 2, 1), "gy", ahead)
-    last = lax.ppermute(flat[:, :, columns - 2 :].transpose(0, 2, 1), "gy", behind)
-    edge = jnp.concatenate(
-        [first.transpose(0, 2, 1), jnp.zeros((3, cells, LANES - 4), F32), last.transpose(0, 2, 1)], axis=2
-    )
-    planes = edge.reshape(3, layers, rows, LANES)
-    lines = (0, 1, rows - 2, rows - 1)
-    rim_velocity = jnp.stack([velocity[:, :, x, :] for x in lines], axis=1).reshape(3, 4 * layers, patch)
-    rim_edge = jnp.stack([planes[:, :, x, :] for x in lines], axis=1).reshape(3, 4 * layers, LANES)
-    low_rows, high_rows, rim = run_rim(rows, layers, rim_velocity, rim_edge, received)
+    first, last = run_edges(flat)
+    ahead = lax.ppermute(first, "gy", [(i + 1, i) for i in range(gy_size - 1)])
+    behind = lax.ppermute(last, "gy", [(i, i + 1) for i in range(gy_size - 1)])
+    low_rows, high_rows, rim, edge = run_rim(rows, layers, run_lines(velocity), ahead, behind, received)
 
     up = [(i, i + 1) for i in range(gx_size - 1)]
     below_x = lax.ppermute(high_rows, "gx", up)

time: 96.6 us -> 87.3 us (0.904)
  local copies, waits for them, and re-layouts: 15.2 us -> 2.14 us
  waiting for transfers between devices: 0.01 us -> 7.32 us
  Pallas kernels: 27.9 us -> 32.3 us
  blocking collectives: 27.3 us -> 23.7 us
  other arithmetic: 3.11 us -> 0 us
  starting transfers between devices: 21.9 us -> 20.7 us
    all_to_all x1, waiting for transfers between devices: 0.01 us -> 7.31 us  [exchange(): lax.all_to_all(rows_out.reshape(devices, 2, size), ('gx', 'gy'), split_ax...]
    pallas_call x0 -> x2, Pallas kernels: none -> 4.13 us  [the longest x1 2.13 us: run_edges(): pl.pallas_call(edge_kernel, in_specs=[HBM], out_specs=[VMEM, VMEM], out_s...]
    another operation x2 -> x0, local copies, waits for them, and re-layouts: 4.07 us -> none  [shards(): jnp.stack([velocity[:, :, x, :] for x in lines], axis=1)]
    all_to_all x1, blocking collectives: 27.3 us -> 23.7 us  [exchange(): lax.all_to_all(rows_out.reshape(devices, 2, size), ('gx', 'gy'), split_ax...]
    ppermute x2 -> x0, local copies, waits for them, and re-layouts: 3.35 us -> none  [the longest x1 1.69 us: shards(): first = lax.ppermute(flat[:, :, :2].transpose(0, 2, 1), 'gy', ahead)]
    transpose x3 -> x0, local copies, waits for them, and re-layouts: 3.33 us -> none  [the longest x2 2.86 us: shards(): first = lax.ppermute(flat[:, :, :2].transpose(0, 2, 1), 'gy', ahead)]
    concatenate x1 -> x0, other arithmetic: 2.35 us -> none  [shards(): jnp.concatenate([first.transpose(0, 2, 1), jnp.zeros((3, cells, LANES - 4...]
    reshape x2, local copies, waits for them, and re-layouts: 2.66 us -> 0.62 us  [exchange(): return lax.all_to_all(rows_out.reshape(devices, 2, size), ('gx', 'gy'), s...]
  transfers between devices with their start and end apart: 5 -> 5, of which waited for: 0 -> 1; matrix products, arithmetic and copies ran while one was open for 15% -> 0% of each run, Pallas kernels for 11% -> 16%
where the time goes in v6:
time: 87.3 us; the launch traced here: 86.9 us
  Pallas kernels  32.3 us (37%)
  blocking collectives  23.7 us (27%)
  starting transfers between devices  20.7 us (24%)
  waiting for transfers between devices  7.32 us (8%)
  local copies, waits for them, and re-layouts  2.14 us (2%)
    all_to_all x1, blocking collectives, exchange(): lax.all_to_all(rows_out.reshape(devices, 2, size), ('gx', 'gy'), split_ax...  23.7 us
    all_to_all x1, starting transfers between devices, exchange(): lax.all_to_all(rows_out.reshape(devices, 2, size), ('gx', 'gy'), split_ax...  11.5 us
    pallas_call x1, Pallas kernels, run_first(): pl.pallas_call(functools.partial(first_kernel, layers), in_specs=[HBM, VM...  10.2 us
    all_to_all x1, waiting for transfers between devices, exchange(): lax.all_to_all(rows_out.reshape(devices, 2, size), ('gx', 'gy'), split_ax...  7.31 us
    pallas_call x1, Pallas kernels, run_last(): pl.pallas_call(functools.partial(last_kernel, layers), in_specs=[VMEM] *...  7.3 us
    pallas_call x1, Pallas kernels, run_gather(): pl.pallas_call(gather_kernel, in_specs=[VMEM] * 3 + [HBM], out_specs=VMEM...  5.72 us
    pallas_call x1, Pallas kernels, run_spread(): pl.pallas_call(functools.partial(spread_kernel, gy_size, slots), in_specs...  4.28 us
    ppermute x1, starting transfers between devices, shards(): ahead = lax.ppermute(first, 'gy', [(i + 1, i) for i in range(gy_size - 1)])  2.98 us
  transfers between devices with their start and end apart: 5, of which 1 were waited for; matrix products, arithmetic and copies ran while one was open for 0% of the time, Pallas kernels for 16%

profile of v6, /device:TPU:1, one launch (start us, length us, event | category | flops | bytes accessed | tf_op | source)
XLA Modules:
  0.0 86.9 jit_solution(13336843036549446731)
XLA Ops:
  0.6 4.3 %spread.1 = (bf16[256,1664]{1,0:T(8,128)(2,1)S(1)}, f32[64,128]{1,0:T(8,128)S(1)}) custom-call(f32[3,8,128]{2,1,0:T(8,128)} %bitcast.6, f32[8]{0:T(128)} %stiff_hbm.1, s32[8,128]{1,0:T(8,128)} %links_hbm.1, s32[8,8]{1,0:T(8,128)} %bitcast.13, s32[8,8]{1,0:T(8,128)} %patch_slots_hbm.1, bf16[8,1024,512]{2,1,0:T(8,128)(2,1)} %bitcast.10), custom_call_target="tpu_custom_call" | custom-call | flops 1000000000 | bytes 9437184 | tf_op jit(solution)/shard_map/spread/pallas_call | solution.py:427
  4.9 1.2 %reshape.31 = bf16[128,2,1664]{2,1,0:T(2,128)(2,1)} reshape(bf16[256,1664]{1,0:T(8,128)(2,1)S(1)} %get-tuple-element.14) | data formatting | bytes 1703936 | tf_op jit(solution)/shard_map/reshape | solution.py:577
  6.1 11.5 %all-to-all-start = ((bf16[128,2,1664]{2,1,0:T(2,128)(2,1)}), bf16[128,2,1664]{2,1,0:T(2,128)(2,1)S(1)}, u32[]{:S(2)}, u32[]{:S(2)}) async-start(bf16[128,2,1664]{2,1,0:T(2,128)(2,1)} %reshape.31), calls=%async_computation | async-start | bytes 1703936 | tf_op jit(solution)/shard_map/all_to_all | solution.py:576
  17.6 2.1 %edges.1 = (f32[8,1024]{1,0:T(8,128)S(1)}, f32[8,1024]{1,0:T(8,128)S(1)}) custom-call(f32[3,1024,512]{2,1,0:T(8,128)} %bitcast.8), custom_call_target="tpu_custom_call" | custom-call | flops 100000000 | bytes 3145728 | tf_op jit(solution)/shard_map/edges/pallas_call | solution.py:455
  19.8 3.0 %collective-permute-start = (f32[8,1024]{1,0:T(8,128)S(1)}, f32[8,1024]{1,0:T(8,128)S(1)}, u32[]{:S(2)}, u32[]{:S(2)}) collective-permute-start(f32[8,1024]{1,0:T(8,128)S(1)} %get-tuple-element.12), channel_id=1, source_target_pairs={{1,0},{2,1},{3,2},{4,3},{5,4},{6,5},{7,6},{9,8},{10,9},{11,10},{12... | collective-permute-start | bytes 98312 | tf_op jit(solution)/shard_map/ppermute | solution.py:584
  22.8 2.6 %collective-permute-start.1 = (f32[8,1024]{1,0:T(8,128)S(1)}, f32[8,1024]{1,0:T(8,128)S(1)}, u32[]{:S(2)}, u32[]{:S(2)}) collective-permute-start(f32[8,1024]{1,0:T(8,128)S(1)} %get-tuple-element.13), channel_id=1, source_target_pairs={{0,1},{1,2},{2,3},{3,4},{4,5},{5,6},{6,7},{8,9},{9,10},{10,11},{11... | collective-permute-start | bytes 98312 | tf_op jit(solution)/shard_map/ppermute | solution.py:585
  25.4 2.0 %lines.1.velocity = f32[3,128,512]{2,1,0:T(8,128)S(1)} custom-call(f32[3,32,32,512]{3,2,1,0:T(8,128)} %velocity.1), custom_call_target="tpu_custom_call" | custom-call | flops 100000000 | bytes 3145728 | tf_op jit(solution)/shard_map/lines/pallas_call | solution.py:470
  27.4 7.3 %all-to-all-done = bf16[128,2,1664]{2,1,0:T(2,128)(2,1)S(1)} async-done(((bf16[128,2,1664]{2,1,0:T(2,128)(2,1)}), bf16[128,2,1664]{2,1,0:T(2,128)(2,1)S(1)}, u32[]{:S(2)}, u32[]{:S(2)}) %all-to-all-start) | async-done | bytes 852000 | tf_op jit(solution)/shard_map/all_to_all | solution.py:576
  34.7 0.3 reshape.32.received
  35.0 0.0 collective-permute-done.ahead
  35.0 0.0 collective-permute-done.1.behind
  35.0 0.7 rim.1
  35.7 2.4 %collective-permute-start.2 = (bf16[3,2,32,640]{3,2,1,0:T(8,128)(2,1)S(1)}, bf16[3,2,32,640]{3,2,1,0:T(8,128)(2,1)S(1)}, u32[]{:S(2)}, u32[]{:S(2)}) collective-permute-start(bf16[3,2,32,640]{3,2,1,0:T(8,128)(2,1)S(1)} %get-tuple-element.17), channel_id=1, source_target_pairs={{0,8},{8,16},{16,24},{24,32},{32,40},{40,48},{48,56},{56,64},{64,7... | collective-permute-start | bytes 737288 | tf_op jit(solution)/shard_map/ppermute | solution.py:589
  38.1 1.3 %collective-permute-start.3 = (bf16[3,2,32,640]{3,2,1,0:T(8,128)(2,1)S(1)}, bf16[3,2,32,640]{3,2,1,0:T(8,128)(2,1)S(1)}, u32[]{:S(2)}, u32[]{:S(2)}) collective-permute-start(bf16[3,2,32,640]{3,2,1,0:T(8,128)(2,1)S(1)} %get-tuple-element.18), channel_id=1, source_target_pairs={{8,0},{16,8},{24,16},{32,24},{40,32},{48,40},{56,48},{64,56},{72,6... | collective-permute-start | bytes 737288 | tf_op jit(solution)/shard_map/ppermute | solution.py:590
  39.4 10.2 %sweep_first.1.u1_in = f32[3,5,1024,128]{3,2,1,0:T(8,128)S(1)} custom-call(f32[3,1024,512]{2,1,0:T(8,128)} %bitcast.9, f32[3,1024,128]{2,1,0:T(8,128)S(1)} %get-tuple-element.15.edges, bf16[256,1664]{1,0:T(8,128)(2,1)S(1)} %reshape.32.received), custom_call_target="tpu_custom_call" | custom-call | flops 2000000000 | bytes 25165824 | tf_op jit(solution)/shard_map/sweep_first/pallas_call | solution.py:505
  49.6 0.0 copy-start
  49.6 0.0 collective-permute-done.2.below_x
  49.6 0.0 collective-permute-done.3.above_x
  49.6 7.3 %sweep_last.1 = (f32[3,1024,512]{2,1,0:T(8,128)}, bf16[256,1536]{1,0:T(8,128)(2,1)S(1)}, f32[3,5,1024,128]{3,2,1,0:T(8,128)S(1)}) custom-call(f32[3,5,1024,128]{3,2,1,0:T(8,128)S(1)} %sweep_first.1.u1_in, f32[2,3,5,32,128]{4,3,2,1,0:T(8,128)S(1)} %get-tuple-element.16.rim, ...), custom_call_target="tpu_custom_call", output_to_operand_aliasing={{2}: (0, {})} | custom-call | flops 2000000000 | bytes 16777216 | tf_op jit(solution)/shard_map/sweep_last/pallas_call | solution.py:520
  56.9 0.3 reshape.34
  57.2 23.7 %all_to_all.10 = bf16[128,2,1536]{2,1,0:T(2,128)(2,1)S(1)} all-to-all(bf16[128,2,1536]{2,1,0:T(2,128)(2,1)S(1)} %reshape.34), channel_id=1, replica_groups=mesh['gx'=16,'gy'=8] {'gx','gy'}, dimensions={0} | all-to-all | bytes 1572864 | tf_op jit(solution)/shard_map/all_to_all | solution.py:576
  80.9 0.3 reshape.35.returned
  81.2 0.0 copy-done
  81.2 5.7 %interp.1 = f32[3,8,128]{2,1,0:T(8,128)} custom-call(f32[3,8,128]{2,1,0:T(8,128)S(1)} %bitcast.7, f32[64,128]{1,0:T(8,128)S(1)} %get-tuple-element.20.dest, bf16[256,1536]{1,0:T(8,128)(2,1)S(1)} %reshape.35.returned, bf16[8,1024,512]{2,1,0:T(8,128)(2,1)} %bitcast.11), custom_call_target="tpu_custom_call" | custom-call | flops 1000000000 | bytes 9437184 | tf_op jit(solution)/shard_map/interp/pallas_call | solution.py:545
Async XLA Ops:
  6.1 28.5 %all-to-all-start = ((bf16[128,2,1664]{2,1,0:T(2,128)(2,1)}), bf16[128,2,1664]{2,1,0:T(2,128)(2,1)S(1)}, u32[]{:S(2)}, u32[]{:S(2)}) async-start(bf16[128,2,1664]{2,1,0:T(2,128)(2,1)} %reshape.31), calls=%async_computation | async-start | bytes 1703936 | tf_op jit(solution)/shard_map/all_to_all | solution.py:576
  19.8 15.2 %collective-permute-start = (f32[8,1024]{1,0:T(8,128)S(1)}, f32[8,1024]{1,0:T(8,128)S(1)}, u32[]{:S(2)}, u32[]{:S(2)}) collective-permute-start(f32[8,1024]{1,0:T(8,128)S(1)} %get-tuple-element.12), channel_id=1, source_target_pairs={{1,0},{2,1},{3,2},{4,3},{5,4},{6,5},{7,6},{9,8},{10,9},{11,10},{12... | collective-permute-start | bytes 98312 | tf_op jit(solution)/shard_map/ppermute | solution.py:584
  22.8 12.3 %collective-permute-start.1 = (f32[8,1024]{1,0:T(8,128)S(1)}, f32[8,1024]{1,0:T(8,128)S(1)}, u32[]{:S(2)}, u32[]{:S(2)}) collective-permute-start(f32[8,1024]{1,0:T(8,128)S(1)} %get-tuple-element.13), channel_id=1, source_target_pairs={{0,1},{1,2},{2,3},{3,4},{4,5},{5,6},{6,7},{8,9},{9,10},{10,11},{11... | collective-permute-start | bytes 98312 | tf_op jit(solution)/shard_map/ppermute | solution.py:585
  35.7 13.9 %collective-permute-start.2 = (bf16[3,2,32,640]{3,2,1,0:T(8,128)(2,1)S(1)}, bf16[3,2,32,640]{3,2,1,0:T(8,128)(2,1)S(1)}, u32[]{:S(2)}, u32[]{:S(2)}) collective-permute-start(bf16[3,2,32,640]{3,2,1,0:T(8,128)(2,1)S(1)} %get-tuple-element.17), channel_id=1, source_target_pairs={{0,8},{8,16},{16,24},{24,32},{32,40},{40,48},{48,56},{56,64},{64,7... | collective-permute-start | bytes 737288 | tf_op jit(solution)/shard_map/ppermute | solution.py:589
  38.1 11.5 %collective-permute-start.3 = (bf16[3,2,32,640]{3,2,1,0:T(8,128)(2,1)S(1)}, bf16[3,2,32,640]{3,2,1,0:T(8,128)(2,1)S(1)}, u32[]{:S(2)}, u32[]{:S(2)}) collective-permute-start(bf16[3,2,32,640]{3,2,1,0:T(8,128)(2,1)S(1)} %get-tuple-element.18), channel_id=1, source_target_pairs={{8,0},{16,8},{24,16},{32,24},{40,32},{48,40},{56,48},{64,56},{72,6... | collective-permute-start | bytes 737288 | tf_op jit(solution)/shard_map/ppermute | solution.py:590
  49.6 31.7 %copy-start = (f32[8,3,128]{2,0,1:T(8,128)S(1)}, f32[8,3,128]{2,0,1:T(8,128)}, u32[]{:S(2)}) copy-start(f32[8,3,128]{2,0,1:T(8,128)} %param.8) | copy-start | bytes 36868

commit v7 on v6

--- a/solution.py
+++ b/solution.py
@@ -16,6 +16,7 @@
 BF16 = jnp.bfloat16
 LANES = 128
 BELOW, ABOVE = 2, 10
+NEAR = 1
 
 
 def dot(a, b):
@@ -177,7 +178,10 @@
     layers, patch = low_rows.shape[2], velocity.shape[2]
     slots, cells = received.shape[0], ahead.shape[1]
 
-    turned = jnp.transpose(jnp.concatenate([ahead[...], behind[...], jnp.zeros((LANES - 16, cells), F32)], axis=0))
+    sides = beside()
+    from_ahead = jnp.where(sides[3] > 0.0, ahead[...], 0.0)
+    from_behind = jnp.where(sides[2] > 0.0, behind[...], 0.0)
+    turned = jnp.transpose(jnp.concatenate([from_ahead, from_behind, jnp.zeros((LANES - 16, cells), F32)], axis=0))
     turned = turned.astype(BF16)
     row, lane = iota((LANES, LANES), 0), iota((LANES, LANES), 1)
     for c in range(3):
@@ -300,12 +304,16 @@
             sweep_pair(u0, layers, step * depth - 1 + 2 * i, nothing, nothing, store, count)
 
 
-def last_kernel(layers, u1_in, rim, below_x, above_x, received, fluid_hbm, replies, u1, mid, halo, fluid, pick, sems):
+def last_kernel(
+    layers, u1_in, rim, below_x, above_x, received, dw_hbm, fluid_hbm, replies, u1, near_dw, mid, halo, fluid, pick, sems
+):
     count, cells = u1.shape[1:3]
     rows, tiles = cells // layers, count - 1
     patch, slots = tiles * LANES, received.shape[0]
     sides = beside()
     mask = edge_mask(sides)
+    ahead = pltpu.make_async_copy(dw_hbm.at[pl.ds(0, near_dw.shape[0])], near_dw, sems.at[layers // 8])
+    ahead.start()
 
     heads = received[:, 3 * patch :].astype(F32)
     slot = (heads[:, 0:1] * 32.0 + heads[:, 1:2] - 1.0).astype(jnp.int32)
@@ -316,7 +324,8 @@
         for c in range(3):
             for j in range(2):
                 for t in range(count):
-                    halo[side, c, j, t] = source[c, j, :, t * LANES : (t + 1) * LANES].astype(F32)
+                    arrived = source[c, j, :, t * LANES : (t + 1) * LANES].astype(F32)
+                    halo[side, c, j, t] = jnp.where(sides[side] > 0.0, arrived, 0.0)
     for side in range(2):
         near, row = 1 - side, (rows - 1) * side
         slope = -transport_rate if side else transport_rate
@@ -371,13 +380,14 @@
         replies[:, c * patch : (c + 1) * patch] = dot(pick[...], fluid[c].astype(BF16)).astype(BF16)
     for step in range(layers // depth):
         write(step).wait()
-
-
-def gather_kernel(pts, dest, returned, dw_hbm, out, dw, picked, moved, sems):
+    ahead.wait()
+
+
+def gather_kernel(pts, dest, returned, near_dw, dw_hbm, out, dw, picked, moved, sems):
     entries, slots = dest.shape[0], returned.shape[0]
-    blocks, patch, points = dw.shape[0], dw.shape[2], pts.shape[2]
+    near, blocks, patch, points = near_dw.shape[0], dw.shape[0], dw.shape[2], pts.shape[2]
     inter = entries // blocks
-    for b in range(blocks):
+    for b in range(near, blocks):
         pltpu.make_async_copy(dw_hbm.at[b], dw.at[b], sems.at[b]).start()
     to = dest[:, 0:1].astype(jnp.int32)
     pick = (iota((entries, slots), 1) == to).astype(F32).astype(BF16)
@@ -385,20 +395,27 @@
         picked[c] = dot(pick, returned[:, c * patch : (c + 1) * patch])
     k_of_lane = lax.rem(iota((points, LANES), 1), inter)
 
-    @pl.loop(0, blocks)
-    def _(b):
+    def block(b, weights):
         at = pl.ds(pl.multiple_of(b * inter, inter), inter)
         parts = [picked[c, at, :] for c in range(3)]
         parts.append(jnp.zeros((LANES - 3 * inter, patch), F32))
         cells = jnp.concatenate(parts, axis=0).astype(BF16)
-        pltpu.make_async_copy(dw_hbm.at[b], dw.at[b], sems.at[b]).wait()
-        every = lax.dot_general(dw[b], cells, (((1,), (1,)), ((), ())), preferred_element_type=F32)
+        every = lax.dot_general(weights, cells, (((1,), (1,)), ((), ())), preferred_element_type=F32)
         folded = jnp.zeros((points, LANES), F32)
         for k in range(inter):
             folded += jnp.where(k_of_lane == k, every[k * points : (k + 1) * points], 0.0)
         turned = jnp.transpose(folded)
         for c in range(3):
             moved[c, pl.ds(b, 1), :] = jnp.sum(turned[c * inter : (c + 1) * inter], axis=0, keepdims=True)
+
+    @pl.loop(0, near)
+    def _(b):
+        block(b, near_dw[b])
+
+    @pl.loop(near, blocks)
+    def _(b):
+        pltpu.make_async_copy(dw_hbm.at[b], dw.at[b], sems.at[b]).wait()
+        block(b, dw[b])
 
     for c in range(3):
         out[c] = pts[c] + fiber_step * moved[c]
@@ -514,37 +531,38 @@
     )(in_hbm(velocity), edge, received)
 
 
-def run_last(layers, u1, rim, below_x, above_x, received):
+def run_last(layers, near, u1, rim, below_x, above_x, received, dw):
     count, cells = u1.shape[1:3]
     patch, slots = (count - 1) * LANES, received.shape[0]
     return pl.pallas_call(
         functools.partial(last_kernel, layers),
-        in_specs=[VMEM] * 5,
-        out_specs=[HBM, VMEM, VMEM],
+        in_specs=[VMEM] * 5 + [HBM],
+        out_specs=[HBM, VMEM, VMEM, VMEM],
         out_shape=[
             jax.ShapeDtypeStruct((3, cells, patch), F32),
             jax.ShapeDtypeStruct((slots, 3 * patch), BF16),
             jax.ShapeDtypeStruct(u1.shape, F32),
+            jax.ShapeDtypeStruct((near, *dw.shape[1:]), BF16),
         ],
         scratch_shapes=[
             pltpu.VMEM((2, 3, count, layers, LANES), F32),
             pltpu.VMEM((2, 3, 2, count, layers, LANES), F32),
             pltpu.VMEM((3, cells, patch), F32),
             pltpu.VMEM((slots, cells), BF16),
-            pltpu.SemaphoreType.DMA((layers // 8,)),
+            pltpu.SemaphoreType.DMA((layers // 8 + 1,)),
         ],
         input_output_aliases={0: 2},
-        compiler_params=params(24),
+        compiler_params=params(34),
         cost_estimate=cost(2 * 10**9, 16),
         name="sweep_last",
-    )(u1, rim, below_x, above_x, received)[:2]
-
-
-def run_gather(pts, dest, returned, dw):
+    )(u1, rim, below_x, above_x, received, in_hbm(dw))
+
+
+def run_gather(pts, dest, returned, near_dw, dw):
     blocks, patch = dw.shape[0], dw.shape[2]
     return pl.pallas_call(
         gather_kernel,
-        in_specs=[VMEM] * 3 + [HBM],
+        in_specs=[VMEM] * 4 + [HBM],
         out_specs=VMEM,
         out_shape=jax.ShapeDtypeStruct(pts.shape, F32),
         scratch_shapes=[
@@ -556,7 +574,7 @@
         compiler_params=params(24),
         cost_estimate=cost(10**9, 9),
         name="interp",
-    )(pts, dest, returned, in_hbm(dw))
+    )(pts, dest, returned, near_dw, in_hbm(dw))
 
 
 def shards(velocity, fiber_points, stiffness, links, delta_weights, owners, patch_slots):
@@ -581,16 +599,16 @@
 
     flat = velocity.reshape(3, cells, columns)
     first, last = run_edges(flat)
-    ahead = lax.ppermute(first, "gy", [(i + 1, i) for i in range(gy_size - 1)])
-    behind = lax.ppermute(last, "gy", [(i, i + 1) for i in range(gy_size - 1)])
+    ahead = lax.ppermute(first, "gy", [((i + 1) % gy_size, i) for i in range(gy_size)])
+    behind = lax.ppermute(last, "gy", [(i, (i + 1) % gy_size) for i in range(gy_size)])
     low_rows, high_rows, rim, edge = run_rim(rows, layers, run_lines(velocity), ahead, behind, received)
 
-    up = [(i, i + 1) for i in range(gx_size - 1)]
+    up = [(i, (i + 1) % gx_size) for i in range(gx_size)]
     below_x = lax.ppermute(high_rows, "gx", up)
     above_x = lax.ppermute(low_rows, "gx", [(b, a) for a, b in up])
     u1 = run_first(layers, flat, edge, received)
-    fluid, replies = run_last(layers, u1, rim, below_x, above_x, received)
-    moved = run_gather(pts, dest, exchange(replies), dw)
+    fluid, replies, _, near_dw = run_last(layers, NEAR, u1, rim, below_x, above_x, received, dw)
+    moved = run_gather(pts, dest, exchange(replies), near_dw, dw)
     return fluid.reshape(3, layers, rows, columns), moved.transpose(1, 0, 2)
 
 

time: 87.3 us -> 85.7 us (0.982)
  waiting for transfers between devices: 7.32 us -> 11.1 us
  blocking collectives: 23.7 us -> 21 us
  starting transfers between devices: 20.7 us -> 18.1 us
    all_to_all x1, waiting for transfers between devices: 7.31 us -> 11.1 us  [exchange(): lax.all_to_all(rows_out.reshape(devices, 2, size), ('gx', 'gy'), split_ax...]
    ppermute x2, starting transfers between devices: 5.58 us -> 1.79 us  [the longest x1 1.08 us: shards(): lax.ppermute(first, 'gy', [((i + 1) % gy_size, i) for i in range(gy_size)])]
    ppermute x1, starting transfers between devices: 1.29 us -> 4.35 us  [shards(): above_x = lax.ppermute(low_rows, 'gx', [(b, a) for a, b in up])]
    all_to_all x1, blocking collectives: 23.7 us -> 21 us  [exchange(): lax.all_to_all(rows_out.reshape(devices, 2, size), ('gx', 'gy'), split_ax...]
    ppermute x1, starting transfers between devices: 2.36 us -> 0.5 us  [shards(): below_x = lax.ppermute(high_rows, 'gx', up)]
  transfers between devices with their start and end apart: 5 -> 5, of which waited for: 1 -> 1; matrix products, arithmetic and copies ran while one was open for 0% -> 0% of each run, Pallas kernels for 16% -> 17%
where the time goes in v7:
time: 85.7 us; the launch traced here: 85.5 us
  Pallas kernels  32.3 us (38%)
  blocking collectives  21 us (25%)
  starting transfers between devices  18.1 us (21%)
  waiting for transfers between devices  11.1 us (13%)
  local copies, waits for them, and re-layouts  2.14 us (2%)
    all_to_all x1, blocking collectives, exchange(): lax.all_to_all(rows_out.reshape(devices, 2, size), ('gx', 'gy'), split_ax...  21 us
    all_to_all x1, starting transfers between devices, exchange(): lax.all_to_all(rows_out.reshape(devices, 2, size), ('gx', 'gy'), split_ax...  11.5 us
    all_to_all x1, waiting for transfers between devices, exchange(): lax.all_to_all(rows_out.reshape(devices, 2, size), ('gx', 'gy'), split_ax...  11.1 us
    pallas_call x1, Pallas kernels, run_first(): pl.pallas_call(functools.partial(first_kernel, layers), in_specs=[HBM, VM...  10.2 us
    pallas_call x1, Pallas kernels, run_last(): pl.pallas_call(functools.partial(last_kernel, layers), in_specs=[VMEM] *...  7.34 us
    pallas_call x1, Pallas kernels, run_gather(): pl.pallas_call(gather_kernel, in_specs=[VMEM] * 4 + [HBM], out_specs=VMEM...  5.72 us
    ppermute x1, starting transfers between devices, shards(): above_x = lax.ppermute(low_rows, 'gx', [(b, a) for a, b in up])  4.35 us
    pallas_call x1, Pallas kernels, run_spread(): pl.pallas_call(functools.partial(spread_kernel, gy_size, slots), in_specs...  4.28 us
  transfers between devices with their start and end apart: 5, of which 1 were waited for; matrix products, arithmetic and copies ran while one was open for 0% of the time, Pallas kernels for 17%

profile of v7, /device:TPU:1, one launch (start us, length us, event | category | flops | bytes accessed | tf_op | source)
XLA Modules:
  0.0 85.5 jit_solution(4779870920155032704)
XLA Ops:
  0.6 4.3 %spread.1 = (bf16[256,1664]{1,0:T(8,128)(2,1)S(1)}, f32[64,128]{1,0:T(8,128)S(1)}) custom-call(f32[3,8,128]{2,1,0:T(8,128)} %bitcast.6, f32[8]{0:T(128)} %stiff_hbm.1, s32[8,128]{1,0:T(8,128)} %links_hbm.1, s32[8,8]{1,0:T(8,128)} %bitcast.14, s32[8,8]{1,0:T(8,128)} %patch_slots_hbm.1, bf16[8,1024,512]{2,1,0:T(8,128)(2,1)} %bitcast.8), custom_call_target="tpu_custom_call" | custom-call | flops 1000000000 | bytes 9437184 | tf_op jit(solution)/shard_map/spread/pallas_call | solution.py:444
  4.9 1.2 %reshape.31 = bf16[128,2,1664]{2,1,0:T(2,128)(2,1)} reshape(bf16[256,1664]{1,0:T(8,128)(2,1)S(1)} %get-tuple-element.15) | data formatting | bytes 1703936 | tf_op jit(solution)/shard_map/reshape | solution.py:595
  6.1 11.5 %all-to-all-start = ((bf16[128,2,1664]{2,1,0:T(2,128)(2,1)}), bf16[128,2,1664]{2,1,0:T(2,128)(2,1)S(1)}, u32[]{:S(2)}, u32[]{:S(2)}) async-start(bf16[128,2,1664]{2,1,0:T(2,128)(2,1)} %reshape.31), calls=%async_computation | async-start | bytes 1703936 | tf_op jit(solution)/shard_map/all_to_all | solution.py:594
  17.6 2.1 %edges.1 = (f32[8,1024]{1,0:T(8,128)S(1)}, f32[8,1024]{1,0:T(8,128)S(1)}) custom-call(f32[3,1024,512]{2,1,0:T(8,128)} %bitcast.11), custom_call_target="tpu_custom_call" | custom-call | flops 100000000 | bytes 3145728 | tf_op jit(solution)/shard_map/edges/pallas_call | solution.py:472
  19.8 1.1 %collective-permute-start = (f32[8,1024]{1,0:T(8,128)S(1)}, f32[8,1024]{1,0:T(8,128)S(1)}, u32[]{:S(2)}, u32[]{:S(2)}) collective-permute-start(f32[8,1024]{1,0:T(8,128)S(1)} %get-tuple-element.13), channel_id=1, source_target_pairs={{1,0},{2,1},{3,2},{4,3},{5,4},{6,5},{7,6},{0,7},{9,8},{10,9},{11,1... | collective-permute-start | bytes 98312 | tf_op jit(solution)/shard_map/ppermute | solution.py:602
  20.9 0.7 collective-permute-start.1
  21.6 2.0 %lines.1.velocity = f32[3,128,512]{2,1,0:T(8,128)S(1)} custom-call(f32[3,32,32,512]{3,2,1,0:T(8,128)} %velocity.1), custom_call_target="tpu_custom_call" | custom-call | flops 100000000 | bytes 3145728 | tf_op jit(solution)/shard_map/lines/pallas_call | solution.py:487
  23.6 11.1 %all-to-all-done = bf16[128,2,1664]{2,1,0:T(2,128)(2,1)S(1)} async-done(((bf16[128,2,1664]{2,1,0:T(2,128)(2,1)}), bf16[128,2,1664]{2,1,0:T(2,128)(2,1)S(1)}, u32[]{:S(2)}, u32[]{:S(2)}) %all-to-all-start) | async-done | bytes 852000 | tf_op jit(solution)/shard_map/all_to_all | solution.py:594
  34.7 0.3 reshape.32.received
  35.0 0.0 collective-permute-done.ahead
  35.0 0.0 collective-permute-done.1.behind
  35.0 0.7 rim.1
  35.7 0.5 collective-permute-start.2
  36.2 4.4 %collective-permute-start.3 = (bf16[3,2,32,640]{3,2,1,0:T(8,128)(2,1)S(1)}, bf16[3,2,32,640]{3,2,1,0:T(8,128)(2,1)S(1)}, u32[]{:S(2)}, u32[]{:S(2)}) collective-permute-start(bf16[3,2,32,640]{3,2,1,0:T(8,128)(2,1)S(1)} %get-tuple-element.19), channel_id=1, source_target_pairs={{8,0},{16,8},{24,16},{32,24},{40,32},{48,40},{56,48},{64,56},{72,6... | collective-permute-start | bytes 737288 | tf_op jit(solution)/shard_map/ppermute | solution.py:608
  40.6 10.2 %sweep_first.1.u1_in = f32[3,5,1024,128]{3,2,1,0:T(8,128)S(1)} custom-call(f32[3,1024,512]{2,1,0:T(8,128)} %bitcast.12, f32[3,1024,128]{2,1,0:T(8,128)S(1)} %get-tuple-element.16.edges, bf16[256,1664]{1,0:T(8,128)(2,1)S(1)} %reshape.32.received), custom_call_target="tpu_custom_call" | custom-call | flops 2000000000 | bytes 25165824 | tf_op jit(solution)/shard_map/sweep_first/pallas_call | solution.py:522
  50.8 0.0 collective-permute-done.2.below_x
  50.8 0.0 collective-permute-done.3.above_x
  50.8 0.0 copy-start
  50.8 7.3 %sweep_last.1 = (f32[3,1024,512]{2,1,0:T(8,128)}, bf16[256,1536]{1,0:T(8,128)(2,1)S(1)}, f32[3,5,1024,128]{3,2,1,0:T(8,128)S(1)}, bf16[1,1024,512]{2,1,0:T(8,128)(2,1)S(1)}) custom-call(f32[3,5,1024,128]{3,2,1,0:T(8,128)S(1)} %sweep_first.1.u1_in, f32[2,3,5,32,128]{4,3,2,1,0:T(8,128)S(1)} %get-tuple-element.17.rim, ...), custom_call_target="tpu_custom_call", output_to_operand_aliasing={{2}: (0, {})} | custom-call | flops 2000000000 | bytes 16777216 | tf_op jit(solution)/shard_map/sweep_last/pallas_call | solution.py:537
  58.1 0.3 reshape.34
  58.4 21.0 %all_to_all.10 = bf16[128,2,1536]{2,1,0:T(2,128)(2,1)S(1)} all-to-all(bf16[128,2,1536]{2,1,0:T(2,128)(2,1)S(1)} %reshape.34), channel_id=1, replica_groups=mesh['gx'=16,'gy'=8] {'gx','gy'}, dimensions={0} | all-to-all | bytes 1572864 | tf_op jit(solution)/shard_map/all_to_all | solution.py:594
  79.5 0.3 reshape.35.returned
  79.8 0.0 copy-done
  79.8 5.7 %interp.1 = f32[3,8,128]{2,1,0:T(8,128)} custom-call(f32[3,8,128]{2,1,0:T(8,128)S(1)} %bitcast.7, f32[64,128]{1,0:T(8,128)S(1)} %get-tuple-element.21.dest, bf16[256,1536]{1,0:T(8,128)(2,1)S(1)} %reshape.35.returned, bf16[1,1024,512]{2,1,0:T(8,128)(2,1)S(1)} %get-tuple-element.23.near_dw, bf16[8,1024,512]{2,1,0:T(8,128)(2,1)} %bitcast.10), custom_call_target="tpu_custom_call" | custom-call | flops 1000000000 | bytes 9437184 | tf_op jit(solution)/shard_map/interp/pallas_call | solution.py:563
Async XLA Ops:
  6.1 28.5 %all-to-all-start = ((bf16[128,2,1664]{2,1,0:T(2,128)(2,1)}), bf16[128,2,1664]{2,1,0:T(2,128)(2,1)S(1)}, u32[]{:S(2)}, u32[]{:S(2)}) async-start(bf16[128,2,1664]{2,1,0:T(2,128)(2,1)} %reshape.31), calls=%async_computation | async-start | bytes 1703936 | tf_op jit(solution)/shard_map/all_to_all | solution.py:594
  19.8 15.2 %collective-permute-start = (f32[8,1024]{1,0:T(8,128)S(1)}, f32[8,1024]{1,0:T(8,128)S(1)}, u32[]{:S(2)}, u32[]{:S(2)}) collective-permute-start(f32[8,1024]{1,0:T(8,128)S(1)} %get-tuple-element.13), channel_id=1, source_target_pairs={{1,0},{2,1},{3,2},{4,3},{5,4},{6,5},{7,6},{0,7},{9,8},{10,9},{11,1... | collective-permute-start | bytes 98312 | tf_op jit(solution)/shard_map/ppermute | solution.py:602
  20.9 14.2 %collective-permute-start.1 = (f32[8,1024]{1,0:T(8,128)S(1)}, f32[8,1024]{1,0:T(8,128)S(1)}, u32[]{:S(2)}, u32[]{:S(2)}) collective-permute-start(f32[8,1024]{1,0:T(8,128)S(1)} %get-tuple-element.14), channel_id=1, source_target_pairs={{0,1},{1,2},{2,3},{3,4},{4,5},{5,6},{6,7},{7,0},{8,9},{9,10},{10,1... | collective-permute-start | bytes 98312 | tf_op jit(solution)/shard_map/ppermute | solution.py:603
  35.7 15.0 %collective-permute-start.2 = (bf16[3,2,32,640]{3,2,1,0:T(8,128)(2,1)S(1)}, bf16[3,2,32,640]{3,2,1,0:T(8,128)(2,1)S(1)}, u32[]{:S(2)}, u32[]{:S(2)}) collective-permute-start(bf16[3,2,32,640]{3,2,1,0:T(8,128)(2,1)S(1)} %get-tuple-element.18), channel_id=1, source_target_pairs={{0,8},{8,16},{16,24},{24,32},{32,40},{40,48},{48,56},{56,64},{64,7... | collective-permute-start | bytes 737288 | tf_op jit(solution)/shard_map/ppermute | solution.py:607
  36.2 14.5 %collective-permute-start.3 = (bf16[3,2,32,640]{3,2,1,0:T(8,128)(2,1)S(1)}, bf16[3,2,32,640]{3,2,1,0:T(8,128)(2,1)S(1)}, u32[]{:S(2)}, u32[]{:S(2)}) collective-permute-start(bf16[3,2,32,640]{3,2,1,0:T(8,128)(2,1)S(1)} %get-tuple-element.19), channel_id=1, source_target_pairs={{8,0},{16,8},{24,16},{32,24},{40,32},{48,40},{56,48},{64,56},{72,6... | collective-permute-start | bytes 737288 | tf_op jit(solution)/shard_map/ppermute | solution.py:608
  50.8 29.0 %copy-start = (f32[8,3,128]{2,0,1:T(8,128)S(1)}, f32[8,3,128]{2,0,1:T(8,128)}, u32[]{:S(2)}) copy-start(f32[8,3,128]{2,0,1:T(8,128)} %param.8) | copy-start | bytes 36868

commit v8 on v7

--- a/solution.py
+++ b/solution.py
@@ -169,9 +169,11 @@
         return [(row == slot).astype(F32).astype(BF16) for slot in self.slots]
 
     def force(self, chosen, c):
-        here, below, above = chosen
-        main = dot(here, self.received[:, c * self.patch : (c + 1) * self.patch])
-        return force_step * main, force_step * (dot(below, self.tails[c]) + dot(above, self.starts[c]))
+        return force_step * dot(chosen[0], self.received[:, c * self.patch : (c + 1) * self.patch])
+
+    def edges(self, chosen):
+        tails, starts = jnp.concatenate(self.tails, axis=1), jnp.concatenate(self.starts, axis=1)
+        return force_step * (dot(chosen[1], tails) + dot(chosen[2], starts))
 
 
 def rim_kernel(layer_rows, velocity, ahead, behind, received, low_rows, high_rows, rim, edges):
@@ -192,9 +194,10 @@
     row = iota((4 * layers, slots), 0)
     line, z = row // layers, lax.rem(row, layers)
     chosen = arrived.choose(z * layer_rows + jnp.where(line < 2, line, layer_rows - 4 + line))
-    for c in range(3):
-        main, edge = arrived.force(chosen, c)
-        main = velocity[c] + main
+    from_edges = arrived.edges(chosen)
+    for c in range(3):
+        main = velocity[c] + arrived.force(chosen, c)
+        edge = from_edges[:, c * LANES : (c + 1) * LANES]
         for j in range(4):
             at = slice(j * layers, (j + 1) * layers)
             x = j if j < 2 else layer_rows - 4 + j
@@ -293,11 +296,12 @@
         chosen = arrived.choose(iota((part, slots), 0) + step * part)
         for t in range(tiles):
             load(step, t).wait()
+        from_edges = arrived.edges(chosen)
         for c in range(3):
-            main, edge = arrived.force(chosen, c)
+            main = arrived.force(chosen, c)
             for t in range(tiles):
                 u0[c, t, at, :] += main[:, t * LANES : (t + 1) * LANES]
-            u0[c, tiles, at, :] = edges[c, at, :] + edge
+            u0[c, tiles, at, :] = edges[c, at, :] + from_edges[:, c * LANES : (c + 1) * LANES]
 
         @pl.loop(jnp.where(step == 0, 1, 0), jnp.where(step == steps - 1, depth // 2 + 1, depth // 2))
         def _(i):
@@ -312,7 +316,7 @@
     patch, slots = tiles * LANES, received.shape[0]
     sides = beside()
     mask = edge_mask(sides)
-    ahead = pltpu.make_async_copy(dw_hbm.at[pl.ds(0, near_dw.shape[0])], near_dw, sems.at[layers // 8])
+    ahead = pltpu.make_async_copy(dw_hbm.at[pl.ds(0, near_dw.shape[0])], near_dw, sems.at[layers // 4])
     ahead.start()
 
     heads = received[:, 3 * patch :].astype(F32)
@@ -354,7 +358,7 @@
     def store(c, t, here, new):
         fluid[c, here, t * LANES : (t + 1) * LANES] = new
 
-    depth = 8
+    depth = 4
 
     def write(step):
         at = pl.ds(pl.multiple_of(step * depth * rows, depth * rows), depth * rows)
@@ -393,20 +397,21 @@
     pick = (iota((entries, slots), 1) == to).astype(F32).astype(BF16)
     for c in range(3):
         picked[c] = dot(pick, returned[:, c * patch : (c + 1) * patch])
-    k_of_lane = lax.rem(iota((points, LANES), 1), inter)
+    group = iota((inter, inter * points), 0)
+    column = iota((inter, inter * points), 1) // points
 
     def block(b, weights):
         at = pl.ds(pl.multiple_of(b * inter, inter), inter)
         parts = [picked[c, at, :] for c in range(3)]
-        parts.append(jnp.zeros((LANES - 3 * inter, patch), F32))
+        parts.append(jnp.zeros((inter, patch), F32))
         cells = jnp.concatenate(parts, axis=0).astype(BF16)
-        every = lax.dot_general(weights, cells, (((1,), (1,)), ((), ())), preferred_element_type=F32)
-        folded = jnp.zeros((points, LANES), F32)
-        for k in range(inter):
-            folded += jnp.where(k_of_lane == k, every[k * points : (k + 1) * points], 0.0)
-        turned = jnp.transpose(folded)
+        every = lax.dot_general(cells, weights, (((1,), (1,)), ((), ())), preferred_element_type=F32)
         for c in range(3):
-            moved[c, pl.ds(b, 1), :] = jnp.sum(turned[c * inter : (c + 1) * inter], axis=0, keepdims=True)
+            own = jnp.where(group == column, every[c * inter : (c + 1) * inter], 0.0)
+            folded = own[:, :points]
+            for k in range(1, inter):
+                folded = folded + own[:, k * points : (k + 1) * points]
+            moved[c, pl.ds(b, 1), :] = jnp.sum(folded, axis=0, keepdims=True)
 
     @pl.loop(0, near)
     def _(b):
@@ -549,7 +554,7 @@
             pltpu.VMEM((2, 3, 2, count, layers, LANES), F32),
             pltpu.VMEM((3, cells, patch), F32),
             pltpu.VMEM((slots, cells), BF16),
-            pltpu.SemaphoreType.DMA((layers // 8 + 1,)),
+            pltpu.SemaphoreType.DMA((layers // 4 + 1,)),
         ],
         input_output_aliases={0: 2},
         compiler_params=params(34),

time: 85.7 us -> 84.9 us (level)
  Pallas kernels: 32.3 us -> 31.4 us
  transfers between devices with their start and end apart: 5 -> 5, of which waited for: 1 -> 1; matrix products, arithmetic and copies ran while one was open for 0% -> 0% of each run, Pallas kernels for 17% -> 16%
where the time goes in v8:
time: 84.9 us; the launch traced here: 84.6 us
  Pallas kernels  31.4 us (37%)
  blocking collectives  21 us (25%)
  starting transfers between devices  18.1 us (21%)
  waiting for transfers between devices  11.1 us (13%)
  local copies, waits for them, and re-layouts  2.14 us (3%)
    all_to_all x1, blocking collectives, exchange(): lax.all_to_all(rows_out.reshape(devices, 2, size), ('gx', 'gy'), split_ax...  21 us
    all_to_all x1, starting transfers between devices, exchange(): lax.all_to_all(rows_out.reshape(devices, 2, size), ('gx', 'gy'), split_ax...  11.5 us
    all_to_all x1, waiting for transfers between devices, exchange(): lax.all_to_all(rows_out.reshape(devices, 2, size), ('gx', 'gy'), split_ax...  11.1 us
    pallas_call x1, Pallas kernels, run_first(): pl.pallas_call(functools.partial(first_kernel, layers), in_specs=[HBM, VM...  9.76 us
    pallas_call x1, Pallas kernels, run_last(): pl.pallas_call(functools.partial(last_kernel, layers), in_specs=[VMEM] *...  7.24 us
    pallas_call x1, Pallas kernels, run_gather(): pl.pallas_call(gather_kernel, in_specs=[VMEM] * 4 + [HBM], out_specs=VMEM...  5.34 us
    ppermute x1, starting transfers between devices, shards(): above_x = lax.ppermute(low_rows, 'gx', [(b, a) for a, b in up])  4.35 us
    pallas_call x1, Pallas kernels, run_spread(): pl.pallas_call(functools.partial(spread_kernel, gy_size, slots), in_specs...  4.28 us
  transfers between devices with their start and end apart: 5, of which 1 were waited for; matrix products, arithmetic and copies ran while one was open for 0% of the time, Pallas kernels for 16%

profile of v8, /device:TPU:1, one launch (start us, length us, event | category | flops | bytes accessed | tf_op | source)
XLA Modules:
  0.0 84.6 jit_solution(17017596892452661913)
XLA Ops:
  0.6 4.3 %spread.1 = (bf16[256,1664]{1,0:T(8,128)(2,1)S(1)}, f32[64,128]{1,0:T(8,128)S(1)}) custom-call(f32[3,8,128]{2,1,0:T(8,128)} %bitcast.6, f32[8]{0:T(128)} %stiff_hbm.1, s32[8,128]{1,0:T(8,128)} %links_hbm.1, s32[8,8]{1,0:T(8,128)} %bitcast.14, s32[8,8]{1,0:T(8,128)} %patch_slots_hbm.1, bf16[8,1024,512]{2,1,0:T(8,128)(2,1)} %bitcast.8), custom_call_target="tpu_custom_call" | custom-call | flops 1000000000 | bytes 9437184 | tf_op jit(solution)/shard_map/spread/pallas_call | solution.py:449
  4.9 1.2 %reshape.31 = bf16[128,2,1664]{2,1,0:T(2,128)(2,1)} reshape(bf16[256,1664]{1,0:T(8,128)(2,1)S(1)} %get-tuple-element.15) | data formatting | bytes 1703936 | tf_op jit(solution)/shard_map/reshape | solution.py:600
  6.1 11.5 %all-to-all-start = ((bf16[128,2,1664]{2,1,0:T(2,128)(2,1)}), bf16[128,2,1664]{2,1,0:T(2,128)(2,1)S(1)}, u32[]{:S(2)}, u32[]{:S(2)}) async-start(bf16[128,2,1664]{2,1,0:T(2,128)(2,1)} %reshape.31), calls=%async_computation | async-start | bytes 1703936 | tf_op jit(solution)/shard_map/all_to_all | solution.py:599
  17.6 2.1 %edges.1 = (f32[8,1024]{1,0:T(8,128)S(1)}, f32[8,1024]{1,0:T(8,128)S(1)}) custom-call(f32[3,1024,512]{2,1,0:T(8,128)} %bitcast.11), custom_call_target="tpu_custom_call" | custom-call | flops 100000000 | bytes 3145728 | tf_op jit(solution)/shard_map/edges/pallas_call | solution.py:477
  19.8 1.1 %collective-permute-start = (f32[8,1024]{1,0:T(8,128)S(1)}, f32[8,1024]{1,0:T(8,128)S(1)}, u32[]{:S(2)}, u32[]{:S(2)}) collective-permute-start(f32[8,1024]{1,0:T(8,128)S(1)} %get-tuple-element.13), channel_id=1, source_target_pairs={{1,0},{2,1},{3,2},{4,3},{5,4},{6,5},{7,6},{0,7},{9,8},{10,9},{11,1... | collective-permute-start | bytes 98312 | tf_op jit(solution)/shard_map/ppermute | solution.py:607
  20.9 0.7 collective-permute-start.1
  21.6 2.0 %lines.1.velocity = f32[3,128,512]{2,1,0:T(8,128)S(1)} custom-call(f32[3,32,32,512]{3,2,1,0:T(8,128)} %velocity.1), custom_call_target="tpu_custom_call" | custom-call | flops 100000000 | bytes 3145728 | tf_op jit(solution)/shard_map/lines/pallas_call | solution.py:492
  23.6 11.1 %all-to-all-done = bf16[128,2,1664]{2,1,0:T(2,128)(2,1)S(1)} async-done(((bf16[128,2,1664]{2,1,0:T(2,128)(2,1)}), bf16[128,2,1664]{2,1,0:T(2,128)(2,1)S(1)}, u32[]{:S(2)}, u32[]{:S(2)}) %all-to-all-start) | async-done | bytes 852000 | tf_op jit(solution)/shard_map/all_to_all | solution.py:599
  34.7 0.3 reshape.32.received
  35.0 0.0 collective-permute-done.ahead
  35.0 0.0 collective-permute-done.1.behind
  35.0 0.7 rim.1
  35.7 0.5 collective-permute-start.2
  36.2 4.3 %collective-permute-start.3 = (bf16[3,2,32,640]{3,2,1,0:T(8,128)(2,1)S(1)}, bf16[3,2,32,640]{3,2,1,0:T(8,128)(2,1)S(1)}, u32[]{:S(2)}, u32[]{:S(2)}) collective-permute-start(bf16[3,2,32,640]{3,2,1,0:T(8,128)(2,1)S(1)} %get-tuple-element.19), channel_id=1, source_target_pairs={{8,0},{16,8},{24,16},{32,24},{40,32},{48,40},{56,48},{64,56},{72,6... | collective-permute-start | bytes 737288 | tf_op jit(solution)/shard_map/ppermute | solution.py:613
  40.6 9.8 %sweep_first.1.u1_in = f32[3,5,1024,128]{3,2,1,0:T(8,128)S(1)} custom-call(f32[3,1024,512]{2,1,0:T(8,128)} %bitcast.12, f32[3,1024,128]{2,1,0:T(8,128)S(1)} %get-tuple-element.16.edges, bf16[256,1664]{1,0:T(8,128)(2,1)S(1)} %reshape.32.received), custom_call_target="tpu_custom_call" | custom-call | flops 2000000000 | bytes 25165824 | tf_op jit(solution)/shard_map/sweep_first/pallas_call | solution.py:527
  50.4 0.0 collective-permute-done.2.below_x
  50.4 0.0 collective-permute-done.3.above_x
  50.4 0.0 copy-start
  50.4 7.2 %sweep_last.1 = (f32[3,1024,512]{2,1,0:T(8,128)}, bf16[256,1536]{1,0:T(8,128)(2,1)S(1)}, f32[3,5,1024,128]{3,2,1,0:T(8,128)S(1)}, bf16[1,1024,512]{2,1,0:T(8,128)(2,1)S(1)}) custom-call(f32[3,5,1024,128]{3,2,1,0:T(8,128)S(1)} %sweep_first.1.u1_in, f32[2,3,5,32,128]{4,3,2,1,0:T(8,128)S(1)} %get-tuple-element.17.rim, ...), custom_call_target="tpu_custom_call", output_to_operand_aliasing={{2}: (0, {})} | custom-call | flops 2000000000 | bytes 16777216 | tf_op jit(solution)/shard_map/sweep_last/pallas_call | solution.py:542
  57.6 0.3 reshape.34
  57.9 21.0 %all_to_all.10 = bf16[128,2,1536]{2,1,0:T(2,128)(2,1)S(1)} all-to-all(bf16[128,2,1536]{2,1,0:T(2,128)(2,1)S(1)} %reshape.34), channel_id=1, replica_groups=mesh['gx'=16,'gy'=8] {'gx','gy'}, dimensions={0} | all-to-all | bytes 1572864 | tf_op jit(solution)/shard_map/all_to_all | solution.py:599
  79.0 0.3 reshape.35.returned
  79.3 0.0 copy-done
  79.3 5.3 %interp.1 = f32[3,8,128]{2,1,0:T(8,128)} custom-call(f32[3,8,128]{2,1,0:T(8,128)S(1)} %bitcast.7, f32[64,128]{1,0:T(8,128)S(1)} %get-tuple-element.21.dest, bf16[256,1536]{1,0:T(8,128)(2,1)S(1)} %reshape.35.returned, bf16[1,1024,512]{2,1,0:T(8,128)(2,1)S(1)} %get-tuple-element.23.near_dw, bf16[8,1024,512]{2,1,0:T(8,128)(2,1)} %bitcast.10), custom_call_target="tpu_custom_call" | custom-call | flops 1000000000 | bytes 9437184 | tf_op jit(solution)/shard_map/interp/pallas_call | solution.py:568
Async XLA Ops:
  6.1 28.5 %all-to-all-start = ((bf16[128,2,1664]{2,1,0:T(2,128)(2,1)}), bf16[128,2,1664]{2,1,0:T(2,128)(2,1)S(1)}, u32[]{:S(2)}, u32[]{:S(2)}) async-start(bf16[128,2,1664]{2,1,0:T(2,128)(2,1)} %reshape.31), calls=%async_computation | async-start | bytes 1703936 | tf_op jit(solution)/shard_map/all_to_all | solution.py:599
  19.8 15.2 %collective-permute-start = (f32[8,1024]{1,0:T(8,128)S(1)}, f32[8,1024]{1,0:T(8,128)S(1)}, u32[]{:S(2)}, u32[]{:S(2)}) collective-permute-start(f32[8,1024]{1,0:T(8,128)S(1)} %get-tuple-element.13), channel_id=1, source_target_pairs={{1,0},{2,1},{3,2},{4,3},{5,4},{6,5},{7,6},{0,7},{9,8},{10,9},{11,1... | collective-permute-start | bytes 98312 | tf_op jit(solution)/shard_map/ppermute | solution.py:607
  20.9 14.2 %collective-permute-start.1 = (f32[8,1024]{1,0:T(8,128)S(1)}, f32[8,1024]{1,0:T(8,128)S(1)}, u32[]{:S(2)}, u32[]{:S(2)}) collective-permute-start(f32[8,1024]{1,0:T(8,128)S(1)} %get-tuple-element.14), channel_id=1, source_target_pairs={{0,1},{1,2},{2,3},{3,4},{4,5},{5,6},{6,7},{7,0},{8,9},{9,10},{10,1... | collective-permute-start | bytes 98312 | tf_op jit(solution)/shard_map/ppermute | solution.py:608
  35.7 14.6 %collective-permute-start.2 = (bf16[3,2,32,640]{3,2,1,0:T(8,128)(2,1)S(1)}, bf16[3,2,32,640]{3,2,1,0:T(8,128)(2,1)S(1)}, u32[]{:S(2)}, u32[]{:S(2)}) collective-permute-start(bf16[3,2,32,640]{3,2,1,0:T(8,128)(2,1)S(1)} %get-tuple-element.18), channel_id=1, source_target_pairs={{0,8},{8,16},{16,24},{24,32},{32,40},{40,48},{48,56},{56,64},{64,7... | collective-permute-start | bytes 737288 | tf_op jit(solution)/shard_map/ppermute | solution.py:612
  36.2 14.1 %collective-permute-start.3 = (bf16[3,2,32,640]{3,2,1,0:T(8,128)(2,1)S(1)}, bf16[3,2,32,640]{3,2,1,0:T(8,128)(2,1)S(1)}, u32[]{:S(2)}, u32[]{:S(2)}) collective-permute-start(bf16[3,2,32,640]{3,2,1,0:T(8,128)(2,1)S(1)} %get-tuple-element.19), channel_id=1, source_target_pairs={{8,0},{16,8},{24,16},{32,24},{40,32},{48,40},{56,48},{64,56},{72,6... | collective-permute-start | bytes 737288 | tf_op jit(solution)/shard_map/ppermute | solution.py:613
  50.4 28.9 %copy-start = (f32[8,3,128]{2,0,1:T(8,128)S(1)}, f32[8,3,128]{2,0,1:T(8,128)}, u32[]{:S(2)}) copy-start(f32[8,3,128]{2,0,1:T(8,128)} %param.8) | copy-start | bytes 36868

commit v9 on v8

--- a/solution.py
+++ b/solution.py
@@ -173,12 +173,15 @@
 
     def edges(self, chosen):
         tails, starts = jnp.concatenate(self.tails, axis=1), jnp.concatenate(self.starts, axis=1)
-        return force_step * (dot(chosen[1], tails) + dot(chosen[2], starts))
+        both = jnp.concatenate([tails, starts], axis=0)
+        return force_step * dot(jnp.concatenate([chosen[1], chosen[2]], axis=1), both)
 
 
 def rim_kernel(layer_rows, velocity, ahead, behind, received, low_rows, high_rows, rim, edges):
-    layers, patch = low_rows.shape[2], velocity.shape[2]
-    slots, cells = received.shape[0], ahead.shape[1]
+    layers, patch = low_rows.shape[1], velocity.shape[2]
+    slots, cells, tiles = received.shape[0], ahead.shape[1], patch // LANES
+    corners = [0.0, 0.0]
+    z_lane = iota((layers, LANES), 1)
 
     sides = beside()
     from_ahead = jnp.where(sides[3] > 0.0, ahead[...], 0.0)
@@ -203,12 +206,16 @@
             x = j if j < 2 else layer_rows - 4 + j
             side = edges[c, pl.ds(x, layers, stride=layer_rows), :] + edge[at]
             to = low_rows if j < 2 else high_rows
-            to[c, j % 2, :, :patch] = main[at].astype(BF16)
-            to[c, j % 2, :, patch:] = side.astype(BF16)
+            for t in range(tiles):
+                to[(c * 2 + j % 2) * tiles + t] = main[at, t * LANES : (t + 1) * LANES].astype(BF16)
             if j in (0, 3):
-                for t in range(patch // LANES):
+                for t in range(tiles):
                     rim[j // 3, c, t] = main[at, t * LANES : (t + 1) * LANES]
-                rim[j // 3, c, patch // LANES] = side
+                rim[j // 3, c, tiles] = side
+                corners[j // 3] += jnp.where(z_lane == 2 * c, pltpu.roll(side, 2 * c, axis=1), 0.0)
+                corners[j // 3] += jnp.where(z_lane == 2 * c + 1, pltpu.roll(side, 2 * c + 2, axis=1), 0.0)
+    low_rows[6 * tiles] = corners[0].astype(BF16)
+    high_rows[6 * tiles] = corners[1].astype(BF16)
 
 
 def update(centre, weights, c, east, west, north, south, up, down):
@@ -328,13 +335,20 @@
         for c in range(3):
             for j in range(2):
                 for t in range(count):
-                    arrived = source[c, j, :, t * LANES : (t + 1) * LANES].astype(F32)
+                    if t < tiles:
+                        arrived = source[(c * 2 + j) * tiles + t].astype(F32)
+                    elif j == 1 - side:
+                        corner = source[6 * tiles].astype(F32)
+                        lane = iota(corner.shape, 1)
+                        arrived = jnp.where(lane == 0, pltpu.roll(corner, (LANES - 2 * c) % LANES, axis=1), 0.0)
+                        arrived += jnp.where(lane == LANES - 1, pltpu.roll(corner, LANES - 2 - 2 * c, axis=1), 0.0)
+                    else:
+                        continue
                     halo[side, c, j, t] = jnp.where(sides[side] > 0.0, arrived, 0.0)
     for side in range(2):
         near, row = 1 - side, (rows - 1) * side
         slope = -transport_rate if side else transport_rate
         for t in range(count):
-            scale = sides[side] * mask if t == tiles else sides[side]
             for g in range(0, layers, 8):
                 at = slice(g, g + 8)
                 after, before = (g + 8) % layers, (g - 8) % layers
@@ -343,14 +357,15 @@
                 own = viscosity + slope * rim[side, 0, t, at, :]
                 for c in range(3):
                     v = centre[c]
-                    plane = halo.at[side, c, near]
-                    inner, outer = rim[side, c, t, at, :], halo[side, c, side, t, at, :]
-                    east, west = (outer, inner) if side else (inner, outer)
-                    north, south = shifted(v, plane[(t + 1) % count, at, :], plane[(t - 1) % count, at, :], 1)
-                    up, down = shifted(v, plane[t, after : after + 8, :], plane[t, before : before + 8, :], 0)
-                    mid[side, c, t, at, :] = scale * update(
-                        centre, weights, c, east, west, north, south, up, down
-                    )
+                    if t < tiles:
+                        plane = halo.at[side, c, near]
+                        inner, outer = rim[side, c, t, at, :], halo[side, c, side, t, at, :]
+                        east, west = (outer, inner) if side else (inner, outer)
+                        north, south = shifted(v, plane[(t + 1) % count, at, :], plane[(t - 1) % count, at, :], 1)
+                        up, down = shifted(v, plane[t, after : after + 8, :], plane[t, before : before + 8, :], 0)
+                        mid[side, c, t, at, :] = sides[side] * update(
+                            centre, weights, c, east, west, north, south, up, down
+                        )
                     term = own * v
                     strided = pl.ds(g * rows + row, 8, stride=rows)
                     u1[c, t, strided, :] += term * mask if t == tiles else term
@@ -503,8 +518,7 @@
 
 def run_rim(layer_rows, layers, rim_velocity, ahead, behind, received):
     patch, cells = rim_velocity.shape[2], ahead.shape[1]
-    wide = patch + LANES
-    side = (3, 2, layers, wide)
+    side = (6 * (patch // LANES) + 1, layers, LANES)
     return pl.pallas_call(
         functools.partial(rim_kernel, layer_rows),
         in_specs=[VMEM] * 4,
@@ -512,7 +526,7 @@
         out_shape=[
             jax.ShapeDtypeStruct(side, BF16),
             jax.ShapeDtypeStruct(side, BF16),
-            jax.ShapeDtypeStruct((2, 3, wide // LANES, layers, LANES), F32),
+            jax.ShapeDtypeStruct((2, 3, patch // LANES + 1, layers, LANES), F32),
             jax.ShapeDtypeStruct((3, cells, LANES), F32),
         ],
         compiler_params=params(24),
@@ -550,7 +564,7 @@
             jax.ShapeDtypeStruct((near, *dw.shape[1:]), BF16),
         ],
         scratch_shapes=[
-            pltpu.VMEM((2, 3, count, layers, LANES), F32),
+            pltpu.VMEM((2, 3, count - 1, layers, LANES), F32),
             pltpu.VMEM((2, 3, 2, count, layers, LANES), F32),
             pltpu.VMEM((3, cells, patch), F32),
             pltpu.VMEM((slots, cells), BF16),

time: 84.9 us -> 84.9 us (level)
  no operation moved by 1% of the time
where the time goes in v9:
time: 84.9 us; the launch traced here: 84.6 us
  Pallas kernels  31.4 us (37%)
  blocking collectives  21 us (25%)
  starting transfers between devices  18.1 us (21%)
  waiting for transfers between devices  11.1 us (13%)
  local copies, waits for them, and re-layouts  2.14 us (3%)
    all_to_all x1, blocking collectives, exchange(): lax.all_to_all(rows_out.reshape(devices, 2, size), ('gx', 'gy'), split_ax...  21 us
    all_to_all x1, starting transfers between devices, exchange(): lax.all_to_all(rows_out.reshape(devices, 2, size), ('gx', 'gy'), split_ax...  11.5 us
    all_to_all x1, waiting for transfers between devices, exchange(): lax.all_to_all(rows_out.reshape(devices, 2, size), ('gx', 'gy'), split_ax...  11.1 us
    pallas_call x1, Pallas kernels, run_first(): pl.pallas_call(functools.partial(first_kernel, layers), in_specs=[HBM, VM...  9.76 us
    pallas_call x1, Pallas kernels, run_last(): pl.pallas_call(functools.partial(last_kernel, layers), in_specs=[VMEM] *...  7.22 us
    pallas_call x1, Pallas kernels, run_gather(): pl.pallas_call(gather_kernel, in_specs=[VMEM] * 4 + [HBM], out_specs=VMEM...  5.33 us
    ppermute x1, starting transfers between devices, shards(): above_x = lax.ppermute(low_rows, 'gx', [(b, a) for a, b in up])  4.34 us
    pallas_call x1, Pallas kernels, run_spread(): pl.pallas_call(functools.partial(spread_kernel, gy_size, slots), in_specs...  4.28 us
  transfers between devices with their start and end apart: 5, of which 1 were waited for; matrix products, arithmetic and copies ran while one was open for 0% of the time, Pallas kernels for 16%

profile of v9, /device:TPU:1, one launch (start us, length us, event | category | flops | bytes accessed | tf_op | source)
XLA Modules:
  0.0 84.6 jit_solution(17613640847105309402)
XLA Ops:
  0.6 4.3 %spread.1 = (bf16[256,1664]{1,0:T(8,128)(2,1)S(1)}, f32[64,128]{1,0:T(8,128)S(1)}) custom-call(f32[3,8,128]{2,1,0:T(8,128)} %bitcast.6, f32[8]{0:T(128)} %stiff_hbm.1, s32[8,128]{1,0:T(8,128)} %links_hbm.1, s32[8,8]{1,0:T(8,128)} %bitcast.14, s32[8,8]{1,0:T(8,128)} %patch_slots_hbm.1, bf16[8,1024,512]{2,1,0:T(8,128)(2,1)} %bitcast.8), custom_call_target="tpu_custom_call" | custom-call | flops 1000000000 | bytes 9437184 | tf_op jit(solution)/shard_map/spread/pallas_call | solution.py:464
  4.9 1.2 %reshape.31 = bf16[128,2,1664]{2,1,0:T(2,128)(2,1)} reshape(bf16[256,1664]{1,0:T(8,128)(2,1)S(1)} %get-tuple-element.15) | data formatting | bytes 1703936 | tf_op jit(solution)/shard_map/reshape | solution.py:614
  6.1 11.5 %all-to-all-start = ((bf16[128,2,1664]{2,1,0:T(2,128)(2,1)}), bf16[128,2,1664]{2,1,0:T(2,128)(2,1)S(1)}, u32[]{:S(2)}, u32[]{:S(2)}) async-start(bf16[128,2,1664]{2,1,0:T(2,128)(2,1)} %reshape.31), calls=%async_computation | async-start | bytes 1703936 | tf_op jit(solution)/shard_map/all_to_all | solution.py:613
  17.6 2.1 %edges.1 = (f32[8,1024]{1,0:T(8,128)S(1)}, f32[8,1024]{1,0:T(8,128)S(1)}) custom-call(f32[3,1024,512]{2,1,0:T(8,128)} %bitcast.11), custom_call_target="tpu_custom_call" | custom-call | flops 100000000 | bytes 3145728 | tf_op jit(solution)/shard_map/edges/pallas_call | solution.py:492
  19.8 1.1 %collective-permute-start = (f32[8,1024]{1,0:T(8,128)S(1)}, f32[8,1024]{1,0:T(8,128)S(1)}, u32[]{:S(2)}, u32[]{:S(2)}) collective-permute-start(f32[8,1024]{1,0:T(8,128)S(1)} %get-tuple-element.13), channel_id=1, source_target_pairs={{1,0},{2,1},{3,2},{4,3},{5,4},{6,5},{7,6},{0,7},{9,8},{10,9},{11,1... | collective-permute-start | bytes 98312 | tf_op jit(solution)/shard_map/ppermute | solution.py:621
  20.9 0.7 collective-permute-start.1
  21.6 2.0 %lines.1.velocity = f32[3,128,512]{2,1,0:T(8,128)S(1)} custom-call(f32[3,32,32,512]{3,2,1,0:T(8,128)} %velocity.1), custom_call_target="tpu_custom_call" | custom-call | flops 100000000 | bytes 3145728 | tf_op jit(solution)/shard_map/lines/pallas_call | solution.py:507
  23.6 11.1 %all-to-all-done = bf16[128,2,1664]{2,1,0:T(2,128)(2,1)S(1)} async-done(((bf16[128,2,1664]{2,1,0:T(2,128)(2,1)}), bf16[128,2,1664]{2,1,0:T(2,128)(2,1)S(1)}, u32[]{:S(2)}, u32[]{:S(2)}) %all-to-all-start) | async-done | bytes 852000 | tf_op jit(solution)/shard_map/all_to_all | solution.py:613
  34.7 0.3 reshape.32.received
  35.0 0.0 collective-permute-done.ahead
  35.0 0.0 collective-permute-done.1.behind
  35.0 0.7 rim.1
  35.7 0.5 collective-permute-start.2
  36.2 4.3 %collective-permute-start.3 = (bf16[25,32,128]{2,1,0:T(8,128)(2,1)S(1)}, bf16[25,32,128]{2,1,0:T(8,128)(2,1)S(1)}, u32[]{:S(2)}, u32[]{:S(2)}) collective-permute-start(bf16[25,32,128]{2,1,0:T(8,128)(2,1)S(1)} %get-tuple-element.19), channel_id=1, source_target_pairs={{8,0},{16,8},{24,16},{32,24},{40,32},{48,40},{56,48},{64,56},{72,6... | collective-permute-start | bytes 614408 | tf_op jit(solution)/shard_map/ppermute | solution.py:627
  40.6 9.8 %sweep_first.1.u1_in = f32[3,5,1024,128]{3,2,1,0:T(8,128)S(1)} custom-call(f32[3,1024,512]{2,1,0:T(8,128)} %bitcast.12, f32[3,1024,128]{2,1,0:T(8,128)S(1)} %get-tuple-element.16.edges, bf16[256,1664]{1,0:T(8,128)(2,1)S(1)} %reshape.32.received), custom_call_target="tpu_custom_call" | custom-call | flops 2000000000 | bytes 25165824 | tf_op jit(solution)/shard_map/sweep_first/pallas_call | solution.py:541
  50.4 0.0 collective-permute-done.2.below_x
  50.4 0.0 collective-permute-done.3.above_x
  50.4 0.0 copy-start
  50.4 7.2 %sweep_last.1 = (f32[3,1024,512]{2,1,0:T(8,128)}, bf16[256,1536]{1,0:T(8,128)(2,1)S(1)}, f32[3,5,1024,128]{3,2,1,0:T(8,128)S(1)}, bf16[1,1024,512]{2,1,0:T(8,128)(2,1)S(1)}) custom-call(f32[3,5,1024,128]{3,2,1,0:T(8,128)S(1)} %sweep_first.1.u1_in, f32[2,3,5,32,128]{4,3,2,1,0:T(8,128)S(1)} %get-tuple-element.17.rim, ...), custom_call_target="tpu_custom_call", output_to_operand_aliasing={{2}: (0, {})} | custom-call | flops 2000000000 | bytes 16777216 | tf_op jit(solution)/shard_map/sweep_last/pallas_call | solution.py:556
  57.6 0.3 reshape.34
  57.9 21.0 %all_to_all.10 = bf16[128,2,1536]{2,1,0:T(2,128)(2,1)S(1)} all-to-all(bf16[128,2,1536]{2,1,0:T(2,128)(2,1)S(1)} %reshape.34), channel_id=1, replica_groups=mesh['gx'=16,'gy'=8] {'gx','gy'}, dimensions={0} | all-to-all | bytes 1572864 | tf_op jit(solution)/shard_map/all_to_all | solution.py:613
  79.0 0.3 reshape.35.returned
  79.3 0.0 copy-done
  79.3 5.3 %interp.1 = f32[3,8,128]{2,1,0:T(8,128)} custom-call(f32[3,8,128]{2,1,0:T(8,128)S(1)} %bitcast.7, f32[64,128]{1,0:T(8,128)S(1)} %get-tuple-element.21.dest, bf16[256,1536]{1,0:T(8,128)(2,1)S(1)} %reshape.35.returned, bf16[1,1024,512]{2,1,0:T(8,128)(2,1)S(1)} %get-tuple-element.23.near_dw, bf16[8,1024,512]{2,1,0:T(8,128)(2,1)} %bitcast.10), custom_call_target="tpu_custom_call" | custom-call | flops 1000000000 | bytes 9437184 | tf_op jit(solution)/shard_map/interp/pallas_call | solution.py:582
Async XLA Ops:
  6.1 28.5 %all-to-all-start = ((bf16[128,2,1664]{2,1,0:T(2,128)(2,1)}), bf16[128,2,1664]{2,1,0:T(2,128)(2,1)S(1)}, u32[]{:S(2)}, u32[]{:S(2)}) async-start(bf16[128,2,1664]{2,1,0:T(2,128)(2,1)} %reshape.31), calls=%async_computation | async-start | bytes 1703936 | tf_op jit(solution)/shard_map/all_to_all | solution.py:613
  19.8 15.2 %collective-permute-start = (f32[8,1024]{1,0:T(8,128)S(1)}, f32[8,1024]{1,0:T(8,128)S(1)}, u32[]{:S(2)}, u32[]{:S(2)}) collective-permute-start(f32[8,1024]{1,0:T(8,128)S(1)} %get-tuple-element.13), channel_id=1, source_target_pairs={{1,0},{2,1},{3,2},{4,3},{5,4},{6,5},{7,6},{0,7},{9,8},{10,9},{11,1... | collective-permute-start | bytes 98312 | tf_op jit(solution)/shard_map/ppermute | solution.py:621
  20.9 14.2 %collective-permute-start.1 = (f32[8,1024]{1,0:T(8,128)S(1)}, f32[8,1024]{1,0:T(8,128)S(1)}, u32[]{:S(2)}, u32[]{:S(2)}) collective-permute-start(f32[8,1024]{1,0:T(8,128)S(1)} %get-tuple-element.14), channel_id=1, source_target_pairs={{0,1},{1,2},{2,3},{3,4},{4,5},{5,6},{6,7},{7,0},{8,9},{9,10},{10,1... | collective-permute-start | bytes 98312 | tf_op jit(solution)/shard_map/ppermute | solution.py:622
  35.7 14.6 %collective-permute-start.2 = (bf16[25,32,128]{2,1,0:T(8,128)(2,1)S(1)}, bf16[25,32,128]{2,1,0:T(8,128)(2,1)S(1)}, u32[]{:S(2)}, u32[]{:S(2)}) collective-permute-start(bf16[25,32,128]{2,1,0:T(8,128)(2,1)S(1)} %get-tuple-element.18), channel_id=1, source_target_pairs={{0,8},{8,16},{16,24},{24,32},{32,40},{40,48},{48,56},{56,64},{64,7... | collective-permute-start | bytes 614408 | tf_op jit(solution)/shard_map/ppermute | solution.py:626
  36.2 14.1 %collective-permute-start.3 = (bf16[25,32,128]{2,1,0:T(8,128)(2,1)S(1)}, bf16[25,32,128]{2,1,0:T(8,128)(2,1)S(1)}, u32[]{:S(2)}, u32[]{:S(2)}) collective-permute-start(bf16[25,32,128]{2,1,0:T(8,128)(2,1)S(1)} %get-tuple-element.19), channel_id=1, source_target_pairs={{8,0},{16,8},{24,16},{32,24},{40,32},{48,40},{56,48},{64,56},{72,6... | collective-permute-start | bytes 614408 | tf_op jit(solution)/shard_map/ppermute | solution.py:627
  50.4 28.9 %copy-start = (f32[8,3,128]{2,0,1:T(8,128)S(1)}, f32[8,3,128]{2,0,1:T(8,128)}, u32[]{:S(2)}) copy-start(f32[8,3,128]{2,0,1:T(8,128)} %param.8) | copy-start | bytes 36868

commit v10 on v9

--- a/solution.py
+++ b/solution.py
@@ -273,7 +273,7 @@
                     store(c, t, here, update(centre, weights, c, east, west, north, south, above, below))
 
 
-def first_kernel(layers, velocity, edges, received, u1, u0, sems):
+def place_kernel(layers, velocity, edges, received, low_in, u0, low_rows, sems):
     count, cells = u0.shape[1:3]
     rows, tiles = cells // layers, count - 1
     depth, slots = 8, received.shape[0]
@@ -289,13 +289,7 @@
         for t in range(tiles):
             load(step, t).start()
     arrived = Arrived(received, tiles * LANES)
-    mask = edge_mask(beside())
-
-    def store(c, t, here, new):
-        u1[c, t, here, :] = new * mask if t == tiles else new
-
-    def nothing(c, t, z):
-        return 0.0
+    low_rows[...] = low_in[...]
 
     @pl.loop(0, steps)
     def _(step):
@@ -310,9 +304,20 @@
                 u0[c, t, at, :] += main[:, t * LANES : (t + 1) * LANES]
             u0[c, tiles, at, :] = edges[c, at, :] + from_edges[:, c * LANES : (c + 1) * LANES]
 
-        @pl.loop(jnp.where(step == 0, 1, 0), jnp.where(step == steps - 1, depth // 2 + 1, depth // 2))
-        def _(i):
-            sweep_pair(u0, layers, step * depth - 1 + 2 * i, nothing, nothing, store, count)
+
+def first_kernel(layers, u0, u1):
+    count = u0.shape[1]
+    mask = edge_mask(beside())
+
+    def store(c, t, here, new):
+        u1[c, t, here, :] = new * mask if t == count - 1 else new
+
+    def nothing(c, t, z):
+        return 0.0
+
+    @pl.loop(0, layers // 2)
+    def _(i):
+        sweep_pair(u0, layers, 2 * i, nothing, nothing, store, count)
 
 
 def last_kernel(
@@ -535,19 +540,33 @@
     )(rim_velocity, ahead, behind, received)
 
 
-def run_first(layers, velocity, edge, received):
+def run_place(layers, velocity, edge, received, low_rows):
     cells, patch = velocity.shape[1:]
-    block = (3, patch // LANES + 1, cells, LANES)
+    return pl.pallas_call(
+        functools.partial(place_kernel, layers),
+        in_specs=[HBM, VMEM, VMEM, VMEM],
+        out_specs=[VMEM, VMEM],
+        out_shape=[
+            jax.ShapeDtypeStruct((3, patch // LANES + 1, cells, LANES), F32),
+            jax.ShapeDtypeStruct(low_rows.shape, BF16),
+        ],
+        scratch_shapes=[pltpu.SemaphoreType.DMA((layers // 8 * (patch // LANES),))],
+        compiler_params=params(24),
+        cost_estimate=cost(10**9, 8),
+        name="place",
+    )(in_hbm(velocity), edge, received, low_rows)
+
+
+def run_first(layers, u0):
     return pl.pallas_call(
         functools.partial(first_kernel, layers),
-        in_specs=[HBM, VMEM, VMEM],
+        in_specs=[VMEM],
         out_specs=VMEM,
-        out_shape=jax.ShapeDtypeStruct(block, F32),
-        scratch_shapes=[pltpu.VMEM(block, F32), pltpu.SemaphoreType.DMA((layers // 8 * (patch // LANES),))],
+        out_shape=jax.ShapeDtypeStruct(u0.shape, F32),
         compiler_params=params(24),
         cost_estimate=cost(2 * 10**9, 24),
         name="sweep_first",
-    )(in_hbm(velocity), edge, received)
+    )(u0)
 
 
 def run_last(layers, near, u1, rim, below_x, above_x, received, dw):
@@ -624,8 +643,9 @@
 
     up = [(i, (i + 1) % gx_size) for i in range(gx_size)]
     below_x = lax.ppermute(high_rows, "gx", up)
+    u0, low_rows = run_place(layers, flat, edge, received, low_rows)
     above_x = lax.ppermute(low_rows, "gx", [(b, a) for a, b in up])
-    u1 = run_first(layers, flat, edge, received)
+    u1 = run_first(layers, u0)
     fluid, replies, _, near_dw = run_last(layers, NEAR, u1, rim, below_x, above_x, received, dw)
     moved = run_gather(pts, dest, exchange(replies), near_dw, dw)
     return fluid.reshape(3, layers, rows, columns), moved.transpose(1, 0, 2)

time: 84.9 us -> 85.9 us (1.012)
    pallas_call x1 -> x2, Pallas kernels: 9.76 us -> 10 us  [the longest x1 6.47 us: run_first(): pl.pallas_call(functools.partial(first_kernel, layers), in_specs=[VMEM],...]
  transfers between devices with their start and end apart: 5 -> 5, of which waited for: 1 -> 1; matrix products, arithmetic and copies ran while one was open for 0% -> 0% of each run, Pallas kernels for 16% -> 17%
where the time goes in v10:
time: 85.9 us; the launch traced here: 85.7 us
  Pallas kernels  31.7 us (37%)
  blocking collectives  21.8 us (25%)
  starting transfers between devices  18.2 us (21%)
  waiting for transfers between devices  11.1 us (13%)
  local copies, waits for them, and re-layouts  2.14 us (2%)
    all_to_all x1, blocking collectives, exchange(): lax.all_to_all(rows_out.reshape(devices, 2, size), ('gx', 'gy'), split_ax...  21.8 us
    all_to_all x1, starting transfers between devices, exchange(): lax.all_to_all(rows_out.reshape(devices, 2, size), ('gx', 'gy'), split_ax...  11.5 us
    all_to_all x1, waiting for transfers between devices, exchange(): lax.all_to_all(rows_out.reshape(devices, 2, size), ('gx', 'gy'), split_ax...  11.1 us
    pallas_call x1, Pallas kernels, run_last(): pl.pallas_call(functools.partial(last_kernel, layers), in_specs=[VMEM] *...  7.22 us
    pallas_call x1, Pallas kernels, run_first(): pl.pallas_call(functools.partial(first_kernel, layers), in_specs=[VMEM],...  6.47 us
    pallas_call x1, Pallas kernels, run_gather(): pl.pallas_call(gather_kernel, in_specs=[VMEM] * 4 + [HBM], out_specs=VMEM...  5.34 us
    ppermute x1, starting transfers between devices, shards(): above_x = lax.ppermute(low_rows, 'gx', [(b, a) for a, b in up])  4.41 us
    pallas_call x1, Pallas kernels, run_spread(): pl.pallas_call(functools.partial(spread_kernel, gy_size, slots), in_specs...  4.28 us
  transfers between devices with their start and end apart: 5, of which 1 were waited for; matrix products, arithmetic and copies ran while one was open for 0% of the time, Pallas kernels for 17%

profile of v10, /device:TPU:1, one launch (start us, length us, event | category | flops | bytes accessed | tf_op | source)
XLA Modules:
  0.0 85.7 jit_solution(14896064661945316931)
XLA Ops:
  0.6 4.3 %spread.1 = (bf16[256,1664]{1,0:T(8,128)(2,1)S(1)}, f32[64,128]{1,0:T(8,128)S(1)}) custom-call(f32[3,8,128]{2,1,0:T(8,128)} %bitcast.6, f32[8]{0:T(128)} %stiff_hbm.1, s32[8,128]{1,0:T(8,128)} %links_hbm.1, s32[8,8]{1,0:T(8,128)} %bitcast.14, s32[8,8]{1,0:T(8,128)} %patch_slots_hbm.1, bf16[8,1024,512]{2,1,0:T(8,128)(2,1)} %bitcast.8), custom_call_target="tpu_custom_call" | custom-call | flops 1000000000 | bytes 9437184 | tf_op jit(solution)/shard_map/spread/pallas_call | solution.py:469
  4.9 1.2 %reshape.31 = bf16[128,2,1664]{2,1,0:T(2,128)(2,1)} reshape(bf16[256,1664]{1,0:T(8,128)(2,1)S(1)} %get-tuple-element.17) | data formatting | bytes 1703936 | tf_op jit(solution)/shard_map/reshape | solution.py:633
  6.1 11.5 %all-to-all-start = ((bf16[128,2,1664]{2,1,0:T(2,128)(2,1)}), bf16[128,2,1664]{2,1,0:T(2,128)(2,1)S(1)}, u32[]{:S(2)}, u32[]{:S(2)}) async-start(bf16[128,2,1664]{2,1,0:T(2,128)(2,1)} %reshape.31), calls=%async_computation | async-start | bytes 1703936 | tf_op jit(solution)/shard_map/all_to_all | solution.py:632
  17.6 2.1 %edges.1 = (f32[8,1024]{1,0:T(8,128)S(1)}, f32[8,1024]{1,0:T(8,128)S(1)}) custom-call(f32[3,1024,512]{2,1,0:T(8,128)} %bitcast.11), custom_call_target="tpu_custom_call" | custom-call | flops 100000000 | bytes 3145728 | tf_op jit(solution)/shard_map/edges/pallas_call | solution.py:497
  19.8 1.1 %collective-permute-start = (f32[8,1024]{1,0:T(8,128)S(1)}, f32[8,1024]{1,0:T(8,128)S(1)}, u32[]{:S(2)}, u32[]{:S(2)}) collective-permute-start(f32[8,1024]{1,0:T(8,128)S(1)} %get-tuple-element.15), channel_id=1, source_target_pairs={{1,0},{2,1},{3,2},{4,3},{5,4},{6,5},{7,6},{0,7},{9,8},{10,9},{11,1... | collective-permute-start | bytes 98312 | tf_op jit(solution)/shard_map/ppermute | solution.py:640
  20.9 0.7 collective-permute-start.1
  21.6 2.0 %lines.1.velocity = f32[3,128,512]{2,1,0:T(8,128)S(1)} custom-call(f32[3,32,32,512]{3,2,1,0:T(8,128)} %velocity.1), custom_call_target="tpu_custom_call" | custom-call | flops 100000000 | bytes 3145728 | tf_op jit(solution)/shard_map/lines/pallas_call | solution.py:512
  23.6 11.1 %all-to-all-done = bf16[128,2,1664]{2,1,0:T(2,128)(2,1)S(1)} async-done(((bf16[128,2,1664]{2,1,0:T(2,128)(2,1)}), bf16[128,2,1664]{2,1,0:T(2,128)(2,1)S(1)}, u32[]{:S(2)}, u32[]{:S(2)}) %all-to-all-start) | async-done | bytes 852000 | tf_op jit(solution)/shard_map/all_to_all | solution.py:632
  34.7 0.3 reshape.32.received
  35.0 0.0 collective-permute-done.ahead
  35.0 0.0 collective-permute-done.1.behind
  35.0 0.7 rim.1
  35.7 0.5 collective-permute-start.2
  36.2 3.5 %place.1 = (f32[3,5,1024,128]{3,2,1,0:T(8,128)S(1)}, bf16[25,32,128]{2,1,0:T(8,128)(2,1)S(1)}) custom-call(f32[3,1024,512]{2,1,0:T(8,128)} %bitcast.12, f32[3,1024,128]{2,1,0:T(8,128)S(1)} %get-tuple-element.18.edges, bf16[256,1664]{1,0:T(8,128)(2,1)S(1)} %reshape.32.received, bf16[25,32,128]{2,1,0:T(8,128)(2,1)S(1)} %get-tuple-element.19.low_in), custom_call_target="tpu_custom_call" | custom-call | flops 1000000000 | bytes 8388608 | tf_op jit(solution)/shard_map/place/pallas_call | solution.py:545
  39.8 4.4 %collective-permute-start.3 = (bf16[25,32,128]{2,1,0:T(8,128)(2,1)S(1)}, bf16[25,32,128]{2,1,0:T(8,128)(2,1)S(1)}, u32[]{:S(2)}, u32[]{:S(2)}) collective-permute-start(bf16[25,32,128]{2,1,0:T(8,128)(2,1)S(1)} %get-tuple-element.23), channel_id=1, source_target_pairs={{8,0},{16,8},{24,16},{32,24},{40,32},{48,40},{56,48},{64,56},{72,6... | collective-permute-start | bytes 614408 | tf_op jit(solution)/shard_map/ppermute | solution.py:647
  44.2 6.5 %sweep_first.1.u1_in = f32[3,5,1024,128]{3,2,1,0:T(8,128)S(1)} custom-call(f32[3,5,1024,128]{3,2,1,0:T(8,128)S(1)} %get-tuple-element.20.u0), custom_call_target="tpu_custom_call" | custom-call | flops 2000000000 | bytes 25165824 | tf_op jit(solution)/shard_map/sweep_first/pallas_call | solution.py:561
  50.7 0.0 collective-permute-done.2.below_x
  50.7 0.0 collective-permute-done.3.above_x
  50.7 0.0 copy-start
  50.7 7.2 %sweep_last.1 = (f32[3,1024,512]{2,1,0:T(8,128)}, bf16[256,1536]{1,0:T(8,128)(2,1)S(1)}, f32[3,5,1024,128]{3,2,1,0:T(8,128)S(1)}, bf16[1,1024,512]{2,1,0:T(8,128)(2,1)S(1)}) custom-call(f32[3,5,1024,128]{3,2,1,0:T(8,128)S(1)} %sweep_first.1.u1_in, f32[2,3,5,32,128]{4,3,2,1,0:T(8,128)S(1)} %get-tuple-element.21.rim, ...), custom_call_target="tpu_custom_call", output_to_operand_aliasing={{2}: (0, {})} | custom-call | flops 2000000000 | bytes 16777216 | tf_op jit(solution)/shard_map/sweep_last/pallas_call | solution.py:575
  57.9 0.3 reshape.34
  58.2 21.8 %all_to_all.10 = bf16[128,2,1536]{2,1,0:T(2,128)(2,1)S(1)} all-to-all(bf16[128,2,1536]{2,1,0:T(2,128)(2,1)S(1)} %reshape.34), channel_id=1, replica_groups=mesh['gx'=16,'gy'=8] {'gx','gy'}, dimensions={0} | all-to-all | bytes 1572864 | tf_op jit(solution)/shard_map/all_to_all | solution.py:632
  80.0 0.3 reshape.35.returned
  80.3 5.3 %interp.1 = f32[3,8,128]{2,1,0:T(8,128)} custom-call(f32[3,8,128]{2,1,0:T(8,128)S(1)} %bitcast.7, f32[64,128]{1,0:T(8,128)S(1)} %get-tuple-element.25.dest, bf16[256,1536]{1,0:T(8,128)(2,1)S(1)} %reshape.35.returned, bf16[1,1024,512]{2,1,0:T(8,128)(2,1)S(1)} %get-tuple-element.27.near_dw, bf16[8,1024,512]{2,1,0:T(8,128)(2,1)} %bitcast.10), custom_call_target="tpu_custom_call" | custom-call | flops 1000000000 | bytes 9437184 | tf_op jit(solution)/shard_map/interp/pallas_call | solution.py:601
  (1 shorter events, 0.0 us)
Async XLA Ops:
  6.1 28.5 %all-to-all-start = ((bf16[128,2,1664]{2,1,0:T(2,128)(2,1)}), bf16[128,2,1664]{2,1,0:T(2,128)(2,1)S(1)}, u32[]{:S(2)}, u32[]{:S(2)}) async-start(bf16[128,2,1664]{2,1,0:T(2,128)(2,1)} %reshape.31), calls=%async_computation | async-start | bytes 1703936 | tf_op jit(solution)/shard_map/all_to_all | solution.py:632
  19.8 15.2 %collective-permute-start = (f32[8,1024]{1,0:T(8,128)S(1)}, f32[8,1024]{1,0:T(8,128)S(1)}, u32[]{:S(2)}, u32[]{:S(2)}) collective-permute-start(f32[8,1024]{1,0:T(8,128)S(1)} %get-tuple-element.15), channel_id=1, source_target_pairs={{1,0},{2,1},{3,2},{4,3},{5,4},{6,5},{7,6},{0,7},{9,8},{10,9},{11,1... | collective-permute-start | bytes 98312 | tf_op jit(solution)/shard_map/ppermute | solution.py:640
  20.9 14.2 %collective-permute-start.1 = (f32[8,1024]{1,0:T(8,128)S(1)}, f32[8,1024]{1,0:T(8,128)S(1)}, u32[]{:S(2)}, u32[]{:S(2)}) collective-permute-start(f32[8,1024]{1,0:T(8,128)S(1)} %get-tuple-element.16), channel_id=1, source_target_pairs={{0,1},{1,2},{2,3},{3,4},{4,5},{5,6},{6,7},{7,0},{8,9},{9,10},{10,1... | collective-permute-start | bytes 98312 | tf_op jit(solution)/shard_map/ppermute | solution.py:641
  35.7 15.0 %collective-permute-start.2 = (bf16[25,32,128]{2,1,0:T(8,128)(2,1)S(1)}, bf16[25,32,128]{2,1,0:T(8,128)(2,1)S(1)}, u32[]{:S(2)}, u32[]{:S(2)}) collective-permute-start(bf16[25,32,128]{2,1,0:T(8,128)(2,1)S(1)} %get-tuple-element.22), channel_id=1, source_target_pairs={{0,8},{8,16},{16,24},{24,32},{32,40},{40,48},{48,56},{56,64},{64,7... | collective-permute-start | bytes 614408 | tf_op jit(solution)/shard_map/ppermute | solution.py:645
  39.8 10.9 %collective-permute-start.3 = (bf16[25,32,128]{2,1,0:T(8,128)(2,1)S(1)}, bf16[25,32,128]{2,1,0:T(8,128)(2,1)S(1)}, u32[]{:S(2)}, u32[]{:S(2)}) collective-permute-start(bf16[25,32,128]{2,1,0:T(8,128)(2,1)S(1)} %get-tuple-element.23), channel_id=1, source_target_pairs={{8,0},{16,8},{24,16},{32,24},{40,32},{48,40},{56,48},{64,56},{72,6... | collective-permute-start | bytes 614408 | tf_op jit(solution)/shard_map/ppermute | solution.py:647
  50.7 29.6 %copy-start = (f32[8,3,128]{2,0,1:T(8,128)S(1)}, f32[8,3,128]{2,0,1:T(8,128)}, u32[]{:S(2)}) copy-start(f32[8,3,128]{2,0,1:T(8,128)} %param.8) | copy-start | bytes 36868

commit v11 on v9

--- a/solution.py
+++ b/solution.py
@@ -381,8 +381,7 @@
 
     @pl.loop(0, layers // depth)
     def _(step):
-        @pl.loop(0, depth // 2)
-        def _(i):
+        for i in range(depth // 2):
             sweep_pair(
                 u1,
                 layers,

time: 84.9 us -> 84.6 us (level)
  no operation moved by 1% of the time
where the time goes in v11:
time: 84.6 us; the launch traced here: 84.4 us
  Pallas kernels  31.2 us (37%)
  blocking collectives  21 us (25%)
  starting transfers between devices  18.1 us (21%)
  waiting for transfers between devices  11.1 us (13%)
  local copies, waits for them, and re-layouts  2.14 us (3%)
    all_to_all x1, blocking collectives, exchange(): lax.all_to_all(rows_out.reshape(devices, 2, size), ('gx', 'gy'), split_ax...  21 us
    all_to_all x1, starting transfers between devices, exchange(): lax.all_to_all(rows_out.reshape(devices, 2, size), ('gx', 'gy'), split_ax...  11.5 us
    all_to_all x1, waiting for transfers between devices, exchange(): lax.all_to_all(rows_out.reshape(devices, 2, size), ('gx', 'gy'), split_ax...  11.1 us
    pallas_call x1, Pallas kernels, run_first(): pl.pallas_call(functools.partial(first_kernel, layers), in_specs=[HBM, VM...  9.76 us
    pallas_call x1, Pallas kernels, run_last(): pl.pallas_call(functools.partial(last_kernel, layers), in_specs=[VMEM] *...  6.97 us
    pallas_call x1, Pallas kernels, run_gather(): pl.pallas_call(gather_kernel, in_specs=[VMEM] * 4 + [HBM], out_specs=VMEM...  5.34 us
    ppermute x1, starting transfers between devices, shards(): above_x = lax.ppermute(low_rows, 'gx', [(b, a) for a, b in up])  4.34 us
    pallas_call x1, Pallas kernels, run_spread(): pl.pallas_call(functools.partial(spread_kernel, gy_size, slots), in_specs...  4.28 us
  transfers between devices with their start and end apart: 5, of which 1 were waited for; matrix products, arithmetic and copies ran while one was open for 0% of the time, Pallas kernels for 16%

profile of v11, /device:TPU:1, one launch (start us, length us, event | category | flops | bytes accessed | tf_op | source)
XLA Modules:
  0.0 84.4 jit_solution(18126345232189997900)
XLA Ops:
  0.6 4.3 %spread.1 = (bf16[256,1664]{1,0:T(8,128)(2,1)S(1)}, f32[64,128]{1,0:T(8,128)S(1)}) custom-call(f32[3,8,128]{2,1,0:T(8,128)} %bitcast.6, f32[8]{0:T(128)} %stiff_hbm.1, s32[8,128]{1,0:T(8,128)} %links_hbm.1, s32[8,8]{1,0:T(8,128)} %bitcast.14, s32[8,8]{1,0:T(8,128)} %patch_slots_hbm.1, bf16[8,1024,512]{2,1,0:T(8,128)(2,1)} %bitcast.8), custom_call_target="tpu_custom_call" | custom-call | flops 1000000000 | bytes 9437184 | tf_op jit(solution)/shard_map/spread/pallas_call | solution.py:463
  4.9 1.2 %reshape.31 = bf16[128,2,1664]{2,1,0:T(2,128)(2,1)} reshape(bf16[256,1664]{1,0:T(8,128)(2,1)S(1)} %get-tuple-element.15) | data formatting | bytes 1703936 | tf_op jit(solution)/shard_map/reshape | solution.py:613
  6.1 11.5 %all-to-all-start = ((bf16[128,2,1664]{2,1,0:T(2,128)(2,1)}), bf16[128,2,1664]{2,1,0:T(2,128)(2,1)S(1)}, u32[]{:S(2)}, u32[]{:S(2)}) async-start(bf16[128,2,1664]{2,1,0:T(2,128)(2,1)} %reshape.31), calls=%async_computation | async-start | bytes 1703936 | tf_op jit(solution)/shard_map/all_to_all | solution.py:612
  17.6 2.1 %edges.1 = (f32[8,1024]{1,0:T(8,128)S(1)}, f32[8,1024]{1,0:T(8,128)S(1)}) custom-call(f32[3,1024,512]{2,1,0:T(8,128)} %bitcast.11), custom_call_target="tpu_custom_call" | custom-call | flops 100000000 | bytes 3145728 | tf_op jit(solution)/shard_map/edges/pallas_call | solution.py:491
  19.8 1.1 %collective-permute-start = (f32[8,1024]{1,0:T(8,128)S(1)}, f32[8,1024]{1,0:T(8,128)S(1)}, u32[]{:S(2)}, u32[]{:S(2)}) collective-permute-start(f32[8,1024]{1,0:T(8,128)S(1)} %get-tuple-element.13), channel_id=1, source_target_pairs={{1,0},{2,1},{3,2},{4,3},{5,4},{6,5},{7,6},{0,7},{9,8},{10,9},{11,1... | collective-permute-start | bytes 98312 | tf_op jit(solution)/shard_map/ppermute | solution.py:620
  20.9 0.7 collective-permute-start.1
  21.6 2.0 %lines.1.velocity = f32[3,128,512]{2,1,0:T(8,128)S(1)} custom-call(f32[3,32,32,512]{3,2,1,0:T(8,128)} %velocity.1), custom_call_target="tpu_custom_call" | custom-call | flops 100000000 | bytes 3145728 | tf_op jit(solution)/shard_map/lines/pallas_call | solution.py:506
  23.6 11.1 %all-to-all-done = bf16[128,2,1664]{2,1,0:T(2,128)(2,1)S(1)} async-done(((bf16[128,2,1664]{2,1,0:T(2,128)(2,1)}), bf16[128,2,1664]{2,1,0:T(2,128)(2,1)S(1)}, u32[]{:S(2)}, u32[]{:S(2)}) %all-to-all-start) | async-done | bytes 852000 | tf_op jit(solution)/shard_map/all_to_all | solution.py:612
  34.7 0.3 reshape.32.received
  35.0 0.0 collective-permute-done.ahead
  35.0 0.0 collective-permute-done.1.behind
  35.0 0.7 rim.1
  35.7 0.5 collective-permute-start.2
  36.2 4.3 %collective-permute-start.3 = (bf16[25,32,128]{2,1,0:T(8,128)(2,1)S(1)}, bf16[25,32,128]{2,1,0:T(8,128)(2,1)S(1)}, u32[]{:S(2)}, u32[]{:S(2)}) collective-permute-start(bf16[25,32,128]{2,1,0:T(8,128)(2,1)S(1)} %get-tuple-element.19), channel_id=1, source_target_pairs={{8,0},{16,8},{24,16},{32,24},{40,32},{48,40},{56,48},{64,56},{72,6... | collective-permute-start | bytes 614408 | tf_op jit(solution)/shard_map/ppermute | solution.py:626
  40.6 9.8 %sweep_first.1.u1_in = f32[3,5,1024,128]{3,2,1,0:T(8,128)S(1)} custom-call(f32[3,1024,512]{2,1,0:T(8,128)} %bitcast.12, f32[3,1024,128]{2,1,0:T(8,128)S(1)} %get-tuple-element.16.edges, bf16[256,1664]{1,0:T(8,128)(2,1)S(1)} %reshape.32.received), custom_call_target="tpu_custom_call" | custom-call | flops 2000000000 | bytes 25165824 | tf_op jit(solution)/shard_map/sweep_first/pallas_call | solution.py:540
  50.4 0.0 collective-permute-done.2.below_x
  50.4 0.0 collective-permute-done.3.above_x
  50.4 0.0 copy-start
  50.4 7.0 %sweep_last.1 = (f32[3,1024,512]{2,1,0:T(8,128)}, bf16[256,1536]{1,0:T(8,128)(2,1)S(1)}, f32[3,5,1024,128]{3,2,1,0:T(8,128)S(1)}, bf16[1,1024,512]{2,1,0:T(8,128)(2,1)S(1)}) custom-call(f32[3,5,1024,128]{3,2,1,0:T(8,128)S(1)} %sweep_first.1.u1_in, f32[2,3,5,32,128]{4,3,2,1,0:T(8,128)S(1)} %get-tuple-element.17.rim, ...), custom_call_target="tpu_custom_call", output_to_operand_aliasing={{2}: (0, {})} | custom-call | flops 2000000000 | bytes 16777216 | tf_op jit(solution)/shard_map/sweep_last/pallas_call | solution.py:555
  57.4 0.3 reshape.34
  57.7 21.0 %all_to_all.10 = bf16[128,2,1536]{2,1,0:T(2,128)(2,1)S(1)} all-to-all(bf16[128,2,1536]{2,1,0:T(2,128)(2,1)S(1)} %reshape.34), channel_id=1, replica_groups=mesh['gx'=16,'gy'=8] {'gx','gy'}, dimensions={0} | all-to-all | bytes 1572864 | tf_op jit(solution)/shard_map/all_to_all | solution.py:612
  78.7 0.3 reshape.35.returned
  79.0 0.0 copy-done
  79.0 5.3 %interp.1 = f32[3,8,128]{2,1,0:T(8,128)} custom-call(f32[3,8,128]{2,1,0:T(8,128)S(1)} %bitcast.7, f32[64,128]{1,0:T(8,128)S(1)} %get-tuple-element.21.dest, bf16[256,1536]{1,0:T(8,128)(2,1)S(1)} %reshape.35.returned, bf16[1,1024,512]{2,1,0:T(8,128)(2,1)S(1)} %get-tuple-element.23.near_dw, bf16[8,1024,512]{2,1,0:T(8,128)(2,1)} %bitcast.10), custom_call_target="tpu_custom_call" | custom-call | flops 1000000000 | bytes 9437184 | tf_op jit(solution)/shard_map/interp/pallas_call | solution.py:581
Async XLA Ops:
  6.1 28.5 %all-to-all-start = ((bf16[128,2,1664]{2,1,0:T(2,128)(2,1)}), bf16[128,2,1664]{2,1,0:T(2,128)(2,1)S(1)}, u32[]{:S(2)}, u32[]{:S(2)}) async-start(bf16[128,2,1664]{2,1,0:T(2,128)(2,1)} %reshape.31), calls=%async_computation | async-start | bytes 1703936 | tf_op jit(solution)/shard_map/all_to_all | solution.py:612
  19.8 15.2 %collective-permute-start = (f32[8,1024]{1,0:T(8,128)S(1)}, f32[8,1024]{1,0:T(8,128)S(1)}, u32[]{:S(2)}, u32[]{:S(2)}) collective-permute-start(f32[8,1024]{1,0:T(8,128)S(1)} %get-tuple-element.13), channel_id=1, source_target_pairs={{1,0},{2,1},{3,2},{4,3},{5,4},{6,5},{7,6},{0,7},{9,8},{10,9},{11,1... | collective-permute-start | bytes 98312 | tf_op jit(solution)/shard_map/ppermute | solution.py:620
  20.9 14.2 %collective-permute-start.1 = (f32[8,1024]{1,0:T(8,128)S(1)}, f32[8,1024]{1,0:T(8,128)S(1)}, u32[]{:S(2)}, u32[]{:S(2)}) collective-permute-start(f32[8,1024]{1,0:T(8,128)S(1)} %get-tuple-element.14), channel_id=1, source_target_pairs={{0,1},{1,2},{2,3},{3,4},{4,5},{5,6},{6,7},{7,0},{8,9},{9,10},{10,1... | collective-permute-start | bytes 98312 | tf_op jit(solution)/shard_map/ppermute | solution.py:621
  35.7 14.6 %collective-permute-start.2 = (bf16[25,32,128]{2,1,0:T(8,128)(2,1)S(1)}, bf16[25,32,128]{2,1,0:T(8,128)(2,1)S(1)}, u32[]{:S(2)}, u32[]{:S(2)}) collective-permute-start(bf16[25,32,128]{2,1,0:T(8,128)(2,1)S(1)} %get-tuple-element.18), channel_id=1, source_target_pairs={{0,8},{8,16},{16,24},{24,32},{32,40},{40,48},{48,56},{56,64},{64,7... | collective-permute-start | bytes 614408 | tf_op jit(solution)/shard_map/ppermute | solution.py:625
  36.2 14.1 %collective-permute-start.3 = (bf16[25,32,128]{2,1,0:T(8,128)(2,1)S(1)}, bf16[25,32,128]{2,1,0:T(8,128)(2,1)S(1)}, u32[]{:S(2)}, u32[]{:S(2)}) collective-permute-start(bf16[25,32,128]{2,1,0:T(8,128)(2,1)S(1)} %get-tuple-element.19), channel_id=1, source_target_pairs={{8,0},{16,8},{24,16},{32,24},{40,32},{48,40},{56,48},{64,56},{72,6... | collective-permute-start | bytes 614408 | tf_op jit(solution)/shard_map/ppermute | solution.py:626
  50.4 28.6 %copy-start = (f32[8,3,128]{2,0,1:T(8,128)S(1)}, f32[8,3,128]{2,0,1:T(8,128)}, u32[]{:S(2)}) copy-start(f32[8,3,128]{2,0,1:T(8,128)} %param.8) | copy-start | bytes 36868
